TPU v7x, 512 devices: a whole 4x8x8 slice. The times are simulated.
512 devices in a mesh: node: 32 (over y, z_lo), hst: 8 (over x, core), dp: 2 (over z_hi).
Axes of the slice: x: 4, y: 8, z: 8 (z_hi: 2, z_lo: 4; z = z_hi * 4 + z_lo), core: 2. Of those that a mesh axis runs over, the one named last changes fastest.
Arguments:
- partials: bfloat16 [8, 4096, 128, 192], P('hst', 'dp', 'node'), may hold values from -6 to 6
- counts: int32 [2, 8, 256, 128], P('dp', 'hst', 'node'), may hold values from 0 to 5
- perm: int32 [128], replicated, may hold values from 0 to 127, each once
- fm_proj: bfloat16 [128, 32], replicated, may hold values from -0.5 to 0.5
- ln_gain: float32 [4096], replicated, may hold values from 0.1 to 1.9
- w_in: bfloat16 [4096, 4096], P('hst', 'node'), may hold values from -0.09375 to 0.09375
- d_hidden: bfloat16 [2, 8, 256, 4096], P('dp', 'hst', None, 'node'), may hold values from -0.5 to 0.5
Outputs:
- hidden: bfloat16 [2, 8, 256, 4096], P('dp', 'hst', None, 'node')
- grad_w: float32 [4096, 4096], P('hst', 'node')
Inputs may be any that keep to these rules, and one draw needn't show every extreme that they name: perm names each of the 128 features once.
All inputs are finite; a program needn't handle non-finite values.
Results may differ from a plain program's by a relative error of at most 0.03.
Values may be sent and summed in bfloat16 or wider, within the bound.
No kernel may reach another device: no remote copies, remote signals or barrier semaphores. Data moves between devices by JAX's collectives and lax.ppermute only.
A program may use at most 64 MiB of HBM per device.

v0:
```python
import jax
import jax.numpy as jnp
from jax import lax
from jax.sharding import PartitionSpec as P


def normalize(flat_rows, ln_gain):
    middle = jnp.mean(flat_rows, axis=-1, keepdims=True)
    centered = flat_rows - middle
    variance = jnp.mean(centered * centered, axis=-1, keepdims=True)
    return (centered * lax.rsqrt(variance + 1e-05) * ln_gain).astype(jnp.bfloat16)


def local(partials, counts, perm, fm_proj, ln_gain, w_in, d_hidden):
    local_rows = partials[0]
    samples = counts.shape[2]
    summed = (
        lax.psum_scatter(local_rows, "hst", scatter_dimension=0, tiled=True)
        .astype(jnp.float32)
        .astype(jnp.bfloat16)
    )
    shard_rows = lax.all_to_all(summed, "node", split_axis=0, concat_axis=1, tiled=True)
    ordered = jnp.take(shard_rows, perm, axis=1)
    counts_here = counts[0, 0]
    divisor = jnp.maximum(counts_here, 1).astype(jnp.float32)[:, :, None]
    pooled = jnp.where(
        counts_here[:, :, None] > 0, ordered.astype(jnp.float32) / divisor, 0.0
    ).astype(jnp.bfloat16)
    projected = jnp.einsum(
        "sfe,fk->sek", pooled, fm_proj, preferred_element_type=jnp.float32
    ).astype(jnp.bfloat16)
    pairwise = jnp.einsum("sfe,sek->sfk", pooled, projected, preferred_element_type=jnp.float32)
    z_local = normalize(pairwise.reshape(samples, -1), ln_gain)
    z_group = lax.all_gather(z_local, "node", axis=0, tiled=True)
    pre_act = jnp.dot(
        z_group, lax.all_gather(w_in, "hst", axis=0, tiled=True), preferred_element_type=jnp.float32
    )
    sigma = jax.nn.sigmoid(pre_act)
    hidden = (pre_act * sigma).astype(jnp.bfloat16)
    d_pre = (d_hidden[0, 0].astype(jnp.float32) * sigma * (1.0 + pre_act * (1.0 - sigma))).astype(
        jnp.bfloat16
    )
    share_rows = w_in.shape[0]
    term = lax.dot_general(
        z_group, d_pre, (((0,), (0,)), ((), ())), preferred_element_type=jnp.float32
    )
    term = lax.optimization_barrier(term.astype(jnp.bfloat16)).astype(jnp.float32)
    total = lax.psum(term.astype(jnp.bfloat16), ("hst", "dp")).astype(jnp.float32)
    grad_w = lax.dynamic_slice_in_dim(total, lax.axis_index("hst") * share_rows, share_rows, 0)
    return (hidden[None, None], grad_w)


def solution(mesh):
    in_specs = (
        P("hst", "dp", "node", None),
        P("dp", "hst", "node", None),
        P(),
        P(),
        P(),
        P("hst", "node"),
        P("dp", "hst", None, "node"),
    )
    out_specs = (P("dp", "hst", None, "node"), P("hst", "node"))
    return jax.shard_map(local, mesh=mesh, in_specs=in_specs, out_specs=out_specs, check_vma=False)
```

profile of v0, /device:TPU:56, one launch (start us, length us, event | category | flops | bytes accessed | tf_op | source)
XLA Modules:
  0.0 511.7 jit_solution(8624118692096548327)
XLA Ops:
  7.2 7.2 %copy.31 = bf16[1,2048,4,192]{3,2,1,0:T(4,128)(2,1)} copy(bf16[1,2048,4,192]{1,3,2,0:T(8,128)(2,1)} %param.7) | data formatting | bytes 6291456 | tf_op args[0]
  14.5 0.7 all-gather.5.cloned.1.call-update
  15.3 1.3 dynamic-slice
  17.2 84.8 %all-reduce.6.cloned.1.call-done = bf16[2048,4,192]{2,1,0:T(4,128)(2,1)} async-done(((bf16[2048,4,192]{2,1,0:T(4,128)(2,1)}), bf16[2048,4,192]{2,1,0:T(4,128)(2,1)}) %all-reduce.6.cloned.1.call-update) | async-done | bytes 3145744
  102.0 2.0 constant_dynamic-slice_fusion
  104.0 10.6 %all-to-all-start = ((bf16[256,4,192]{2,1,0:T(4,128)(2,1)}), bf16[256,4,192]{2,1,0:T(4,128)(2,1)S(1)}, u32[]{:S(2)}, u32[]{:S(2)}) async-start(bf16[256,4,192]{2,1,0:T(4,128)(2,1)} %constant_dynamic-slice_fusion), calls=%async_computation | async-start | bytes 1048576 | tf_op jit(solution)/shard_map/all_to_all | solution.py:22
  114.8 13.5 %all-to-all-done = bf16[256,4,192]{2,1,0:T(4,128)(2,1)S(1)} async-done(((bf16[256,4,192]{2,1,0:T(4,128)(2,1)}), bf16[256,4,192]{2,1,0:T(4,128)(2,1)S(1)}, u32[]{:S(2)}, u32[]{:S(2)}) %all-to-all-start) | async-done | bytes 393248 | tf_op jit(solution)/shard_map/all_to_all | solution.py:22
  128.3 0.1 copy.37
  128.3 0.1 copy.33
  128.4 0.6 gather_fusion
  129.1 0.4 copy.34
  129.5 0.6 fusion.24
  130.1 0.2 copy.35
  130.3 0.2 reshape.50
  130.6 0.2 multiply_reduce_fusion
  130.8 0.7 multiply_convert_fusion.1
  131.6 0.0 all-reduce.4.cloned.1.call-start
  131.6 1.4 all-gather.5.cloned.1.call-done
  133.0 153.8 %all-gather.3.cloned.1.call-done = bf16[256,4096]{1,0:T(8,128)(2,1)} async-done(((bf16[8,4096]{1,0:T(8,128)(2,1)}), bf16[256,4096]{1,0:T(8,128)(2,1)}) %all-gather.3.cloned.1.call-update) | async-done | bytes 2097168 | tf_op jit(solution)/shard_map/all_gather | solution.py:34
  286.8 2.7 fusion.29
  289.5 1.8 convolution_convert_fusion
  291.4 0.7 fusion.16
  292.1 211.5 %all-reduce.4.cloned.1.call-done = bf16[4096,128]{1,0:T(8,128)(2,1)} async-done(((bf16[4096,128]{1,0:T(8,128)(2,1)}), bf16[4096,128]{1,0:T(8,128)(2,1)}) %all-reduce.4.cloned.1.call-update) | async-done | bytes 1048592 | tf_op jit(solution)/shard_map/psum | solution.py:48
  503.6 1.6 dynamic-slice_convert_fusion
  (25 shorter events, 0.2 us)
Async XLA Ops:
  7.2 122.3 %copy-start = (bf16[128,32]{0,1:T(8,128)(2,1)S(1)}, bf16[128,32]{0,1:T(8,128)(2,1)}, u32[]{:S(2)}) copy-start(bf16[128,32]{0,1:T(8,128)(2,1)} %param.10) | copy-start | bytes 24580
  7.2 94.8 %all-reduce.6.cloned.1.call-start = ((), (), s32[]{:S(2)}) async-start(), calls=%async_computation.4 | async-start | bytes 8388608
  14.4 0.8 copy-start.5
  14.5 100.3 %copy-start.3 = (s32[1,1,8,128]{3,2,1,0:T(8,128)S(1)}, s32[1,1,8,128]{3,2,1,0:T(8,128)}, u32[]{:S(2)}) copy-start(s32[1,1,8,128]{3,2,1,0:T(8,128)} %param.8) | copy-start | bytes 12292
  14.5 118.5 %all-gather.5.cloned.1.call-start = ((), (), s32[]{:S(2)}) async-start(), calls=%async_computation.2 | async-start | bytes 1179648 | tf_op jit(solution)/shard_map/all_gather | solution.py:36
  104.0 24.2 %all-to-all-start = ((bf16[256,4,192]{2,1,0:T(4,128)(2,1)}), bf16[256,4,192]{2,1,0:T(4,128)(2,1)S(1)}, u32[]{:S(2)}, u32[]{:S(2)}) async-start(bf16[256,4,192]{2,1,0:T(4,128)(2,1)} %constant_dynamic-slice_fusion), calls=%async_computation | async-start | bytes 1048576 | tf_op jit(solution)/shard_map/all_to_all | solution.py:22
  114.7 172.1 %all-gather.3.cloned.1.call-start = ((), (), s32[]{:S(2)}) async-start(), calls=%async_computation.1 | async-start | bytes 2162688 | tf_op jit(solution)/shard_map/all_gather | solution.py:34
  129.5 1.3 copy-start.4
  130.3 159.2 %copy-start.2 = (bf16[1,1,256,128]{3,2,1,0:T(8,128)(2,1)S(1)}, bf16[1,1,256,128]{3,2,1,0:T(8,128)(2,1)}, u32[]{:S(2)}) copy-start(bf16[1,1,256,128]{3,2,1,0:T(8,128)(2,1)} %param.13) | copy-start | bytes 196612
  131.6 372.0 %all-reduce.4.cloned.1.call-start = ((), (), s32[]{:S(2)}) async-start(), calls=%async_computation.3 | async-start | bytes 2097152 | tf_op jit(solution)/shard_map/psum | solution.py:48
  286.8 2.7 copy-start.1
Sparse Core Ops, SparseCore 0:
  14.6 87.3 all-reduce.5
  104.2 28.7 all-gather.4
  135.6 151.1 all-gather.2
  291.5 212.0 all-reduce.3
where the time goes:
time: 512 us
  waiting for transfers between devices  466 us (91%)
  between operations  14.6 us (3%)
  local copies, waits for them, and re-layouts  12.2 us (2%)
  starting transfers between devices  10.8 us (2%)
  matrix products  5.13 us (1%)
    psum x1, waiting for transfers between devices, local(): lax.psum(term.astype(jnp.bfloat16), ('hst', 'dp')).astype(jnp.float32)  212 us
    all_gather x1, waiting for transfers between devices, local(): z_group = lax.all_gather(z_local, 'node', axis=0, tiled=True)  154 us
    unnamed x5, waiting for transfers between devices  85.6 us
    all_to_all x1, waiting for transfers between devices, local(): lax.all_to_all(summed, 'node', split_axis=0, concat_axis=1, tiled=True)  13.5 us
    all_to_all x1, starting transfers between devices, local(): lax.all_to_all(summed, 'node', split_axis=0, concat_axis=1, tiled=True)  10.6 us
    unnamed x15, local copies, waits for them, and re-layouts  10.6 us
  transfers between devices with their start and end apart: 5, of which 5 were waited for; matrix products, arithmetic and copies ran while one was open for 1% of the time, Pallas kernels for 0%

commit v1 on v0

v1 whole, which is shorter than its diff:
```python
import jax
import jax.numpy as jnp
from jax import lax
from jax.sharding import PartitionSpec as P

N_X = 4
N_CORE = 2
N_Y = 8
N_Z = 4

CORE_SWAP = [(h, h ^ 1) for h in range(N_X * N_CORE)]
X_UP = [(2 * x + c, 2 * ((x + 1) % N_X) + c) for x in range(N_X) for c in range(N_CORE)]
X_DOWN = [(b, a) for a, b in X_UP]
Y_UP = [(N_Z * y + z, N_Z * ((y + 1) % N_Y) + z) for y in range(N_Y) for z in range(N_Z)]
Y_DOWN = [(b, a) for a, b in Y_UP]
DP_SWAP = [(0, 1), (1, 0)]


def z_shift(k):
    return [(N_Z * y + z, N_Z * y + (z + k) % N_Z) for y in range(N_Y) for z in range(N_Z)]


def add(*terms):
    total = terms[0].astype(jnp.float32)
    for term in terms[1:]:
        total = total + term.astype(jnp.float32)
    return total


def pick(pieces, index):
    return lax.dynamic_index_in_dim(pieces, index, 0, keepdims=False)


def scatter_sum(pieces):
    h = lax.axis_index("hst")
    x, c = h // N_CORE, h % N_CORE
    given = lax.dynamic_index_in_dim(pieces, 1 - c, 1, keepdims=False)
    kept = lax.dynamic_index_in_dim(pieces, c, 1, keepdims=False)
    got = lax.ppermute(given, "hst", CORE_SWAP)
    pair = add(kept, got).astype(jnp.bfloat16)
    half = pair.shape[1] // 2
    far = pick(pair, (x + 2) % N_X)
    up, down = pick(pair, (x + 1) % N_X), pick(pair, (x + 3) % N_X)
    own = pick(pair, x)
    far_up = lax.ppermute(far[:half], "hst", X_UP)
    far_down = lax.ppermute(far[half:], "hst", X_DOWN)
    up_b = lax.ppermute(up[half:], "hst", X_UP)
    down_a = lax.ppermute(down[:half], "hst", X_DOWN)
    up_a = lax.ppermute(add(up[:half], far_up).astype(jnp.bfloat16), "hst", X_UP)
    down_b = lax.ppermute(add(down[half:], far_down).astype(jnp.bfloat16), "hst", X_DOWN)
    return jnp.concatenate([add(own[:half], up_a, down_a), add(own[half:], up_b, down_b)], 0)


def normalize(flat_rows, ln_gain):
    middle = jnp.mean(flat_rows, axis=-1, keepdims=True)
    centered = flat_rows - middle
    variance = jnp.mean(centered * centered, axis=-1, keepdims=True)
    return (centered * lax.rsqrt(variance + 1e-05) * ln_gain).astype(jnp.bfloat16)


def gather_nodes(block):
    near = [block] + [lax.ppermute(block, "node", z_shift(k)) for k in range(1, N_Z)]
    line = jnp.concatenate(near, 0)
    half = line.shape[0] // 2
    ups, downs = [line], [line]
    for _ in range(3):
        ups.append(lax.ppermute(ups[-1], "node", Y_UP))
        downs.append(lax.ppermute(downs[-1], "node", Y_DOWN))
    far_a = lax.ppermute(ups[-1][:half], "node", Y_UP)
    far_b = lax.ppermute(downs[-1][half:], "node", Y_DOWN)
    return jnp.concatenate(ups + [far_a, far_b] + downs[:0:-1], 0)


def local(partials, counts, perm, fm_proj, ln_gain, w_in, d_hidden):
    samples = counts.shape[2]
    group, hidden_here = d_hidden.shape[2], d_hidden.shape[3]
    w_full = lax.all_gather(w_in, "hst", axis=0, tiled=True)

    n = lax.axis_index("node")
    y, z = n // N_Z, n % N_Z
    steps = jnp.arange(N_Y * N_Z)
    order = ((y - steps // N_Z) % N_Y) * N_Z + (z - steps % N_Z) % N_Z
    d_hid = jnp.take(d_hidden[0, 0].reshape(N_Y * N_Z, samples, hidden_here), order, axis=0)
    d_hid = d_hid.reshape(group, hidden_here)

    rows = partials.shape[2] * partials.shape[3]
    flat = partials[0].transpose(1, 2, 0).reshape(rows, N_X, N_CORE, group).transpose(1, 2, 0, 3)
    summed = scatter_sum(flat).astype(jnp.bfloat16).T
    shard_rows = lax.all_to_all(
        summed.reshape(N_Y * N_Z, samples, rows), "node", split_axis=0, concat_axis=0, tiled=True
    )
    shard_rows = shard_rows.transpose(1, 0, 2).reshape(samples, -1, partials.shape[3])
    ordered = jnp.take(shard_rows, perm, axis=1)
    counts_here = counts[0, 0]
    divisor = jnp.maximum(counts_here, 1).astype(jnp.float32)[:, :, None]
    pooled = jnp.where(
        counts_here[:, :, None] > 0, ordered.astype(jnp.float32) / divisor, 0.0
    ).astype(jnp.bfloat16)
    projected = jnp.einsum(
        "sfe,fk->sek", pooled, fm_proj, preferred_element_type=jnp.float32
    ).astype(jnp.bfloat16)
    pairwise = jnp.einsum("sfe,sek->sfk", pooled, projected, preferred_element_type=jnp.float32)
    z_local = normalize(pairwise.reshape(samples, -1), ln_gain)

    z_group = gather_nodes(z_local)
    pre_act = jnp.dot(z_group, w_full, preferred_element_type=jnp.float32)
    sigma = jax.nn.sigmoid(pre_act)
    hidden = (pre_act * sigma).astype(jnp.bfloat16)
    hidden = jnp.take(hidden.reshape(N_Y * N_Z, samples, hidden_here), order, axis=0)
    d_pre = (d_hid.astype(jnp.float32) * sigma * (1.0 + pre_act * (1.0 - sigma))).astype(
        jnp.bfloat16
    )
    term = lax.dot_general(
        z_group, d_pre, (((0,), (0,)), ((), ())), preferred_element_type=jnp.float32
    ).astype(jnp.bfloat16)
    share = scatter_sum(term.reshape(N_X, N_CORE, w_in.shape[0], hidden_here)).astype(jnp.bfloat16)
    other = lax.ppermute(share, "dp", DP_SWAP)
    grad_w = add(share, other)
    return (hidden.reshape(1, 1, group, hidden_here), grad_w)


def solution(mesh):
    in_specs = (
        P("hst", "dp", "node", None),
        P("dp", "hst", "node", None),
        P(),
        P(),
        P(),
        P("hst", "node"),
        P("dp", "hst", None, "node"),
    )
    out_specs = (P("dp", "hst", None, "node"), P("hst", "node"))
    return jax.shard_map(local, mesh=mesh, in_specs=in_specs, out_specs=out_specs, check_vma=False)
```

time: 512 us -> 202 us (0.39)
  waiting for transfers between devices: 466 us -> 55.9 us
  starting transfers between devices: 10.8 us -> 99.2 us
  other arithmetic: 3.28 us -> 15.4 us
    psum x1 -> x0, waiting for transfers between devices: 212 us -> none  [local(): lax.psum(term.astype(jnp.bfloat16), ('hst', 'dp')).astype(jnp.float32)]
    all_gather x2 -> x1, waiting for transfers between devices: 155 us -> 0.02 us  [local(): w_full = lax.all_gather(w_in, 'hst', axis=0, tiled=True)]
    unnamed x5 -> x1, waiting for transfers between devices: 85.6 us -> 0.02 us
    ppermute x0 -> x26, starting transfers between devices: none -> 85.4 us  [the longest x3 16.5 us: gather_nodes(): ups.append(lax.ppermute(ups[-1], 'node', Y_UP))]
    ppermute x0 -> x26, waiting for transfers between devices: none -> 44.9 us  [the longest x3 9.25 us: gather_nodes(): ups.append(lax.ppermute(ups[-1], 'node', Y_UP))]
    unnamed x15 -> x26, local copies, waits for them, and re-layouts: 10.6 us -> 0.28 us
    dynamic_slice x0 -> x1, other arithmetic: none -> 7.4 us  [scatter_sum(): given = lax.dynamic_index_in_dim(pieces, 1 - c, 1, keepdims=False)]
    reshape x0 -> x3, local copies, waits for them, and re-layouts: none -> 5.54 us  [the longest x1 4.75 us: local(): partials[0].transpose(1, 2, 0).reshape(rows, N_X, N_CORE, group)]
  transfers between devices with their start and end apart: 5 -> 28, of which waited for: 5 -> 17; matrix products, arithmetic and copies ran while one was open for 1% -> 6% of each run, Pallas kernels for 0% -> 0%
where the time goes in v1:
time: 202 us; the launch traced here: 201 us
  starting transfers between devices  99.2 us (49%)
  waiting for transfers between devices  55.9 us (28%)
  other arithmetic  15.4 us (8%)
  between operations  14.9 us (7%)
  local copies, waits for them, and re-layouts  12.6 us (6%)
  matrix products  3.35 us (2%)
    ppermute x3, starting transfers between devices, gather_nodes(): ups.append(lax.ppermute(ups[-1], 'node', Y_UP))  16.5 us
    all_to_all x1, starting transfers between devices, local(): lax.all_to_all(summed.reshape(N_Y * N_Z, samples, rows), 'node', split_ax...  13.7 us
    all_to_all x1, waiting for transfers between devices, local(): lax.all_to_all(summed.reshape(N_Y * N_Z, samples, rows), 'node', split_ax...  10.9 us
    ppermute x3, starting transfers between devices, gather_nodes(): lax.ppermute(block, 'node', z_shift(k))  9.56 us
    ppermute x3, waiting for transfers between devices, gather_nodes(): ups.append(lax.ppermute(ups[-1], 'node', Y_UP))  9.25 us
    ppermute x2, starting transfers between devices, scatter_sum(): down_a = lax.ppermute(down[:half], 'hst', X_DOWN)  8.08 us
    dynamic_slice x1, other arithmetic, scatter_sum(): given = lax.dynamic_index_in_dim(pieces, 1 - c, 1, keepdims=False)  7.4 us
    ppermute x2, starting transfers between devices, scatter_sum(): far_down = lax.ppermute(far[half:], 'hst', X_DOWN)  7.38 us
  transfers between devices with their start and end apart: 28, of which 17 were waited for; matrix products, arithmetic and copies ran while one was open for 6% of the time, Pallas kernels for 0%

profile of v1, /device:TPU:56, one launch (start us, length us, event | category | flops | bytes accessed | tf_op | source)
XLA Modules:
  0.0 201.2 jit_solution(9603864688763600421)
XLA Ops:
  7.2 4.8 %reshape.110 = bf16[768,4,2,256]{3,2,1,0:T(2,128)(2,1)S(1)} reshape(bf16[4,192,2048]{2,1,0:T(8,128)(2,1)} %bitcast.125) | data formatting | bytes 6291456 | tf_op jit(solution)/shard_map/reshape | solution.py:87
  12.0 7.4 %dynamic-slice_bitcast_fusion = (bf16[4,1,768,256]{3,1,0,2:T(2,128)(2,1)S(1)}, f32[4,1,768,256]{3,1,0,2:T(1,128)}) fusion(bf16[768,4,2,256]{3,2,1,0:T(2,128)(2,1)S(1)} %reshape.110, s32[]{:T(128)S(6)} %select_n.108, s32[]{:T(128)S(6)} %select_n.107), kind=kLoop, calls=%fused_computation.7 | loop fusion | flops 786432 | bytes 7864328 | tf_op jit(solution)/shard_map/jit(dynamic_index_in_dim)/dynamic_slice | solution.py:37
  24.6 3.4 %collective-permute-done = bf16[4,768,256]{2,0,1:T(4,128)(2,1)} collective-permute-done((bf16[4,768,256]{2,0,1:T(4,128)(2,1)}, bf16[4,768,256]{2,0,1:T(4,128)(2,1)}, u32[]{:S(2)}, u32[]{:S(2)}) %collective-permute-start) | collective-permute-done | bytes 1572896 | tf_op jit(solution)/shard_map/ppermute | solution.py:39
  33.7 3.4 %collective-permute-start.1 = (bf16[384,256]{1,0:T(8,128)(2,1)S(1)}, bf16[384,256]{1,0:T(8,128)(2,1)S(1)}, u32[]{:S(2)}, u32[]{:S(2)}) collective-permute-start(bf16[384,256]{1,0:T(8,128)(2,1)S(1)} %bitcast.127), channel_id=1, source_target_pairs={{0,4},{2,6},{4,8},{6,10},{8,12},{10,14},{12,0},{14,2},{1,5},{3,7},... | collective-permute-start | bytes 589832 | tf_op jit(solution)/shard_map/ppermute | solution.py:45
  37.2 3.7 %collective-permute-start.3 = (bf16[384,256]{1,0:T(8,128)(2,1)S(1)}, bf16[384,256]{1,0:T(8,128)(2,1)S(1)}, u32[]{:S(2)}, u32[]{:S(2)}) collective-permute-start(bf16[384,256]{1,0:T(8,128)(2,1)S(1)} %bitcast.128), channel_id=1, source_target_pairs={{4,0},{6,2},{8,4},{10,6},{12,8},{14,10},{0,12},{2,14},{5,1},{7,3},... | collective-permute-start | bytes 589832 | tf_op jit(solution)/shard_map/ppermute | solution.py:48
  40.9 3.5 %collective-permute-start.5 = (bf16[384,256]{1,0:T(8,128)(2,1)S(1)}, bf16[384,256]{1,0:T(8,128)(2,1)S(1)}, u32[]{:S(2)}, u32[]{:S(2)}) collective-permute-start(bf16[384,256]{1,0:T(8,128)(2,1)S(1)} %bitcast.130), channel_id=1, source_target_pairs={{4,0},{6,2},{8,4},{10,6},{12,8},{14,10},{0,12},{2,14},{5,1},{7,3},... | collective-permute-start | bytes 589832 | tf_op jit(solution)/shard_map/ppermute | solution.py:46
  49.0 3.6 %collective-permute-done.5 = bf16[384,256]{1,0:T(8,128)(2,1)S(1)} collective-permute-done((bf16[384,256]{1,0:T(8,128)(2,1)S(1)}, bf16[384,256]{1,0:T(8,128)(2,1)S(1)}, u32[]{:S(2)}, u32[]{:S(2)}) %collective-permute-start.5) | collective-permute-done | bytes 196640 | tf_op jit(solution)/shard_map/ppermute | solution.py:46
  52.7 5.2 %collective-permute-start.6 = (bf16[384,256]{1,0:T(8,128)(2,1)S(1)}, bf16[384,256]{1,0:T(8,128)(2,1)S(1)}, u32[]{:S(2)}, u32[]{:S(2)}) collective-permute-start(bf16[384,256]{1,0:T(8,128)(2,1)S(1)} %fusion.5), channel_id=1, source_target_pairs={{4,0},{6,2},{8,4},{10,6},{12,8},{14,10},{0,12},{2,14},{5,1},{7,3},... | collective-permute-start | bytes 589832 | tf_op jit(solution)/shard_map/ppermute | solution.py:50
  62.1 13.7 %all-to-all-start = ((bf16[32,8,768]{2,1,0:T(8,128)(2,1)}), bf16[32,8,768]{2,1,0:T(8,128)(2,1)S(1)}, u32[]{:S(2)}, u32[]{:S(2)}) async-start(bf16[32,8,768]{2,1,0:T(8,128)(2,1)} %bitcast.14), calls=%async_computation | async-start | bytes 786432 | tf_op jit(solution)/shard_map/all_to_all | solution.py:89
  75.9 10.9 %all-to-all-done = bf16[32,8,768]{2,1,0:T(8,128)(2,1)S(1)} async-done(((bf16[32,8,768]{2,1,0:T(8,128)(2,1)}), bf16[32,8,768]{2,1,0:T(8,128)(2,1)S(1)}, u32[]{:S(2)}, u32[]{:S(2)}) %all-to-all-start) | async-done | bytes 393248 | tf_op jit(solution)/shard_map/all_to_all | solution.py:89
  95.7 4.0 %collective-permute-start.9 = (bf16[8,4096]{1,0:T(8,128)(2,1)S(1)}, bf16[8,4096]{1,0:T(8,128)(2,1)S(1)}, u32[]{:S(2)}, u32[]{:S(2)}) collective-permute-start(bf16[8,4096]{1,0:T(8,128)(2,1)S(1)} %get-tuple-element.6), channel_id=1, source_target_pairs={{0,48},{16,0},{32,16},{48,32},{64,112},{80,64},{96,80},{112,96},{1... | collective-permute-start | bytes 196616 | tf_op jit(solution)/shard_map/ppermute | solution.py:62
  102.5 5.4 %collective-permute-start.10 = (bf16[32,4096]{1,0:T(8,128)(2,1)S(1)}, bf16[32,4096]{1,0:T(8,128)(2,1)S(1)}, u32[]{:S(2)}, u32[]{:S(2)}) collective-permute-start(bf16[32,4096]{1,0:T(8,128)(2,1)S(1)} %pad_maximum_fusion), channel_id=1, source_target_pairs={{0,64},{16,80},{32,96},{48,112},{64,128},{80,144},{96,160},{112,17... | collective-permute-start | bytes 786440 | tf_op jit(solution)/shard_map/ppermute | solution.py:67
  109.9 3.3 %collective-permute-done.10 = bf16[32,4096]{1,0:T(8,128)(2,1)S(1)} collective-permute-done((bf16[32,4096]{1,0:T(8,128)(2,1)S(1)}, bf16[32,4096]{1,0:T(8,128)(2,1)S(1)}, u32[]{:S(2)}, u32[]{:S(2)}) %collective-permute-start.10) | collective-permute-done | bytes 262176 | tf_op jit(solution)/shard_map/ppermute | solution.py:67
  113.1 5.6 %collective-permute-start.11 = (bf16[32,4096]{1,0:T(8,128)(2,1)S(1)}, bf16[32,4096]{1,0:T(8,128)(2,1)S(1)}, u32[]{:S(2)}, u32[]{:S(2)}) collective-permute-start(bf16[32,4096]{1,0:T(8,128)(2,1)S(1)} %collective-permute-done.10), channel_id=1, source_target_pairs={{0,64},{16,80},{32,96},{48,112},{64,128},{80,144},{96,160},{112,17... | collective-permute-start | bytes 786440 | tf_op jit(solution)/shard_map/ppermute | solution.py:67
  121.0 4.1 %collective-permute-done.11 = bf16[32,4096]{1,0:T(8,128)(2,1)S(1)} collective-permute-done((bf16[32,4096]{1,0:T(8,128)(2,1)S(1)}, bf16[32,4096]{1,0:T(8,128)(2,1)S(1)}, u32[]{:S(2)}, u32[]{:S(2)}) %collective-permute-start.11) | collective-permute-done | bytes 262176 | tf_op jit(solution)/shard_map/ppermute | solution.py:67
  125.1 5.6 %collective-permute-start.12 = (bf16[32,4096]{1,0:T(8,128)(2,1)S(1)}, bf16[32,4096]{1,0:T(8,128)(2,1)S(1)}, u32[]{:S(2)}, u32[]{:S(2)}) collective-permute-start(bf16[32,4096]{1,0:T(8,128)(2,1)S(1)} %collective-permute-done.11), channel_id=1, source_target_pairs={{0,64},{16,80},{32,96},{48,112},{64,128},{80,144},{96,160},{112,17... | collective-permute-start | bytes 786440 | tf_op jit(solution)/shard_map/ppermute | solution.py:67
  135.2 5.6 %collective-permute-start.13 = (bf16[16,4096]{1,0:T(8,128)(2,1)S(1)}, bf16[16,4096]{1,0:T(8,128)(2,1)S(1)}, u32[]{:S(2)}, u32[]{:S(2)}) collective-permute-start(bf16[16,4096]{1,0:T(8,128)(2,1)S(1)} %slice.118), channel_id=1, source_target_pairs={{0,64},{16,80},{32,96},{48,112},{64,128},{80,144},{96,160},{112,17... | collective-permute-start | bytes 393224 | tf_op jit(solution)/shard_map/ppermute | solution.py:69
  143.4 6.1 %collective-permute-done.17 = bf16[16,4096]{1,0:T(8,128)(2,1)S(1)} collective-permute-done((bf16[16,4096]{1,0:T(8,128)(2,1)S(1)}, bf16[16,4096]{1,0:T(8,128)(2,1)S(1)}, u32[]{:S(2)}, u32[]{:S(2)}) %collective-permute-start.17) | collective-permute-done | bytes 131104 | tf_op jit(solution)/shard_map/ppermute | solution.py:70
  159.0 4.4 %collective-permute-start.21 = (bf16[256,128]{1,0:T(8,128)(2,1)S(1)}, bf16[256,128]{1,0:T(8,128)(2,1)S(1)}, u32[]{:S(2)}, u32[]{:S(2)}) collective-permute-start(bf16[256,128]{1,0:T(8,128)(2,1)S(1)} %get-tuple-element.20), channel_id=1, source_target_pairs={{4,0},{6,2},{8,4},{10,6},{12,8},{14,10},{0,12},{2,14},{5,1},{7,3},... | collective-permute-start | bytes 196616 | tf_op jit(solution)/shard_map/ppermute | solution.py:48
  163.4 3.9 %collective-permute-start.23 = (bf16[256,128]{1,0:T(8,128)(2,1)S(1)}, bf16[256,128]{1,0:T(8,128)(2,1)S(1)}, u32[]{:S(2)}, u32[]{:S(2)}) collective-permute-start(bf16[256,128]{1,0:T(8,128)(2,1)S(1)} %get-tuple-element.21), channel_id=1, source_target_pairs={{4,0},{6,2},{8,4},{10,6},{12,8},{14,10},{0,12},{2,14},{5,1},{7,3},... | collective-permute-start | bytes 196616 | tf_op jit(solution)/shard_map/ppermute | solution.py:46
  171.3 3.9 %collective-permute-done.20 = bf16[256,128]{1,0:T(8,128)(2,1)S(1)} collective-permute-done((bf16[256,128]{1,0:T(8,128)(2,1)S(1)}, bf16[256,128]{1,0:T(8,128)(2,1)S(1)}, u32[]{:S(2)}, u32[]{:S(2)}) %collective-permute-start.20) | collective-permute-done | bytes 65568 | tf_op jit(solution)/shard_map/ppermute | solution.py:49
  177.9 3.6 %collective-permute-done.24 = bf16[256,128]{1,0:T(8,128)(2,1)S(1)} collective-permute-done((bf16[256,128]{1,0:T(8,128)(2,1)S(1)}, bf16[256,128]{1,0:T(8,128)(2,1)S(1)}, u32[]{:S(2)}, u32[]{:S(2)}) %collective-permute-start.24) | collective-permute-done | bytes 65568 | tf_op jit(solution)/shard_map/ppermute | solution.py:50
  181.5 5.0 %collective-permute-start.25 = (bf16[512,128]{1,0:T(8,128)(2,1)S(1)}, bf16[512,128]{1,0:T(8,128)(2,1)S(1)}, u32[]{:S(2)}, u32[]{:S(2)}) collective-permute-start(bf16[512,128]{1,0:T(8,128)(2,1)S(1)} %pad_maximum_fusion.1), channel_id=1, source_target_pairs={{0,1},{1,0},{2,3},{3,2},{4,5},{5,4},{6,7},{7,6},{8,9},{9,8},{10,11... | collective-permute-start | bytes 393224 | tf_op jit(solution)/shard_map/ppermute | solution.py:117
  187.2 6.4 %collective-permute-done.25 = bf16[512,128]{1,0:T(8,128)(2,1)S(1)} collective-permute-done((bf16[512,128]{1,0:T(8,128)(2,1)S(1)}, bf16[512,128]{1,0:T(8,128)(2,1)S(1)}, u32[]{:S(2)}, u32[]{:S(2)}) %collective-permute-start.25) | collective-permute-done | bytes 131104 | tf_op jit(solution)/shard_map/ppermute | solution.py:117
  (108 shorter events, 60.0 us)
Async XLA Ops:
  7.2 142.4 %all-gather.2.cloned.1.call-start = ((), (), s32[]{:S(2)}) async-start(), calls=%async_computation.1 | async-start | bytes 1179648 | tf_op jit(solution)/shard_map/all_gather | solution.py:77
  33.7 13.1 %collective-permute-start.1 = (bf16[384,256]{1,0:T(8,128)(2,1)S(1)}, bf16[384,256]{1,0:T(8,128)(2,1)S(1)}, u32[]{:S(2)}, u32[]{:S(2)}) collective-permute-start(bf16[384,256]{1,0:T(8,128)(2,1)S(1)} %bitcast.127), channel_id=1, source_target_pairs={{0,4},{2,6},{4,8},{6,10},{8,12},{10,14},{12,0},{14,2},{1,5},{3,7},... | collective-permute-start | bytes 589832 | tf_op jit(solution)/shard_map/ppermute | solution.py:45
  37.2 20.7 %collective-permute-start.3 = (bf16[384,256]{1,0:T(8,128)(2,1)S(1)}, bf16[384,256]{1,0:T(8,128)(2,1)S(1)}, u32[]{:S(2)}, u32[]{:S(2)}) collective-permute-start(bf16[384,256]{1,0:T(8,128)(2,1)S(1)} %bitcast.128), channel_id=1, source_target_pairs={{4,0},{6,2},{8,4},{10,6},{12,8},{14,10},{0,12},{2,14},{5,1},{7,3},... | collective-permute-start | bytes 589832 | tf_op jit(solution)/shard_map/ppermute | solution.py:48
  40.9 11.7 %collective-permute-start.5 = (bf16[384,256]{1,0:T(8,128)(2,1)S(1)}, bf16[384,256]{1,0:T(8,128)(2,1)S(1)}, u32[]{:S(2)}, u32[]{:S(2)}) collective-permute-start(bf16[384,256]{1,0:T(8,128)(2,1)S(1)} %bitcast.130), channel_id=1, source_target_pairs={{4,0},{6,2},{8,4},{10,6},{12,8},{14,10},{0,12},{2,14},{5,1},{7,3},... | collective-permute-start | bytes 589832 | tf_op jit(solution)/shard_map/ppermute | solution.py:46
  44.4 16.3 %collective-permute-start.4 = (bf16[384,256]{1,0:T(8,128)(2,1)S(1)}, bf16[384,256]{1,0:T(8,128)(2,1)S(1)}, u32[]{:S(2)}, u32[]{:S(2)}) collective-permute-start(bf16[384,256]{1,0:T(8,128)(2,1)S(1)} %bitcast.129), channel_id=1, source_target_pairs={{0,4},{2,6},{4,8},{6,10},{8,12},{10,14},{12,0},{14,2},{1,5},{3,7},... | collective-permute-start | bytes 589832 | tf_op jit(solution)/shard_map/ppermute | solution.py:47
  46.8 13.8 %collective-permute-start.2 = (bf16[384,256]{1,0:T(8,128)(2,1)S(1)}, bf16[384,256]{1,0:T(8,128)(2,1)S(1)}, u32[]{:S(2)}, u32[]{:S(2)}) collective-permute-start(bf16[384,256]{1,0:T(8,128)(2,1)S(1)} %fusion.8), channel_id=1, source_target_pairs={{0,4},{2,6},{4,8},{6,10},{8,12},{10,14},{12,0},{14,2},{1,5},{3,7},... | collective-permute-start | bytes 589832 | tf_op jit(solution)/shard_map/ppermute | solution.py:49
  52.7 8.4 %collective-permute-start.6 = (bf16[384,256]{1,0:T(8,128)(2,1)S(1)}, bf16[384,256]{1,0:T(8,128)(2,1)S(1)}, u32[]{:S(2)}, u32[]{:S(2)}) collective-permute-start(bf16[384,256]{1,0:T(8,128)(2,1)S(1)} %fusion.5), channel_id=1, source_target_pairs={{4,0},{6,2},{8,4},{10,6},{12,8},{14,10},{0,12},{2,14},{5,1},{7,3},... | collective-permute-start | bytes 589832 | tf_op jit(solution)/shard_map/ppermute | solution.py:50
  62.1 24.7 %all-to-all-start = ((bf16[32,8,768]{2,1,0:T(8,128)(2,1)}), bf16[32,8,768]{2,1,0:T(8,128)(2,1)S(1)}, u32[]{:S(2)}, u32[]{:S(2)}) async-start(bf16[32,8,768]{2,1,0:T(8,128)(2,1)} %bitcast.14), calls=%async_computation | async-start | bytes 786432 | tf_op jit(solution)/shard_map/all_to_all | solution.py:89
  90.2 10.2 %collective-permute-start.7 = (bf16[8,4096]{1,0:T(8,128)(2,1)S(1)}, bf16[8,4096]{1,0:T(8,128)(2,1)S(1)}, u32[]{:S(2)}, u32[]{:S(2)}) collective-permute-start(bf16[8,4096]{1,0:T(8,128)(2,1)S(1)} %get-tuple-element.6), channel_id=1, source_target_pairs={{0,16},{16,32},{32,48},{48,0},{64,80},{80,96},{96,112},{112,64},{1... | collective-permute-start | bytes 196616 | tf_op jit(solution)/shard_map/ppermute | solution.py:62
  92.6 7.8 %collective-permute-start.8 = (bf16[8,4096]{1,0:T(8,128)(2,1)S(1)}, bf16[8,4096]{1,0:T(8,128)(2,1)S(1)}, u32[]{:S(2)}, u32[]{:S(2)}) collective-permute-start(bf16[8,4096]{1,0:T(8,128)(2,1)S(1)} %get-tuple-element.6), channel_id=1, source_target_pairs={{0,32},{16,48},{32,0},{48,16},{64,96},{80,112},{96,64},{112,80},{1... | collective-permute-start | bytes 196616 | tf_op jit(solution)/shard_map/ppermute | solution.py:62
  102.5 10.6 %collective-permute-start.10 = (bf16[32,4096]{1,0:T(8,128)(2,1)S(1)}, bf16[32,4096]{1,0:T(8,128)(2,1)S(1)}, u32[]{:S(2)}, u32[]{:S(2)}) collective-permute-start(bf16[32,4096]{1,0:T(8,128)(2,1)S(1)} %pad_maximum_fusion), channel_id=1, source_target_pairs={{0,64},{16,80},{32,96},{48,112},{64,128},{80,144},{96,160},{112,17... | collective-permute-start | bytes 786440 | tf_op jit(solution)/shard_map/ppermute | solution.py:67
  107.9 11.1 %collective-permute-start.14 = (bf16[32,4096]{1,0:T(8,128)(2,1)S(1)}, bf16[32,4096]{1,0:T(8,128)(2,1)S(1)}, u32[]{:S(2)}, u32[]{:S(2)}) collective-permute-start(bf16[32,4096]{1,0:T(8,128)(2,1)S(1)} %pad_maximum_fusion), channel_id=1, source_target_pairs={{64,0},{80,16},{96,32},{112,48},{128,64},{144,80},{160,96},{176,11... | collective-permute-start | bytes 786440 | tf_op jit(solution)/shard_map/ppermute | solution.py:68
  113.1 12.0 %collective-permute-start.11 = (bf16[32,4096]{1,0:T(8,128)(2,1)S(1)}, bf16[32,4096]{1,0:T(8,128)(2,1)S(1)}, u32[]{:S(2)}, u32[]{:S(2)}) collective-permute-start(bf16[32,4096]{1,0:T(8,128)(2,1)S(1)} %collective-permute-done.10), channel_id=1, source_target_pairs={{0,64},{16,80},{32,96},{48,112},{64,128},{80,144},{96,160},{112,17... | collective-permute-start | bytes 786440 | tf_op jit(solution)/shard_map/ppermute | solution.py:67
  119.1 12.3 %collective-permute-start.15 = (bf16[32,4096]{1,0:T(8,128)(2,1)S(1)}, bf16[32,4096]{1,0:T(8,128)(2,1)S(1)}, u32[]{:S(2)}, u32[]{:S(2)}) collective-permute-start(bf16[32,4096]{1,0:T(8,128)(2,1)S(1)} %collective-permute-done.14), channel_id=1, source_target_pairs={{64,0},{80,16},{96,32},{112,48},{128,64},{144,80},{160,96},{176,11... | collective-permute-start | bytes 786440 | tf_op jit(solution)/shard_map/ppermute | solution.py:68
  125.1 10.1 %collective-permute-start.12 = (bf16[32,4096]{1,0:T(8,128)(2,1)S(1)}, bf16[32,4096]{1,0:T(8,128)(2,1)S(1)}, u32[]{:S(2)}, u32[]{:S(2)}) collective-permute-start(bf16[32,4096]{1,0:T(8,128)(2,1)S(1)} %collective-permute-done.11), channel_id=1, source_target_pairs={{0,64},{16,80},{32,96},{48,112},{64,128},{80,144},{96,160},{112,17... | collective-permute-start | bytes 786440 | tf_op jit(solution)/shard_map/ppermute | solution.py:67
  131.3 10.0 %collective-permute-start.16 = (bf16[32,4096]{1,0:T(8,128)(2,1)S(1)}, bf16[32,4096]{1,0:T(8,128)(2,1)S(1)}, u32[]{:S(2)}, u32[]{:S(2)}) collective-permute-start(bf16[32,4096]{1,0:T(8,128)(2,1)S(1)} %collective-permute-done.15), channel_id=1, source_target_pairs={{64,0},{80,16},{96,32},{112,48},{128,64},{144,80},{160,96},{176,11... | collective-permute-start | bytes 786440 | tf_op jit(solution)/shard_map/ppermute | solution.py:68
  135.2 8.2 %collective-permute-start.13 = (bf16[16,4096]{1,0:T(8,128)(2,1)S(1)}, bf16[16,4096]{1,0:T(8,128)(2,1)S(1)}, u32[]{:S(2)}, u32[]{:S(2)}) collective-permute-start(bf16[16,4096]{1,0:T(8,128)(2,1)S(1)} %slice.118), channel_id=1, source_target_pairs={{0,64},{16,80},{32,96},{48,112},{64,128},{80,144},{96,160},{112,17... | collective-permute-start | bytes 393224 | tf_op jit(solution)/shard_map/ppermute | solution.py:69
  141.4 8.1 %collective-permute-start.17 = (bf16[16,4096]{1,0:T(8,128)(2,1)S(1)}, bf16[16,4096]{1,0:T(8,128)(2,1)S(1)}, u32[]{:S(2)}, u32[]{:S(2)}) collective-permute-start(bf16[16,4096]{1,0:T(8,128)(2,1)S(1)} %slice.119), channel_id=1, source_target_pairs={{64,0},{80,16},{96,32},{112,48},{128,64},{144,80},{160,96},{176,11... | collective-permute-start | bytes 393224 | tf_op jit(solution)/shard_map/ppermute | solution.py:70
  156.4 11.0 %collective-permute-start.19 = (bf16[256,128]{1,0:T(8,128)(2,1)S(1)}, bf16[256,128]{1,0:T(8,128)(2,1)S(1)}, u32[]{:S(2)}, u32[]{:S(2)}) collective-permute-start(bf16[256,128]{1,0:T(8,128)(2,1)S(1)} %get-tuple-element.19), channel_id=1, source_target_pairs={{0,4},{2,6},{4,8},{6,10},{8,12},{10,14},{12,0},{14,2},{1,5},{3,7},... | collective-permute-start | bytes 196616 | tf_op jit(solution)/shard_map/ppermute | solution.py:45
  159.0 12.3 %collective-permute-start.21 = (bf16[256,128]{1,0:T(8,128)(2,1)S(1)}, bf16[256,128]{1,0:T(8,128)(2,1)S(1)}, u32[]{:S(2)}, u32[]{:S(2)}) collective-permute-start(bf16[256,128]{1,0:T(8,128)(2,1)S(1)} %get-tuple-element.20), channel_id=1, source_target_pairs={{4,0},{6,2},{8,4},{10,6},{12,8},{14,10},{0,12},{2,14},{5,1},{7,3},... | collective-permute-start | bytes 196616 | tf_op jit(solution)/shard_map/ppermute | solution.py:48
  163.4 7.8 %collective-permute-start.23 = (bf16[256,128]{1,0:T(8,128)(2,1)S(1)}, bf16[256,128]{1,0:T(8,128)(2,1)S(1)}, u32[]{:S(2)}, u32[]{:S(2)}) collective-permute-start(bf16[256,128]{1,0:T(8,128)(2,1)S(1)} %get-tuple-element.21), channel_id=1, source_target_pairs={{4,0},{6,2},{8,4},{10,6},{12,8},{14,10},{0,12},{2,14},{5,1},{7,3},... | collective-permute-start | bytes 196616 | tf_op jit(solution)/shard_map/ppermute | solution.py:46
  167.4 7.8 %collective-permute-start.20 = (bf16[256,128]{1,0:T(8,128)(2,1)S(1)}, bf16[256,128]{1,0:T(8,128)(2,1)S(1)}, u32[]{:S(2)}, u32[]{:S(2)}) collective-permute-start(bf16[256,128]{1,0:T(8,128)(2,1)S(1)} %fusion.22), channel_id=1, source_target_pairs={{0,4},{2,6},{4,8},{6,10},{8,12},{10,14},{12,0},{14,2},{1,5},{3,7},... | collective-permute-start | bytes 196616 | tf_op jit(solution)/shard_map/ppermute | solution.py:49
  169.3 8.5 %collective-permute-start.22 = (bf16[256,128]{1,0:T(8,128)(2,1)S(1)}, bf16[256,128]{1,0:T(8,128)(2,1)S(1)}, u32[]{:S(2)}, u32[]{:S(2)}) collective-permute-start(bf16[256,128]{1,0:T(8,128)(2,1)S(1)} %get-tuple-element.22), channel_id=1, source_target_pairs={{0,4},{2,6},{4,8},{6,10},{8,12},{10,14},{12,0},{14,2},{1,5},{3,7},... | collective-permute-start | bytes 196616 | tf_op jit(solution)/shard_map/ppermute | solution.py:47
  181.5 12.2 %collective-permute-start.25 = (bf16[512,128]{1,0:T(8,128)(2,1)S(1)}, bf16[512,128]{1,0:T(8,128)(2,1)S(1)}, u32[]{:S(2)}, u32[]{:S(2)}) collective-permute-start(bf16[512,128]{1,0:T(8,128)(2,1)S(1)} %pad_maximum_fusion.1), channel_id=1, source_target_pairs={{0,1},{1,0},{2,3},{3,2},{4,5},{5,4},{6,7},{7,6},{8,9},{9,8},{10,11... | collective-permute-start | bytes 393224 | tf_op jit(solution)/shard_map/ppermute | solution.py:117
  (10 other events, 148.1 us)
Sparse Core Ops, SparseCore 0:
  24.6 34.1 all-gather.1

commit v2 on v1

v2 whole, which is shorter than its diff:
```python
import jax
import jax.numpy as jnp
from jax import lax
from jax.experimental import pallas as pl
from jax.experimental.pallas import tpu as pltpu
from jax.sharding import PartitionSpec as P

N_X = 4
N_CORE = 2
N_Y = 8
N_Z = 4
VMEM = 12 * 2**20

def swaps(size, partner):
    return [(i, partner(i)) for i in range(size)]


CORE_SWAP = swaps(N_X * N_CORE, lambda h: h ^ 1)
X_EVEN = swaps(N_X * N_CORE, lambda h: h ^ 2)
X_ODD = swaps(N_X * N_CORE, lambda h: h ^ 6)
Z_NEAR = swaps(N_Y * N_Z, lambda n: n ^ 1)
Z_FAR = swaps(N_Y * N_Z, lambda n: n ^ 2)
Y_EVEN = swaps(N_Y * N_Z, lambda n: n ^ N_Z)
Y_ODD = swaps(N_Y * N_Z, lambda n: (((n // N_Z + 1) ^ 1) - 1) % N_Y * N_Z + n % N_Z)
DP_SWAP = swaps(2, lambda d: d ^ 1)
Y_DISTANCE = (0, 1, -1, 2, -2, 3, -3, 4)
Y_SLOT = (0, 1, 3, 5, 7, 6, 4, 2)


def add(*terms):
    total = terms[0].astype(jnp.float32)
    for term in terms[1:]:
        total = total + term.astype(jnp.float32)
    return total


def pack_kernel(columns_ref, rows_ref, out_ref):
    out_ref[...] = rows_ref[...]


def pair_kernel(columns_ref, rows_ref, got_ref, a_keep, a_send, b_keep, b_send):
    step = pl.program_id(0)
    total = add(rows_ref[...], got_ref[...]).astype(a_keep.dtype)
    half = total.shape[0] // 2

    @pl.when(step <= 1)
    def _():
        a_keep[0] = total[:half]

    @pl.when(step >= 2)
    def _():
        a_send[0] = total[:half]

    @pl.when(step % 2 == 0)
    def _():
        b_keep[0] = total[half:]

    @pl.when(step % 2 == 1)
    def _():
        b_send[0] = total[half:]


def turn_kernel(a_keep, a_one, a_two, b_keep, b_one, b_two, out_ref):
    half = a_two.shape[0]
    for first, keep, one, two in ((0, a_keep, a_one, a_two), (half, b_keep, b_one, b_two)):
        for row in range(0, half, 128):
            rows = slice(row, row + 128)
            total = add(keep[0, rows], one[0, rows], two[rows])
            out_ref[:, first + row : first + row + 128] = total.T.astype(out_ref.dtype)


def sum_partials(flat):
    rows, samples = flat.shape[0], flat.shape[1] // (N_X * N_CORE)
    half = rows // 2
    h = lax.axis_index("hst")
    x, core = h // N_CORE, h % N_CORE
    column = (x ^ jnp.array([0, 3, 1, 2], jnp.int32)) * N_CORE
    params = pltpu.CompilerParams(vmem_limit_bytes=VMEM)
    block = pl.BlockSpec((rows, samples), lambda j, c: (j, 0))
    picked = pl.BlockSpec((rows, samples), lambda j, c: (0, c[j]))
    given = pl.pallas_call(
        pack_kernel,
        out_shape=jax.ShapeDtypeStruct((N_X * rows, samples), flat.dtype),
        grid_spec=pltpu.PrefetchScalarGridSpec(
            num_scalar_prefetch=1, grid=(N_X,), in_specs=[picked], out_specs=block
        ),
        compiler_params=params,
        name="pack",
    )(column + (1 - core), flat)
    got = lax.ppermute(given, "hst", CORE_SWAP)

    def half_block(index):
        return pl.BlockSpec((1, half, samples), lambda j, c: (index(j), 0, 0))

    a_keep, a_send, b_keep, b_send = pl.pallas_call(
        pair_kernel,
        out_shape=[jax.ShapeDtypeStruct((2, half, samples), flat.dtype)] * 4,
        grid_spec=pltpu.PrefetchScalarGridSpec(
            num_scalar_prefetch=1,
            grid=(N_X,),
            in_specs=[picked, block],
            out_specs=[
                half_block(lambda j: jnp.minimum(j, 1)),
                half_block(lambda j: j // 3),
                half_block(lambda j: j // 2),
                half_block(lambda j: j // 3),
            ],
        ),
        compiler_params=params,
        name="pair",
    )(column + core, flat, got)
    a_one = lax.ppermute(a_send, "hst", X_EVEN)
    b_one = lax.ppermute(b_send, "hst", X_ODD)
    a_two = lax.ppermute(add(a_keep[1], a_one[1]).astype(flat.dtype), "hst", X_ODD)
    b_two = lax.ppermute(add(b_keep[1], b_one[1]).astype(flat.dtype), "hst", X_EVEN)
    return pl.pallas_call(
        turn_kernel,
        out_shape=jax.ShapeDtypeStruct((samples, rows), flat.dtype),
        compiler_params=params,
        name="turn",
    )(a_keep, a_one, a_two, b_keep, b_one, b_two)


def normalize(flat_rows, ln_gain):
    middle = jnp.mean(flat_rows, axis=-1, keepdims=True)
    centered = flat_rows - middle
    variance = jnp.mean(centered * centered, axis=-1, keepdims=True)
    return (centered * lax.rsqrt(variance + 1e-05) * ln_gain).astype(jnp.bfloat16)


def gather_nodes(block):
    near = jnp.concatenate([block, lax.ppermute(block, "node", Z_NEAR)], 0)
    line = jnp.concatenate([near, lax.ppermute(near, "node", Z_FAR)], 0)
    half = line.shape[0] // 2
    even, odd = line, line
    blocks = [line]
    for _ in range(3):
        even, odd = lax.ppermute(odd, "node", Y_EVEN), lax.ppermute(even, "node", Y_ODD)
        blocks += [even, odd]
    blocks.append(lax.ppermute(odd[:half], "node", Y_EVEN))
    blocks.append(lax.ppermute(even[half:], "node", Y_ODD))
    return jnp.concatenate(blocks, 0)


def node_order():
    n = lax.axis_index("node")
    y, z = n // N_Z, n % N_Z
    sign = 1 - 2 * (y % 2)
    step = jnp.arange(N_Y * N_Z)
    nodes = (y + sign * jnp.array(Y_DISTANCE)[step // N_Z]) % N_Y * N_Z + (z ^ (step % N_Z))
    slots = jnp.array(Y_SLOT)[(sign * (step // N_Z - y)) % N_Y] * N_Z + (z ^ (step % N_Z))
    return nodes, slots


def local(partials, counts, perm, fm_proj, ln_gain, w_in, d_hidden):
    samples = counts.shape[2]
    group, hidden_here = d_hidden.shape[2], d_hidden.shape[3]
    w_full = lax.all_gather(w_in, "hst", axis=0, tiled=True)

    nodes, slots = node_order()
    d_hid = jnp.take(d_hidden[0, 0].reshape(-1, samples, hidden_here), nodes, axis=0, mode="clip")
    d_hid = d_hid.reshape(group, hidden_here)

    rows = partials.shape[2] * partials.shape[3]
    summed = sum_partials(partials[0].transpose(1, 2, 0).reshape(rows, -1))
    shard_rows = lax.all_to_all(
        summed.reshape(N_Y * N_Z, samples, rows), "node", split_axis=0, concat_axis=0, tiled=True
    )
    shard_rows = shard_rows.transpose(1, 0, 2).reshape(samples, -1, partials.shape[3])
    ordered = jnp.take(shard_rows, perm, axis=1, mode="clip")
    counts_here = counts[0, 0]
    divisor = jnp.maximum(counts_here, 1).astype(jnp.float32)[:, :, None]
    pooled = jnp.where(
        counts_here[:, :, None] > 0, ordered.astype(jnp.float32) / divisor, 0.0
    ).astype(jnp.bfloat16)
    projected = jnp.einsum(
        "sfe,fk->sek", pooled, fm_proj, preferred_element_type=jnp.float32
    ).astype(jnp.bfloat16)
    pairwise = jnp.einsum("sfe,sek->sfk", pooled, projected, preferred_element_type=jnp.float32)
    z_local = normalize(pairwise.reshape(samples, -1), ln_gain)

    z_group = gather_nodes(z_local)
    pre_act = jnp.dot(z_group, w_full, preferred_element_type=jnp.float32)
    sigma = jax.nn.sigmoid(pre_act)
    hidden = (pre_act * sigma).astype(jnp.bfloat16).reshape(-1, samples, hidden_here)
    hidden = jnp.take(hidden, slots, axis=0, mode="clip")
    d_pre = (d_hid.astype(jnp.float32) * sigma * (1.0 + pre_act * (1.0 - sigma))).astype(
        jnp.bfloat16
    )
    term = lax.dot_general(
        z_group, d_pre, (((0,), (0,)), ((), ())), preferred_element_type=jnp.float32
    ).astype(jnp.bfloat16)
    terms = lax.all_to_all(
        term.reshape(N_X * N_CORE, w_in.shape[0], hidden_here), "hst", 0, 0, tiled=True
    )
    share = add(*[terms[i] for i in range(N_X * N_CORE)]).astype(jnp.bfloat16)
    other = lax.ppermute(share, "dp", DP_SWAP)
    grad_w = add(share, other)
    return (hidden.reshape(1, 1, group, hidden_here), grad_w)


def solution(mesh):
    in_specs = (
        P("hst", "dp", "node", None),
        P("dp", "hst", "node", None),
        P(),
        P(),
        P(),
        P("hst", "node"),
        P("dp", "hst", None, "node"),
    )
    out_specs = (P("dp", "hst", None, "node"), P("hst", "node"))
    return jax.shard_map(local, mesh=mesh, in_specs=in_specs, out_specs=out_specs, check_vma=False)
```

time: 202 us -> 182 us (0.901); the launches traced: 201 us -> 178 us
  starting transfers between devices: 99.2 us -> 74.6 us
  waiting for transfers between devices: 55.9 us -> 71.4 us
  other arithmetic: 15.4 us -> 2.25 us
  local copies, waits for them, and re-layouts: 12.6 us -> 7.67 us
  Pallas kernels: 0 us -> 3.61 us
    ppermute x25 -> x15, starting transfers between devices: 80.4 us -> 47.4 us  [the longest x3 14.1 us: gather_nodes(): lax.ppermute(even, 'node', Y_ODD)]
    all_to_all x0 -> x1, waiting for transfers between devices: none -> 15.2 us  [local(): lax.all_to_all(term.reshape(N_X * N_CORE, w_in.shape[0], hidden_here), 'h...]
    dynamic_slice x1 -> x0, other arithmetic: 7.4 us -> none  [scatter_sum(): given = lax.dynamic_index_in_dim(pieces, 1 - c, 1, keepdims=False)]
    ppermute x1, starting transfers between devices: 4.99 us -> 10.4 us  [local(): other = lax.ppermute(share, 'dp', DP_SWAP)]
    reshape x1 -> x0, local copies, waits for them, and re-layouts: 4.75 us -> none  [local(): partials[0].transpose(1, 2, 0).reshape(rows, N_X, N_CORE, group)]
    all_to_all x0 -> x1, starting transfers between devices: none -> 3.69 us  [local(): lax.all_to_all(term.reshape(N_X * N_CORE, w_in.shape[0], hidden_here), 'h...]
    pallas_call x0 -> x3, Pallas kernels: none -> 3.61 us  [the longest x1 1.66 us: sum_partials(): pl.pallas_call(pair_kernel, out_shape=[jax.ShapeDtypeStruct((2, half, sam...]
    slice x1 -> x0, other arithmetic: 3.15 us -> none  [scatter_sum(): own[:half]]
  transfers between devices with their start and end apart: 28 -> 19, of which waited for: 17 -> 14; matrix products, arithmetic and copies ran while one was open for 6% -> 4% of each run, Pallas kernels for 0% -> 1%
where the time goes in v2:
time: 182 us; the launch traced here: 178 us
  starting transfers between devices  74.6 us (41%)
  waiting for transfers between devices  71.4 us (39%)
  between operations  14.6 us (8%)
  local copies, waits for them, and re-layouts  7.67 us (4%)
  matrix products  4.3 us (2%)
  Pallas kernels  3.61 us (2%)
  other arithmetic  2.25 us (1%)
    all_to_all x1, waiting for transfers between devices, local(): lax.all_to_all(term.reshape(N_X * N_CORE, w_in.shape[0], hidden_here), 'h...  15.2 us
    ppermute x3, starting transfers between devices, gather_nodes(): lax.ppermute(even, 'node', Y_ODD)  14.1 us
    all_to_all x1, starting transfers between devices, local(): lax.all_to_all(summed.reshape(N_Y * N_Z, samples, rows), 'node', split_ax...  13.1 us
    all_to_all x1, waiting for transfers between devices, local(): lax.all_to_all(summed.reshape(N_Y * N_Z, samples, rows), 'node', split_ax...  10.7 us
    ppermute x1, starting transfers between devices, local(): other = lax.ppermute(share, 'dp', DP_SWAP)  10.4 us
    ppermute x3, waiting for transfers between devices, gather_nodes(): lax.ppermute(odd, 'node', Y_EVEN)  8.18 us
    ppermute x1, waiting for transfers between devices, gather_nodes(): line = jnp.concatenate([near, lax.ppermute(near, 'node', Z_FAR)], 0)  7.16 us
    ppermute x3, starting transfers between devices, gather_nodes(): lax.ppermute(odd, 'node', Y_EVEN)  6.33 us
  transfers between devices with their start and end apart: 19, of which 14 were waited for; matrix products, arithmetic and copies ran while one was open for 4% of the time, Pallas kernels for 1%

profile of v2, /device:TPU:56, one launch (start us, length us, event | category | flops | bytes accessed | tf_op | source)
XLA Modules:
  0.0 178.4 jit_solution(11078427987128417511)
XLA Ops:
  12.7 3.4 %collective-permute-done.got_ref = bf16[3072,256]{1,0:T(8,128)(2,1)S(1)} collective-permute-done((bf16[3072,256]{1,0:T(8,128)(2,1)S(1)}, bf16[3072,256]{1,0:T(8,128)(2,1)S(1)}, u32[]{:S(2)}, u32[]{:S(2)}) %collective-permute-start) | collective-permute-done | bytes 1572896 | tf_op jit(solution)/shard_map/ppermute | solution.py:90
  17.8 3.4 %collective-permute-start.1 = (bf16[2,384,256]{2,1,0:T(8,128)(2,1)S(1)}, bf16[2,384,256]{2,1,0:T(8,128)(2,1)S(1)}, u32[]{:S(2)}, u32[]{:S(2)}) collective-permute-start(bf16[2,384,256]{2,1,0:T(8,128)(2,1)S(1)} %get-tuple-element.7), channel_id=1, source_target_pairs={{0,4},{2,6},{4,0},{6,2},{8,12},{10,14},{12,8},{14,10},{1,5},{3,7},... | collective-permute-start | bytes 1179656 | tf_op jit(solution)/shard_map/ppermute | solution.py:112
  21.2 4.0 %collective-permute-start.3 = (bf16[2,384,256]{2,1,0:T(8,128)(2,1)S(1)}, bf16[2,384,256]{2,1,0:T(8,128)(2,1)S(1)}, u32[]{:S(2)}, u32[]{:S(2)}) collective-permute-start(bf16[2,384,256]{2,1,0:T(8,128)(2,1)S(1)} %get-tuple-element.9), channel_id=1, source_target_pairs={{0,12},{2,14},{4,8},{6,10},{8,4},{10,6},{12,0},{14,2},{1,13},{3,15... | collective-permute-start | bytes 1179656 | tf_op jit(solution)/shard_map/ppermute | solution.py:113
  25.3 5.6 %collective-permute-done.1.a_one = bf16[2,384,256]{2,1,0:T(8,128)(2,1)S(1)} collective-permute-done((bf16[2,384,256]{2,1,0:T(8,128)(2,1)S(1)}, bf16[2,384,256]{2,1,0:T(8,128)(2,1)S(1)}, u32[]{:S(2)}, u32[]{:S(2)}) %collective-permute-start.1) | collective-permute-done | bytes 393248 | tf_op jit(solution)/shard_map/ppermute | solution.py:112
  30.9 4.7 %collective-permute-start.2 = (bf16[384,256]{1,0:T(8,128)(2,1)S(1)}, bf16[384,256]{1,0:T(8,128)(2,1)S(1)}, u32[]{:S(2)}, u32[]{:S(2)}) collective-permute-start(bf16[384,256]{1,0:T(8,128)(2,1)S(1)} %fusion.7), channel_id=1, source_target_pairs={{0,12},{2,14},{4,8},{6,10},{8,4},{10,6},{12,0},{14,2},{1,13},{3,15... | collective-permute-start | bytes 589832 | tf_op jit(solution)/shard_map/ppermute | solution.py:114
  35.6 2.1 %collective-permute-start.4 = (bf16[384,256]{1,0:T(8,128)(2,1)S(1)}, bf16[384,256]{1,0:T(8,128)(2,1)S(1)}, u32[]{:S(2)}, u32[]{:S(2)}) collective-permute-start(bf16[384,256]{1,0:T(8,128)(2,1)S(1)} %fusion.8), channel_id=1, source_target_pairs={{0,4},{2,6},{4,0},{6,2},{8,12},{10,14},{12,8},{14,10},{1,5},{3,7},... | collective-permute-start | bytes 589832 | tf_op jit(solution)/shard_map/ppermute | solution.py:115
  40.1 3.3 %collective-permute-done.4.b_two = bf16[384,256]{1,0:T(8,128)(2,1)S(1)} collective-permute-done((bf16[384,256]{1,0:T(8,128)(2,1)S(1)}, bf16[384,256]{1,0:T(8,128)(2,1)S(1)}, u32[]{:S(2)}, u32[]{:S(2)}) %collective-permute-start.4) | collective-permute-done | bytes 196640 | tf_op jit(solution)/shard_map/ppermute | solution.py:115
  44.3 13.1 %all-to-all-start = ((bf16[32,8,768]{2,1,0:T(8,128)(2,1)}), bf16[32,8,768]{2,1,0:T(8,128)(2,1)S(1)}, u32[]{:S(2)}, u32[]{:S(2)}) async-start(bf16[32,8,768]{2,1,0:T(8,128)(2,1)} %bitcast.8), calls=%async_computation | async-start | bytes 786432 | tf_op jit(solution)/shard_map/all_to_all | solution.py:166
  57.5 10.7 %all-to-all-done = bf16[32,8,768]{2,1,0:T(8,128)(2,1)S(1)} async-done(((bf16[32,8,768]{2,1,0:T(8,128)(2,1)}), bf16[32,8,768]{2,1,0:T(8,128)(2,1)S(1)}, u32[]{:S(2)}, u32[]{:S(2)}) %all-to-all-start) | async-done | bytes 393248 | tf_op jit(solution)/shard_map/all_to_all | solution.py:166
  71.6 2.5 %collective-permute-start.5 = (bf16[8,4096]{1,0:T(8,128)(2,1)S(1)}, bf16[8,4096]{1,0:T(8,128)(2,1)S(1)}, u32[]{:S(2)}, u32[]{:S(2)}) collective-permute-start(bf16[8,4096]{1,0:T(8,128)(2,1)S(1)} %get-tuple-element.11), channel_id=1, source_target_pairs={{0,16},{16,0},{32,48},{48,32},{64,80},{80,64},{96,112},{112,96},{1... | collective-permute-start | bytes 196616 | tf_op jit(solution)/shard_map/ppermute | solution.py:132
  74.7 3.5 %collective-permute-done.5 = bf16[8,4096]{1,0:T(8,128)(2,1)S(1)} collective-permute-done((bf16[8,4096]{1,0:T(8,128)(2,1)S(1)}, bf16[8,4096]{1,0:T(8,128)(2,1)S(1)}, u32[]{:S(2)}, u32[]{:S(2)}) %collective-permute-start.5) | collective-permute-done | bytes 65568 | tf_op jit(solution)/shard_map/ppermute | solution.py:132
  80.3 7.2 %collective-permute-done.6 = bf16[16,4096]{1,0:T(8,128)(2,1)S(1)} collective-permute-done((bf16[16,4096]{1,0:T(8,128)(2,1)S(1)}, bf16[16,4096]{1,0:T(8,128)(2,1)S(1)}, u32[]{:S(2)}, u32[]{:S(2)}) %collective-permute-start.6) | collective-permute-done | bytes 131104 | tf_op jit(solution)/shard_map/ppermute | solution.py:133
  87.4 2.5 %collective-permute-start.7 = (bf16[32,4096]{1,0:T(8,128)(2,1)S(1)}, bf16[32,4096]{1,0:T(8,128)(2,1)S(1)}, u32[]{:S(2)}, u32[]{:S(2)}) collective-permute-start(bf16[32,4096]{1,0:T(8,128)(2,1)S(1)} %pad_maximum_fusion), channel_id=1, source_target_pairs={{0,64},{16,80},{32,96},{48,112},{64,0},{80,16},{96,32},{112,48},{1... | collective-permute-start | bytes 786440 | tf_op jit(solution)/shard_map/ppermute | solution.py:138
  89.9 4.9 %collective-permute-start.8 = (bf16[32,4096]{1,0:T(8,128)(2,1)S(1)}, bf16[32,4096]{1,0:T(8,128)(2,1)S(1)}, u32[]{:S(2)}, u32[]{:S(2)}) collective-permute-start(bf16[32,4096]{1,0:T(8,128)(2,1)S(1)} %pad_maximum_fusion), channel_id=1, source_target_pairs={{0,448},{16,464},{32,480},{48,496},{64,128},{80,144},{96,160},{112... | collective-permute-start | bytes 786440 | tf_op jit(solution)/shard_map/ppermute | solution.py:138
  95.7 4.8 %collective-permute-start.10 = (bf16[32,4096]{1,0:T(8,128)(2,1)S(1)}, bf16[32,4096]{1,0:T(8,128)(2,1)S(1)}, u32[]{:S(2)}, u32[]{:S(2)}) collective-permute-start(bf16[32,4096]{1,0:T(8,128)(2,1)S(1)} %collective-permute-done.7), channel_id=1, source_target_pairs={{0,448},{16,464},{32,480},{48,496},{64,128},{80,144},{96,160},{112... | collective-permute-start | bytes 786440 | tf_op jit(solution)/shard_map/ppermute | solution.py:138
  102.5 7.3 %collective-permute-done.9 = bf16[32,4096]{1,0:T(8,128)(2,1)S(1)} collective-permute-done((bf16[32,4096]{1,0:T(8,128)(2,1)S(1)}, bf16[32,4096]{1,0:T(8,128)(2,1)S(1)}, u32[]{:S(2)}, u32[]{:S(2)}) %collective-permute-start.9) | collective-permute-done | bytes 262176 | tf_op jit(solution)/shard_map/ppermute | solution.py:138
  109.8 4.5 %collective-permute-start.12 = (bf16[32,4096]{1,0:T(8,128)(2,1)S(1)}, bf16[32,4096]{1,0:T(8,128)(2,1)S(1)}, u32[]{:S(2)}, u32[]{:S(2)}) collective-permute-start(bf16[32,4096]{1,0:T(8,128)(2,1)S(1)} %collective-permute-done.9), channel_id=1, source_target_pairs={{0,448},{16,464},{32,480},{48,496},{64,128},{80,144},{96,160},{112... | collective-permute-start | bytes 786440 | tf_op jit(solution)/shard_map/ppermute | solution.py:138
  116.3 4.4 %collective-permute-done.12 = bf16[32,4096]{1,0:T(8,128)(2,1)S(1)} collective-permute-done((bf16[32,4096]{1,0:T(8,128)(2,1)S(1)}, bf16[32,4096]{1,0:T(8,128)(2,1)S(1)}, u32[]{:S(2)}, u32[]{:S(2)}) %collective-permute-start.12) | collective-permute-done | bytes 262176 | tf_op jit(solution)/shard_map/ppermute | solution.py:138
  122.6 4.4 %collective-permute-start.14 = (bf16[16,4096]{1,0:T(8,128)(2,1)S(1)}, bf16[16,4096]{1,0:T(8,128)(2,1)S(1)}, u32[]{:S(2)}, u32[]{:S(2)}) collective-permute-start(bf16[16,4096]{1,0:T(8,128)(2,1)S(1)} %slice.69), channel_id=1, source_target_pairs={{0,448},{16,464},{32,480},{48,496},{64,128},{80,144},{96,160},{112... | collective-permute-start | bytes 393224 | tf_op jit(solution)/shard_map/ppermute | solution.py:141
  127.6 3.2 %collective-permute-done.14 = bf16[16,4096]{1,0:T(8,128)(2,1)S(1)} collective-permute-done((bf16[16,4096]{1,0:T(8,128)(2,1)S(1)}, bf16[16,4096]{1,0:T(8,128)(2,1)S(1)}, u32[]{:S(2)}, u32[]{:S(2)}) %collective-permute-start.14) | collective-permute-done | bytes 131104 | tf_op jit(solution)/shard_map/ppermute | solution.py:141
  134.5 3.7 %all-to-all-start.1 = ((bf16[8,512,128]{2,1,0:T(8,128)(2,1)}), bf16[8,512,128]{2,1,0:T(8,128)(2,1)S(1)}, u32[]{:S(2)}, u32[]{:S(2)}) async-start(bf16[8,512,128]{2,1,0:T(8,128)(2,1)} %bitcast.23), calls=%async_computation.1 | async-start | bytes 2097152 | tf_op jit(solution)/shard_map/all_to_all | solution.py:193
  138.9 15.2 %all-to-all-done.1 = bf16[8,512,128]{2,1,0:T(8,128)(2,1)S(1)} async-done(((bf16[8,512,128]{2,1,0:T(8,128)(2,1)}), bf16[8,512,128]{2,1,0:T(8,128)(2,1)S(1)}, u32[]{:S(2)}, u32[]{:S(2)}) %all-to-all-start.1) | async-done | bytes 1048608 | tf_op jit(solution)/shard_map/all_to_all | solution.py:193
  154.2 10.4 %collective-permute-start.15 = (bf16[512,128]{1,0:T(8,128)(2,1)S(1)}, bf16[512,128]{1,0:T(8,128)(2,1)S(1)}, u32[]{:S(2)}, u32[]{:S(2)}) collective-permute-start(bf16[512,128]{1,0:T(8,128)(2,1)S(1)} %fusion.9), channel_id=1, source_target_pairs={{0,1},{1,0},{2,3},{3,2},{4,5},{5,4},{6,7},{7,6},{8,9},{9,8},{10,11... | collective-permute-start | bytes 393224 | tf_op jit(solution)/shard_map/ppermute | solution.py:197
  165.9 4.8 %collective-permute-done.15 = bf16[512,128]{1,0:T(8,128)(2,1)S(1)} collective-permute-done((bf16[512,128]{1,0:T(8,128)(2,1)S(1)}, bf16[512,128]{1,0:T(8,128)(2,1)S(1)}, u32[]{:S(2)}, u32[]{:S(2)}) %collective-permute-start.15) | collective-permute-done | bytes 131104 | tf_op jit(solution)/shard_map/ppermute | solution.py:197
  (84 shorter events, 30.4 us)
Async XLA Ops:
  7.2 66.9 %copy-start = (bf16[1,1,256,128]{3,2,1,0:T(8,128)(2,1)S(1)}, bf16[1,1,256,128]{3,2,1,0:T(8,128)(2,1)}, u32[]{:S(2)}) copy-start(bf16[1,1,256,128]{3,2,1,0:T(8,128)(2,1)} %param.16) | copy-start | bytes 196612
  7.2 123.6 %all-gather.2.cloned.1.call-start = ((), (), s32[]{:S(2)}) async-start(), calls=%async_computation.2 | async-start | bytes 1179648 | tf_op jit(solution)/shard_map/all_gather | solution.py:158
  9.8 6.3 %copy-start.2 = (bf16[1,2048,4,192]{1,3,2,0:T(8,128)(2,1)S(1)}, bf16[1,2048,4,192]{1,3,2,0:T(8,128)(2,1)}, u32[]{:S(2)}) copy-start(bf16[1,2048,4,192]{1,3,2,0:T(8,128)(2,1)} %param.10) | copy-start | bytes 9437188
  10.8 5.3 %collective-permute-start = (bf16[3072,256]{1,0:T(8,128)(2,1)S(1)}, bf16[3072,256]{1,0:T(8,128)(2,1)S(1)}, u32[]{:S(2)}, u32[]{:S(2)}) collective-permute-start(bf16[3072,256]{1,0:T(8,128)(2,1)S(1)} %pack.1), channel_id=1, source_target_pairs={{0,2},{2,0},{4,6},{6,4},{8,10},{10,8},{12,14},{14,12},{1,3},{3,1},... | collective-permute-start | bytes 4718600 | tf_op jit(solution)/shard_map/ppermute | solution.py:90
  16.1 21.7 %copy-start.4 = (s32[8]{0:T(128)S(1)}, s32[8]{0:T(128)}, u32[]{:S(2)}) copy-start(s32[8]{0:T(128)} %constant.124.clone) | copy-start | bytes 100
  17.8 13.1 %collective-permute-start.1 = (bf16[2,384,256]{2,1,0:T(8,128)(2,1)S(1)}, bf16[2,384,256]{2,1,0:T(8,128)(2,1)S(1)}, u32[]{:S(2)}, u32[]{:S(2)}) collective-permute-start(bf16[2,384,256]{2,1,0:T(8,128)(2,1)S(1)} %get-tuple-element.7), channel_id=1, source_target_pairs={{0,4},{2,6},{4,0},{6,2},{8,12},{10,14},{12,8},{14,10},{1,5},{3,7},... | collective-permute-start | bytes 1179656 | tf_op jit(solution)/shard_map/ppermute | solution.py:112
  21.2 14.4 %collective-permute-start.3 = (bf16[2,384,256]{2,1,0:T(8,128)(2,1)S(1)}, bf16[2,384,256]{2,1,0:T(8,128)(2,1)S(1)}, u32[]{:S(2)}, u32[]{:S(2)}) collective-permute-start(bf16[2,384,256]{2,1,0:T(8,128)(2,1)S(1)} %get-tuple-element.9), channel_id=1, source_target_pairs={{0,12},{2,14},{4,8},{6,10},{8,4},{10,6},{12,0},{14,2},{1,13},{3,15... | collective-permute-start | bytes 1179656 | tf_op jit(solution)/shard_map/ppermute | solution.py:113
  30.9 9.2 %collective-permute-start.2 = (bf16[384,256]{1,0:T(8,128)(2,1)S(1)}, bf16[384,256]{1,0:T(8,128)(2,1)S(1)}, u32[]{:S(2)}, u32[]{:S(2)}) collective-permute-start(bf16[384,256]{1,0:T(8,128)(2,1)S(1)} %fusion.7), channel_id=1, source_target_pairs={{0,12},{2,14},{4,8},{6,10},{8,4},{10,6},{12,0},{14,2},{1,13},{3,15... | collective-permute-start | bytes 589832 | tf_op jit(solution)/shard_map/ppermute | solution.py:114
  35.5 21.9 %copy-start.7 = (s32[128]{0:T(128)S(1)}, s32[128]{0:T(128)}, u32[]{:S(2)}) copy-start(s32[128]{0:T(128)} %param.12) | copy-start | bytes 1540
  35.6 21.9 %copy-start.6 = (s32[1,1,8,128]{3,2,1,0:T(8,128)S(1)}, s32[1,1,8,128]{3,2,1,0:T(8,128)}, u32[]{:S(2)}) copy-start(s32[1,1,8,128]{3,2,1,0:T(8,128)} %param.11) | copy-start | bytes 12292
  35.6 7.7 %collective-permute-start.4 = (bf16[384,256]{1,0:T(8,128)(2,1)S(1)}, bf16[384,256]{1,0:T(8,128)(2,1)S(1)}, u32[]{:S(2)}, u32[]{:S(2)}) collective-permute-start(bf16[384,256]{1,0:T(8,128)(2,1)S(1)} %fusion.8), channel_id=1, source_target_pairs={{0,4},{2,6},{4,0},{6,2},{8,12},{10,14},{12,8},{14,10},{1,5},{3,7},... | collective-permute-start | bytes 589832 | tf_op jit(solution)/shard_map/ppermute | solution.py:115
  44.3 23.9 %all-to-all-start = ((bf16[32,8,768]{2,1,0:T(8,128)(2,1)}), bf16[32,8,768]{2,1,0:T(8,128)(2,1)S(1)}, u32[]{:S(2)}, u32[]{:S(2)}) async-start(bf16[32,8,768]{2,1,0:T(8,128)(2,1)} %bitcast.8), calls=%async_computation | async-start | bytes 786432 | tf_op jit(solution)/shard_map/all_to_all | solution.py:166
  71.6 6.6 %collective-permute-start.5 = (bf16[8,4096]{1,0:T(8,128)(2,1)S(1)}, bf16[8,4096]{1,0:T(8,128)(2,1)S(1)}, u32[]{:S(2)}, u32[]{:S(2)}) collective-permute-start(bf16[8,4096]{1,0:T(8,128)(2,1)S(1)} %get-tuple-element.11), channel_id=1, source_target_pairs={{0,16},{16,0},{32,48},{48,32},{64,80},{80,64},{96,112},{112,96},{1... | collective-permute-start | bytes 196616 | tf_op jit(solution)/shard_map/ppermute | solution.py:132
  78.2 9.2 %collective-permute-start.6 = (bf16[16,4096]{1,0:T(8,128)(2,1)S(1)}, bf16[16,4096]{1,0:T(8,128)(2,1)S(1)}, u32[]{:S(2)}, u32[]{:S(2)}) collective-permute-start(bf16[16,4096]{1,0:T(8,128)(2,1)S(1)} %pad_maximum_fusion.1), channel_id=1, source_target_pairs={{0,32},{16,48},{32,0},{48,16},{64,96},{80,112},{96,64},{112,80},{1... | collective-permute-start | bytes 393224 | tf_op jit(solution)/shard_map/ppermute | solution.py:133
  87.4 8.3 %collective-permute-start.7 = (bf16[32,4096]{1,0:T(8,128)(2,1)S(1)}, bf16[32,4096]{1,0:T(8,128)(2,1)S(1)}, u32[]{:S(2)}, u32[]{:S(2)}) collective-permute-start(bf16[32,4096]{1,0:T(8,128)(2,1)S(1)} %pad_maximum_fusion), channel_id=1, source_target_pairs={{0,64},{16,80},{32,96},{48,112},{64,0},{80,16},{96,32},{112,48},{1... | collective-permute-start | bytes 786440 | tf_op jit(solution)/shard_map/ppermute | solution.py:138
  89.9 10.6 %collective-permute-start.8 = (bf16[32,4096]{1,0:T(8,128)(2,1)S(1)}, bf16[32,4096]{1,0:T(8,128)(2,1)S(1)}, u32[]{:S(2)}, u32[]{:S(2)}) collective-permute-start(bf16[32,4096]{1,0:T(8,128)(2,1)S(1)} %pad_maximum_fusion), channel_id=1, source_target_pairs={{0,448},{16,464},{32,480},{48,496},{64,128},{80,144},{96,160},{112... | collective-permute-start | bytes 786440 | tf_op jit(solution)/shard_map/ppermute | solution.py:138
  95.7 18.6 %collective-permute-start.10 = (bf16[32,4096]{1,0:T(8,128)(2,1)S(1)}, bf16[32,4096]{1,0:T(8,128)(2,1)S(1)}, u32[]{:S(2)}, u32[]{:S(2)}) collective-permute-start(bf16[32,4096]{1,0:T(8,128)(2,1)S(1)} %collective-permute-done.7), channel_id=1, source_target_pairs={{0,448},{16,464},{32,480},{48,496},{64,128},{80,144},{96,160},{112... | collective-permute-start | bytes 786440 | tf_op jit(solution)/shard_map/ppermute | solution.py:138
  100.5 9.3 %collective-permute-start.9 = (bf16[32,4096]{1,0:T(8,128)(2,1)S(1)}, bf16[32,4096]{1,0:T(8,128)(2,1)S(1)}, u32[]{:S(2)}, u32[]{:S(2)}) collective-permute-start(bf16[32,4096]{1,0:T(8,128)(2,1)S(1)} %collective-permute-done.8), channel_id=1, source_target_pairs={{0,64},{16,80},{32,96},{48,112},{64,0},{80,16},{96,32},{112,48},{1... | collective-permute-start | bytes 786440 | tf_op jit(solution)/shard_map/ppermute | solution.py:138
  109.8 10.9 %collective-permute-start.12 = (bf16[32,4096]{1,0:T(8,128)(2,1)S(1)}, bf16[32,4096]{1,0:T(8,128)(2,1)S(1)}, u32[]{:S(2)}, u32[]{:S(2)}) collective-permute-start(bf16[32,4096]{1,0:T(8,128)(2,1)S(1)} %collective-permute-done.9), channel_id=1, source_target_pairs={{0,448},{16,464},{32,480},{48,496},{64,128},{80,144},{96,160},{112... | collective-permute-start | bytes 786440 | tf_op jit(solution)/shard_map/ppermute | solution.py:138
  114.3 8.3 %collective-permute-start.11 = (bf16[32,4096]{1,0:T(8,128)(2,1)S(1)}, bf16[32,4096]{1,0:T(8,128)(2,1)S(1)}, u32[]{:S(2)}, u32[]{:S(2)}) collective-permute-start(bf16[32,4096]{1,0:T(8,128)(2,1)S(1)} %collective-permute-done.10), channel_id=1, source_target_pairs={{0,64},{16,80},{32,96},{48,112},{64,0},{80,16},{96,32},{112,48},{1... | collective-permute-start | bytes 786440 | tf_op jit(solution)/shard_map/ppermute | solution.py:138
  120.7 6.9 %collective-permute-start.13 = (bf16[16,4096]{1,0:T(8,128)(2,1)S(1)}, bf16[16,4096]{1,0:T(8,128)(2,1)S(1)}, u32[]{:S(2)}, u32[]{:S(2)}) collective-permute-start(bf16[16,4096]{1,0:T(8,128)(2,1)S(1)} %slice.68), channel_id=1, source_target_pairs={{0,64},{16,80},{32,96},{48,112},{64,0},{80,16},{96,32},{112,48},{1... | collective-permute-start | bytes 393224 | tf_op jit(solution)/shard_map/ppermute | solution.py:140
  122.6 8.1 %collective-permute-start.14 = (bf16[16,4096]{1,0:T(8,128)(2,1)S(1)}, bf16[16,4096]{1,0:T(8,128)(2,1)S(1)}, u32[]{:S(2)}, u32[]{:S(2)}) collective-permute-start(bf16[16,4096]{1,0:T(8,128)(2,1)S(1)} %slice.69), channel_id=1, source_target_pairs={{0,448},{16,464},{32,480},{48,496},{64,128},{80,144},{96,160},{112... | collective-permute-start | bytes 393224 | tf_op jit(solution)/shard_map/ppermute | solution.py:141
  134.5 19.6 %all-to-all-start.1 = ((bf16[8,512,128]{2,1,0:T(8,128)(2,1)}), bf16[8,512,128]{2,1,0:T(8,128)(2,1)S(1)}, u32[]{:S(2)}, u32[]{:S(2)}) async-start(bf16[8,512,128]{2,1,0:T(8,128)(2,1)} %bitcast.23), calls=%async_computation.1 | async-start | bytes 2097152 | tf_op jit(solution)/shard_map/all_to_all | solution.py:193
  154.2 16.5 %collective-permute-start.15 = (bf16[512,128]{1,0:T(8,128)(2,1)S(1)}, bf16[512,128]{1,0:T(8,128)(2,1)S(1)}, u32[]{:S(2)}, u32[]{:S(2)}) collective-permute-start(bf16[512,128]{1,0:T(8,128)(2,1)S(1)} %fusion.9), channel_id=1, source_target_pairs={{0,1},{1,0},{2,3},{3,2},{4,5},{5,4},{6,7},{7,6},{8,9},{9,8},{10,11... | collective-permute-start | bytes 393224 | tf_op jit(solution)/shard_map/ppermute | solution.py:197
  (4 other events, 8.8 us)
Sparse Core Ops, SparseCore 0:
  25.3 30.8 all-gather.1

commit v3 on v2

--- a/solution.py
+++ b/solution.py
@@ -20,11 +20,21 @@
 X_ODD = swaps(N_X * N_CORE, lambda h: h ^ 6)
 Z_NEAR = swaps(N_Y * N_Z, lambda n: n ^ 1)
 Z_FAR = swaps(N_Y * N_Z, lambda n: n ^ 2)
-Y_EVEN = swaps(N_Y * N_Z, lambda n: n ^ N_Z)
-Y_ODD = swaps(N_Y * N_Z, lambda n: (((n // N_Z + 1) ^ 1) - 1) % N_Y * N_Z + n % N_Z)
+DEVICES = N_Y * N_Z * N_X * N_CORE
+
+
+def y_partner(device, odd):
+    node, h = device // (N_X * N_CORE), device % (N_X * N_CORE)
+    y = ((node // N_Z + odd) ^ 1) - odd
+    return (y % N_Y * N_Z + node % N_Z) * N_X * N_CORE + h
+
+
+Y_FIRST = swaps(DEVICES, lambda i: y_partner(i, i % N_CORE))
+Y_SECOND = swaps(DEVICES, lambda i: y_partner(i, 1 - i % N_CORE))
 DP_SWAP = swaps(2, lambda d: d ^ 1)
 Y_DISTANCE = (0, 1, -1, 2, -2, 3, -3, 4)
 Y_SLOT = (0, 1, 3, 5, 7, 6, 4, 2)
+Z_STEP = (0, 2, 1, 3)
 
 
 def add(*terms):
@@ -34,11 +44,11 @@
     return total
 
 
-def pack_kernel(columns_ref, rows_ref, out_ref):
+def pack_kernel(h_ref, rows_ref, out_ref):
     out_ref[...] = rows_ref[...]
 
 
-def pair_kernel(columns_ref, rows_ref, got_ref, a_keep, a_send, b_keep, b_send):
+def pair_kernel(h_ref, rows_ref, got_ref, a_keep, a_send, b_keep, b_send):
     step = pl.program_id(0)
     total = add(rows_ref[...], got_ref[...]).astype(a_keep.dtype)
     half = total.shape[0] // 2
@@ -51,11 +61,11 @@
     def _():
         a_send[0] = total[:half]
 
-    @pl.when(step % 2 == 0)
+    @pl.when((step == 0) | (step == 3))
     def _():
         b_keep[0] = total[half:]
 
-    @pl.when(step % 2 == 1)
+    @pl.when((step == 1) | (step == 2))
     def _():
         b_send[0] = total[half:]
 
@@ -72,25 +82,24 @@
 def sum_partials(flat):
     rows, samples = flat.shape[0], flat.shape[1] // (N_X * N_CORE)
     half = rows // 2
-    h = lax.axis_index("hst")
-    x, core = h // N_CORE, h % N_CORE
-    column = (x ^ jnp.array([0, 3, 1, 2], jnp.int32)) * N_CORE
+    h = lax.axis_index("hst").astype(jnp.int32).reshape(1)
     params = pltpu.CompilerParams(vmem_limit_bytes=VMEM)
-    block = pl.BlockSpec((rows, samples), lambda j, c: (j, 0))
-    picked = pl.BlockSpec((rows, samples), lambda j, c: (0, c[j]))
+    block = pl.BlockSpec((rows, samples), lambda j, h: (j, 0))
+    theirs = pl.BlockSpec((rows, samples), lambda j, h: (0, h[0] ^ 1 ^ (6 * j % 8)))
+    mine = pl.BlockSpec((rows, samples), lambda j, h: (0, h[0] ^ (6 * j % 8)))
     given = pl.pallas_call(
         pack_kernel,
         out_shape=jax.ShapeDtypeStruct((N_X * rows, samples), flat.dtype),
         grid_spec=pltpu.PrefetchScalarGridSpec(
-            num_scalar_prefetch=1, grid=(N_X,), in_specs=[picked], out_specs=block
+            num_scalar_prefetch=1, grid=(N_X,), in_specs=[theirs], out_specs=block
         ),
         compiler_params=params,
         name="pack",
-    )(column + (1 - core), flat)
+    )(h, flat)
     got = lax.ppermute(given, "hst", CORE_SWAP)
 
     def half_block(index):
-        return pl.BlockSpec((1, half, samples), lambda j, c: (index(j), 0, 0))
+        return pl.BlockSpec((1, half, samples), lambda j, h: (index(j), 0, 0))
 
     a_keep, a_send, b_keep, b_send = pl.pallas_call(
         pair_kernel,
@@ -98,17 +107,17 @@
         grid_spec=pltpu.PrefetchScalarGridSpec(
             num_scalar_prefetch=1,
             grid=(N_X,),
-            in_specs=[picked, block],
+            in_specs=[mine, block],
             out_specs=[
                 half_block(lambda j: jnp.minimum(j, 1)),
+                half_block(lambda j: 1 - j // 3),
                 half_block(lambda j: j // 3),
                 half_block(lambda j: j // 2),
-                half_block(lambda j: j // 3),
             ],
         ),
         compiler_params=params,
         name="pair",
-    )(column + core, flat, got)
+    )(h, flat, got)
     a_one = lax.ppermute(a_send, "hst", X_EVEN)
     b_one = lax.ppermute(b_send, "hst", X_ODD)
     a_two = lax.ppermute(add(a_keep[1], a_one[1]).astype(flat.dtype), "hst", X_ODD)
@@ -129,40 +138,45 @@
 
 
 def gather_nodes(block):
-    near = jnp.concatenate([block, lax.ppermute(block, "node", Z_NEAR)], 0)
-    line = jnp.concatenate([near, lax.ppermute(near, "node", Z_FAR)], 0)
+    far = jnp.concatenate([block, lax.ppermute(block, "node", Z_FAR)], 0)
+    line = jnp.concatenate([far, lax.ppermute(far, "node", Z_NEAR)], 0)
     half = line.shape[0] // 2
-    even, odd = line, line
+
+    def step(rows, pairs):
+        return lax.ppermute(rows, ("node", "hst"), pairs)
+
+    first, second = line, line
     blocks = [line]
     for _ in range(3):
-        even, odd = lax.ppermute(odd, "node", Y_EVEN), lax.ppermute(even, "node", Y_ODD)
-        blocks += [even, odd]
-    blocks.append(lax.ppermute(odd[:half], "node", Y_EVEN))
-    blocks.append(lax.ppermute(even[half:], "node", Y_ODD))
+        first, second = step(second, Y_FIRST), step(first, Y_SECOND)
+        blocks += [first, second]
+    blocks.append(step(second[:half], Y_FIRST))
+    blocks.append(step(first[half:], Y_SECOND))
     return jnp.concatenate(blocks, 0)
 
 
 def node_order():
     n = lax.axis_index("node")
     y, z = n // N_Z, n % N_Z
-    sign = 1 - 2 * (y % 2)
+    sign = (1 - 2 * (y % 2)) * (1 - 2 * (lax.axis_index("hst") % N_CORE))
     step = jnp.arange(N_Y * N_Z)
-    nodes = (y + sign * jnp.array(Y_DISTANCE)[step // N_Z]) % N_Y * N_Z + (z ^ (step % N_Z))
-    slots = jnp.array(Y_SLOT)[(sign * (step // N_Z - y)) % N_Y] * N_Z + (z ^ (step % N_Z))
+    turn = jnp.array(Z_STEP)
+    nodes = (y + sign * jnp.array(Y_DISTANCE)[step // N_Z]) % N_Y * N_Z + (z ^ turn[step % N_Z])
+    slots = jnp.array(Y_SLOT)[sign * (step // N_Z - y) % N_Y] * N_Z + turn[z ^ (step % N_Z)]
     return nodes, slots
 
 
 def local(partials, counts, perm, fm_proj, ln_gain, w_in, d_hidden):
     samples = counts.shape[2]
     group, hidden_here = d_hidden.shape[2], d_hidden.shape[3]
-    w_full = lax.all_gather(w_in, "hst", axis=0, tiled=True)
-
     nodes, slots = node_order()
     d_hid = jnp.take(d_hidden[0, 0].reshape(-1, samples, hidden_here), nodes, axis=0, mode="clip")
     d_hid = d_hid.reshape(group, hidden_here)
 
     rows = partials.shape[2] * partials.shape[3]
     summed = sum_partials(partials[0].transpose(1, 2, 0).reshape(rows, -1))
+    summed, w_in = lax.optimization_barrier((summed, w_in))
+    w_full = lax.all_gather(w_in, "hst", axis=0, tiled=True)
     shard_rows = lax.all_to_all(
         summed.reshape(N_Y * N_Z, samples, rows), "node", split_axis=0, concat_axis=0, tiled=True
     )
@@ -190,12 +204,14 @@
     term = lax.dot_general(
         z_group, d_pre, (((0,), (0,)), ((), ())), preferred_element_type=jnp.float32
     ).astype(jnp.bfloat16)
-    terms = lax.all_to_all(
-        term.reshape(N_X * N_CORE, w_in.shape[0], hidden_here), "hst", 0, 0, tiled=True
-    )
-    share = add(*[terms[i] for i in range(N_X * N_CORE)]).astype(jnp.bfloat16)
-    other = lax.ppermute(share, "dp", DP_SWAP)
-    grad_w = add(share, other)
+    term = term.reshape(N_X * N_CORE, w_in.shape[0], hidden_here)
+    half = w_in.shape[0] // 2
+    shares, others = [], []
+    for rows in (slice(0, half), slice(half, None)):
+        terms = lax.all_to_all(term[:, rows], "hst", 0, 0, tiled=True)
+        shares.append(add(*[terms[i] for i in range(N_X * N_CORE)]).astype(jnp.bfloat16))
+        others.append(lax.ppermute(shares[-1], "dp", DP_SWAP))
+    grad_w = jnp.concatenate([add(*both) for both in zip(shares, others)], 0)
     return (hidden.reshape(1, 1, group, hidden_here), grad_w)
 
 

time: 182 us -> 183 us (level)
  starting transfers between devices: 74.6 us -> 82.9 us
  waiting for transfers between devices: 71.4 us -> 66.5 us
    ppermute x11 -> x12, starting transfers between devices: 41.7 us -> 47.2 us  [the longest x8 25.6 us: step(): return lax.ppermute(rows, ('node', 'hst'), pairs)]
    all_to_all x1 -> x2, waiting for transfers between devices: 15.2 us -> 10.2 us  [local(): terms = lax.all_to_all(term[:, rows], 'hst', 0, 0, tiled=True)]
    all_to_all x1 -> x2, starting transfers between devices: 3.69 us -> 6.98 us  [local(): terms = lax.all_to_all(term[:, rows], 'hst', 0, 0, tiled=True)]
    ppermute x11 -> x12, waiting for transfers between devices: 31.6 us -> 31.6 us  [the longest x8 20.9 us: step(): return lax.ppermute(rows, ('node', 'hst'), pairs)]
  transfers between devices with their start and end apart: 19 -> 21, of which waited for: 14 -> 17; matrix products, arithmetic and copies ran while one was open for 4% -> 2% of each run, Pallas kernels for 1% -> 0%
where the time goes in v3:
time: 183 us; the launch traced here: 180 us
  starting transfers between devices  82.9 us (45%)
  waiting for transfers between devices  66.5 us (36%)
  between operations  14.7 us (8%)
  local copies, waits for them, and re-layouts  8.74 us (5%)
  matrix products  3.31 us (2%)
  Pallas kernels  2.56 us (1%)
    ppermute x8, starting transfers between devices, step(): return lax.ppermute(rows, ('node', 'hst'), pairs)  25.6 us
    ppermute x8, waiting for transfers between devices, step(): return lax.ppermute(rows, ('node', 'hst'), pairs)  20.9 us
    ppermute x2, starting transfers between devices, local(): others.append(lax.ppermute(shares[-1], 'dp', DP_SWAP))  16.4 us
    all_to_all x1, starting transfers between devices, local(): lax.all_to_all(summed.reshape(N_Y * N_Z, samples, rows), 'node', split_ax...  12.5 us
    all_to_all x1, waiting for transfers between devices, local(): lax.all_to_all(summed.reshape(N_Y * N_Z, samples, rows), 'node', split_ax...  10.9 us
    all_to_all x2, waiting for transfers between devices, local(): terms = lax.all_to_all(term[:, rows], 'hst', 0, 0, tiled=True)  10.2 us
    all_to_all x2, starting transfers between devices, local(): terms = lax.all_to_all(term[:, rows], 'hst', 0, 0, tiled=True)  6.98 us
    ppermute x1, waiting for transfers between devices, sum_partials(): a_one = lax.ppermute(a_send, 'hst', X_EVEN)  5.57 us
  transfers between devices with their start and end apart: 21, of which 17 were waited for; matrix products, arithmetic and copies ran while one was open for 2% of the time, Pallas kernels for 0%

profile of v3, /device:TPU:56, one launch (start us, length us, event | category | flops | bytes accessed | tf_op | source)
XLA Modules:
  0.0 180.3 jit_solution(6132259136249355695)
XLA Ops:
  11.5 3.4 %collective-permute-done.got_ref = bf16[3072,256]{1,0:T(8,128)(2,1)S(1)} collective-permute-done((bf16[3072,256]{1,0:T(8,128)(2,1)S(1)}, bf16[3072,256]{1,0:T(8,128)(2,1)S(1)}, u32[]{:S(2)}, u32[]{:S(2)}) %collective-permute-start) | collective-permute-done | bytes 1572896 | tf_op jit(solution)/shard_map/ppermute | solution.py:99
  16.0 3.4 %collective-permute-start.1 = (bf16[2,384,256]{2,1,0:T(8,128)(2,1)S(1)}, bf16[2,384,256]{2,1,0:T(8,128)(2,1)S(1)}, u32[]{:S(2)}, u32[]{:S(2)}) collective-permute-start(bf16[2,384,256]{2,1,0:T(8,128)(2,1)S(1)} %get-tuple-element.9), channel_id=1, source_target_pairs={{0,4},{2,6},{4,0},{6,2},{8,12},{10,14},{12,8},{14,10},{1,5},{3,7},... | collective-permute-start | bytes 1179656 | tf_op jit(solution)/shard_map/ppermute | solution.py:121
  19.4 4.0 %collective-permute-start.3 = (bf16[2,384,256]{2,1,0:T(8,128)(2,1)S(1)}, bf16[2,384,256]{2,1,0:T(8,128)(2,1)S(1)}, u32[]{:S(2)}, u32[]{:S(2)}) collective-permute-start(bf16[2,384,256]{2,1,0:T(8,128)(2,1)S(1)} %get-tuple-element.11), channel_id=1, source_target_pairs={{0,12},{2,14},{4,8},{6,10},{8,4},{10,6},{12,0},{14,2},{1,13},{3,15... | collective-permute-start | bytes 1179656 | tf_op jit(solution)/shard_map/ppermute | solution.py:122
  23.5 5.6 %collective-permute-done.1.a_one = bf16[2,384,256]{2,1,0:T(8,128)(2,1)S(1)} collective-permute-done((bf16[2,384,256]{2,1,0:T(8,128)(2,1)S(1)}, bf16[2,384,256]{2,1,0:T(8,128)(2,1)S(1)}, u32[]{:S(2)}, u32[]{:S(2)}) %collective-permute-start.1) | collective-permute-done | bytes 393248 | tf_op jit(solution)/shard_map/ppermute | solution.py:121
  29.1 4.7 %collective-permute-start.2 = (bf16[384,256]{1,0:T(8,128)(2,1)S(1)}, bf16[384,256]{1,0:T(8,128)(2,1)S(1)}, u32[]{:S(2)}, u32[]{:S(2)}) collective-permute-start(bf16[384,256]{1,0:T(8,128)(2,1)S(1)} %fusion.7), channel_id=1, source_target_pairs={{0,12},{2,14},{4,8},{6,10},{8,4},{10,6},{12,0},{14,2},{1,13},{3,15... | collective-permute-start | bytes 589832 | tf_op jit(solution)/shard_map/ppermute | solution.py:123
  38.3 3.3 %collective-permute-done.4.b_two = bf16[384,256]{1,0:T(8,128)(2,1)S(1)} collective-permute-done((bf16[384,256]{1,0:T(8,128)(2,1)S(1)}, bf16[384,256]{1,0:T(8,128)(2,1)S(1)}, u32[]{:S(2)}, u32[]{:S(2)}) %collective-permute-start.4) | collective-permute-done | bytes 196640 | tf_op jit(solution)/shard_map/ppermute | solution.py:124
  42.6 12.5 %all-to-all-start = ((bf16[32,8,768]{2,1,0:T(8,128)(2,1)}), bf16[32,8,768]{2,1,0:T(8,128)(2,1)S(1)}, u32[]{:S(2)}, u32[]{:S(2)}) async-start(bf16[32,8,768]{2,1,0:T(8,128)(2,1)} %bitcast.9), calls=%async_computation | async-start | bytes 786432 | tf_op jit(solution)/shard_map/all_to_all | solution.py:180
  55.3 10.9 %all-to-all-done = bf16[32,8,768]{2,1,0:T(8,128)(2,1)S(1)} async-done(((bf16[32,8,768]{2,1,0:T(8,128)(2,1)}), bf16[32,8,768]{2,1,0:T(8,128)(2,1)S(1)}, u32[]{:S(2)}, u32[]{:S(2)}) %all-to-all-start) | async-done | bytes 393248 | tf_op jit(solution)/shard_map/all_to_all | solution.py:180
  72.5 4.6 %collective-permute-done.5 = bf16[8,4096]{1,0:T(8,128)(2,1)S(1)} collective-permute-done((bf16[8,4096]{1,0:T(8,128)(2,1)S(1)}, bf16[8,4096]{1,0:T(8,128)(2,1)S(1)}, u32[]{:S(2)}, u32[]{:S(2)}) %collective-permute-start.5) | collective-permute-done | bytes 65568 | tf_op jit(solution)/shard_map/ppermute | solution.py:141
  77.1 2.9 %collective-permute-start.6 = (bf16[16,4096]{1,0:T(8,128)(2,1)S(1)}, bf16[16,4096]{1,0:T(8,128)(2,1)S(1)}, u32[]{:S(2)}, u32[]{:S(2)}) collective-permute-start(bf16[16,4096]{1,0:T(8,128)(2,1)S(1)} %pad_maximum_fusion.2), channel_id=1, source_target_pairs={{0,16},{16,0},{32,48},{48,32},{64,80},{80,64},{96,112},{112,96},{1... | collective-permute-start | bytes 393224 | tf_op jit(solution)/shard_map/ppermute | solution.py:142
  80.0 4.0 %collective-permute-done.6 = bf16[16,4096]{1,0:T(8,128)(2,1)S(1)} collective-permute-done((bf16[16,4096]{1,0:T(8,128)(2,1)S(1)}, bf16[16,4096]{1,0:T(8,128)(2,1)S(1)}, u32[]{:S(2)}, u32[]{:S(2)}) %collective-permute-start.6) | collective-permute-done | bytes 131104 | tf_op jit(solution)/shard_map/ppermute | solution.py:142
  84.0 3.5 %collective-permute-start.7 = (bf16[32,4096]{1,0:T(8,128)(2,1)S(1)}, bf16[32,4096]{1,0:T(8,128)(2,1)S(1)}, u32[]{:S(2)}, u32[]{:S(2)}) collective-permute-start(bf16[32,4096]{1,0:T(8,128)(2,1)S(1)} %pad_maximum_fusion), channel_id=1, source_target_pairs={{0,64},{2,450},{4,68},{6,454},{8,72},{10,458},{12,76},{14,462},{16... | collective-permute-start | bytes 786440 | tf_op jit(solution)/shard_map/ppermute | solution.py:146
  87.4 4.7 %collective-permute-start.8 = (bf16[32,4096]{1,0:T(8,128)(2,1)S(1)}, bf16[32,4096]{1,0:T(8,128)(2,1)S(1)}, u32[]{:S(2)}, u32[]{:S(2)}) collective-permute-start(bf16[32,4096]{1,0:T(8,128)(2,1)S(1)} %pad_maximum_fusion), channel_id=1, source_target_pairs={{0,448},{2,66},{4,452},{6,70},{8,456},{10,74},{12,460},{14,78},{16... | collective-permute-start | bytes 786440 | tf_op jit(solution)/shard_map/ppermute | solution.py:146
  94.8 3.5 %collective-permute-start.10 = (bf16[32,4096]{1,0:T(8,128)(2,1)S(1)}, bf16[32,4096]{1,0:T(8,128)(2,1)S(1)}, u32[]{:S(2)}, u32[]{:S(2)}) collective-permute-start(bf16[32,4096]{1,0:T(8,128)(2,1)S(1)} %collective-permute-done.7), channel_id=1, source_target_pairs={{0,448},{2,66},{4,452},{6,70},{8,456},{10,74},{12,460},{14,78},{16... | collective-permute-start | bytes 786440 | tf_op jit(solution)/shard_map/ppermute | solution.py:146
  100.7 8.9 %collective-permute-done.9 = bf16[32,4096]{1,0:T(8,128)(2,1)S(1)} collective-permute-done((bf16[32,4096]{1,0:T(8,128)(2,1)S(1)}, bf16[32,4096]{1,0:T(8,128)(2,1)S(1)}, u32[]{:S(2)}, u32[]{:S(2)}) %collective-permute-start.9) | collective-permute-done | bytes 262176 | tf_op jit(solution)/shard_map/ppermute | solution.py:146
  109.6 4.8 %collective-permute-start.12 = (bf16[32,4096]{1,0:T(8,128)(2,1)S(1)}, bf16[32,4096]{1,0:T(8,128)(2,1)S(1)}, u32[]{:S(2)}, u32[]{:S(2)}) collective-permute-start(bf16[32,4096]{1,0:T(8,128)(2,1)S(1)} %collective-permute-done.9), channel_id=1, source_target_pairs={{0,448},{2,66},{4,452},{6,70},{8,456},{10,74},{12,460},{14,78},{16... | collective-permute-start | bytes 786440 | tf_op jit(solution)/shard_map/ppermute | solution.py:146
  116.4 3.2 %collective-permute-done.12 = bf16[32,4096]{1,0:T(8,128)(2,1)S(1)} collective-permute-done((bf16[32,4096]{1,0:T(8,128)(2,1)S(1)}, bf16[32,4096]{1,0:T(8,128)(2,1)S(1)}, u32[]{:S(2)}, u32[]{:S(2)}) %collective-permute-start.12) | collective-permute-done | bytes 262176 | tf_op jit(solution)/shard_map/ppermute | solution.py:146
  122.7 3.1 %collective-permute-start.14 = (bf16[16,4096]{1,0:T(8,128)(2,1)S(1)}, bf16[16,4096]{1,0:T(8,128)(2,1)S(1)}, u32[]{:S(2)}, u32[]{:S(2)}) collective-permute-start(bf16[16,4096]{1,0:T(8,128)(2,1)S(1)} %slice.119), channel_id=1, source_target_pairs={{0,448},{2,66},{4,452},{6,70},{8,456},{10,74},{12,460},{14,78},{16... | collective-permute-start | bytes 393224 | tf_op jit(solution)/shard_map/ppermute | solution.py:146
  126.5 4.3 %collective-permute-done.14 = bf16[16,4096]{1,0:T(8,128)(2,1)S(1)} collective-permute-done((bf16[16,4096]{1,0:T(8,128)(2,1)S(1)}, bf16[16,4096]{1,0:T(8,128)(2,1)S(1)}, u32[]{:S(2)}, u32[]{:S(2)}) %collective-permute-start.14) | collective-permute-done | bytes 131104 | tf_op jit(solution)/shard_map/ppermute | solution.py:146
  134.6 3.5 %all-to-all-start.2 = ((bf16[8,256,128]{2,1,0:T(8,128)(2,1)}), bf16[8,256,128]{2,1,0:T(8,128)(2,1)S(1)}, u32[]{:S(2)}, u32[]{:S(2)}) async-start(bf16[8,256,128]{2,1,0:T(8,128)(2,1)} %get-tuple-element.17), calls=%async_computation.2 | async-start | bytes 1048576 | tf_op jit(solution)/shard_map/all_to_all | solution.py:211
  138.8 9.5 %all-to-all-done.2 = bf16[8,256,128]{2,1,0:T(8,128)(2,1)S(1)} async-done(((bf16[8,256,128]{2,1,0:T(8,128)(2,1)}), bf16[8,256,128]{2,1,0:T(8,128)(2,1)S(1)}, u32[]{:S(2)}, u32[]{:S(2)}) %all-to-all-start.2) | async-done | bytes 524320 | tf_op jit(solution)/shard_map/all_to_all | solution.py:211
  148.3 3.5 %all-to-all-start.1 = ((bf16[8,256,128]{2,1,0:T(8,128)(2,1)}), bf16[8,256,128]{2,1,0:T(8,128)(2,1)S(1)}, u32[]{:S(2)}, u32[]{:S(2)}) async-start(bf16[8,256,128]{2,1,0:T(8,128)(2,1)} %get-tuple-element.16), calls=%async_computation.1 | async-start | bytes 1048576 | tf_op jit(solution)/shard_map/all_to_all | solution.py:211
  153.2 8.2 %collective-permute-start.16 = (bf16[256,128]{1,0:T(8,128)(2,1)S(1)}, bf16[256,128]{1,0:T(8,128)(2,1)S(1)}, u32[]{:S(2)}, u32[]{:S(2)}) collective-permute-start(bf16[256,128]{1,0:T(8,128)(2,1)S(1)} %fusion.13), channel_id=1, source_target_pairs={{0,1},{1,0},{2,3},{3,2},{4,5},{5,4},{6,7},{7,6},{8,9},{9,8},{10,11... | collective-permute-start | bytes 196616 | tf_op jit(solution)/shard_map/ppermute | solution.py:213
  162.2 8.2 %collective-permute-start.15 = (bf16[256,128]{1,0:T(8,128)(2,1)S(1)}, bf16[256,128]{1,0:T(8,128)(2,1)S(1)}, u32[]{:S(2)}, u32[]{:S(2)}) collective-permute-start(bf16[256,128]{1,0:T(8,128)(2,1)S(1)} %fusion.12), channel_id=1, source_target_pairs={{0,1},{1,0},{2,3},{3,2},{4,5},{5,4},{6,7},{7,6},{8,9},{9,8},{10,11... | collective-permute-start | bytes 196616 | tf_op jit(solution)/shard_map/ppermute | solution.py:213
  (89 shorter events, 37.5 us)
Async XLA Ops:
  7.2 64.7 %copy-start = (bf16[1,1,256,128]{3,2,1,0:T(8,128)(2,1)S(1)}, bf16[1,1,256,128]{3,2,1,0:T(8,128)(2,1)}, u32[]{:S(2)}) copy-start(bf16[1,1,256,128]{3,2,1,0:T(8,128)(2,1)} %param.16) | copy-start | bytes 196612
  9.6 26.5 %copy-start.3 = (s32[8]{0:T(128)S(1)}, s32[8]{0:T(128)}, u32[]{:S(2)}) copy-start(s32[8]{0:T(128)} %constant.116.clone) | copy-start | bytes 100
  9.6 5.3 %collective-permute-start = (bf16[3072,256]{1,0:T(8,128)(2,1)S(1)}, bf16[3072,256]{1,0:T(8,128)(2,1)S(1)}, u32[]{:S(2)}, u32[]{:S(2)}) collective-permute-start(bf16[3072,256]{1,0:T(8,128)(2,1)S(1)} %pack.1), channel_id=1, source_target_pairs={{0,2},{2,0},{4,6},{6,4},{8,10},{10,8},{12,14},{14,12},{1,3},{3,1},... | collective-permute-start | bytes 4718600 | tf_op jit(solution)/shard_map/ppermute | solution.py:99
  16.0 13.1 %collective-permute-start.1 = (bf16[2,384,256]{2,1,0:T(8,128)(2,1)S(1)}, bf16[2,384,256]{2,1,0:T(8,128)(2,1)S(1)}, u32[]{:S(2)}, u32[]{:S(2)}) collective-permute-start(bf16[2,384,256]{2,1,0:T(8,128)(2,1)S(1)} %get-tuple-element.9), channel_id=1, source_target_pairs={{0,4},{2,6},{4,0},{6,2},{8,12},{10,14},{12,8},{14,10},{1,5},{3,7},... | collective-permute-start | bytes 1179656 | tf_op jit(solution)/shard_map/ppermute | solution.py:121
  19.4 14.4 %collective-permute-start.3 = (bf16[2,384,256]{2,1,0:T(8,128)(2,1)S(1)}, bf16[2,384,256]{2,1,0:T(8,128)(2,1)S(1)}, u32[]{:S(2)}, u32[]{:S(2)}) collective-permute-start(bf16[2,384,256]{2,1,0:T(8,128)(2,1)S(1)} %get-tuple-element.11), channel_id=1, source_target_pairs={{0,12},{2,14},{4,8},{6,10},{8,4},{10,6},{12,0},{14,2},{1,13},{3,15... | collective-permute-start | bytes 1179656 | tf_op jit(solution)/shard_map/ppermute | solution.py:122
  29.1 9.2 %collective-permute-start.2 = (bf16[384,256]{1,0:T(8,128)(2,1)S(1)}, bf16[384,256]{1,0:T(8,128)(2,1)S(1)}, u32[]{:S(2)}, u32[]{:S(2)}) collective-permute-start(bf16[384,256]{1,0:T(8,128)(2,1)S(1)} %fusion.7), channel_id=1, source_target_pairs={{0,12},{2,14},{4,8},{6,10},{8,4},{10,6},{12,0},{14,2},{1,13},{3,15... | collective-permute-start | bytes 589832 | tf_op jit(solution)/shard_map/ppermute | solution.py:123
  33.8 21.4 %copy-start.5 = (s32[1,1,8,128]{3,2,1,0:T(8,128)S(1)}, s32[1,1,8,128]{3,2,1,0:T(8,128)}, u32[]{:S(2)}) copy-start(s32[1,1,8,128]{3,2,1,0:T(8,128)} %param.11) | copy-start | bytes 12292
  33.9 7.7 %collective-permute-start.4 = (bf16[384,256]{1,0:T(8,128)(2,1)S(1)}, bf16[384,256]{1,0:T(8,128)(2,1)S(1)}, u32[]{:S(2)}, u32[]{:S(2)}) collective-permute-start(bf16[384,256]{1,0:T(8,128)(2,1)S(1)} %fusion.8), channel_id=1, source_target_pairs={{0,4},{2,6},{4,0},{6,2},{8,12},{10,14},{12,8},{14,10},{1,5},{3,7},... | collective-permute-start | bytes 589832 | tf_op jit(solution)/shard_map/ppermute | solution.py:124
  42.6 23.5 %all-to-all-start = ((bf16[32,8,768]{2,1,0:T(8,128)(2,1)}), bf16[32,8,768]{2,1,0:T(8,128)(2,1)S(1)}, u32[]{:S(2)}, u32[]{:S(2)}) async-start(bf16[32,8,768]{2,1,0:T(8,128)(2,1)} %bitcast.9), calls=%async_computation | async-start | bytes 786432 | tf_op jit(solution)/shard_map/all_to_all | solution.py:180
  55.1 75.7 %all-gather.2.cloned.1.call-start = ((), (), s32[]{:S(2)}) async-start(), calls=%async_computation.3 | async-start | bytes 1179648 | tf_op jit(solution)/shard_map/all_gather | solution.py:179
  69.5 7.6 %collective-permute-start.5 = (bf16[8,4096]{1,0:T(8,128)(2,1)S(1)}, bf16[8,4096]{1,0:T(8,128)(2,1)S(1)}, u32[]{:S(2)}, u32[]{:S(2)}) collective-permute-start(bf16[8,4096]{1,0:T(8,128)(2,1)S(1)} %get-tuple-element.15), channel_id=1, source_target_pairs={{0,32},{16,48},{32,0},{48,16},{64,96},{80,112},{96,64},{112,80},{1... | collective-permute-start | bytes 196616 | tf_op jit(solution)/shard_map/ppermute | solution.py:141
  77.1 6.9 %collective-permute-start.6 = (bf16[16,4096]{1,0:T(8,128)(2,1)S(1)}, bf16[16,4096]{1,0:T(8,128)(2,1)S(1)}, u32[]{:S(2)}, u32[]{:S(2)}) collective-permute-start(bf16[16,4096]{1,0:T(8,128)(2,1)S(1)} %pad_maximum_fusion.2), channel_id=1, source_target_pairs={{0,16},{16,0},{32,48},{48,32},{64,80},{80,64},{96,112},{112,96},{1... | collective-permute-start | bytes 393224 | tf_op jit(solution)/shard_map/ppermute | solution.py:142
  84.0 10.9 %collective-permute-start.7 = (bf16[32,4096]{1,0:T(8,128)(2,1)S(1)}, bf16[32,4096]{1,0:T(8,128)(2,1)S(1)}, u32[]{:S(2)}, u32[]{:S(2)}) collective-permute-start(bf16[32,4096]{1,0:T(8,128)(2,1)S(1)} %pad_maximum_fusion), channel_id=1, source_target_pairs={{0,64},{2,450},{4,68},{6,454},{8,72},{10,458},{12,76},{14,462},{16... | collective-permute-start | bytes 786440 | tf_op jit(solution)/shard_map/ppermute | solution.py:146
  87.4 11.1 %collective-permute-start.8 = (bf16[32,4096]{1,0:T(8,128)(2,1)S(1)}, bf16[32,4096]{1,0:T(8,128)(2,1)S(1)}, u32[]{:S(2)}, u32[]{:S(2)}) collective-permute-start(bf16[32,4096]{1,0:T(8,128)(2,1)S(1)} %pad_maximum_fusion), channel_id=1, source_target_pairs={{0,448},{2,66},{4,452},{6,70},{8,456},{10,74},{12,460},{14,78},{16... | collective-permute-start | bytes 786440 | tf_op jit(solution)/shard_map/ppermute | solution.py:146
  94.8 19.6 %collective-permute-start.10 = (bf16[32,4096]{1,0:T(8,128)(2,1)S(1)}, bf16[32,4096]{1,0:T(8,128)(2,1)S(1)}, u32[]{:S(2)}, u32[]{:S(2)}) collective-permute-start(bf16[32,4096]{1,0:T(8,128)(2,1)S(1)} %collective-permute-done.7), channel_id=1, source_target_pairs={{0,448},{2,66},{4,452},{6,70},{8,456},{10,74},{12,460},{14,78},{16... | collective-permute-start | bytes 786440 | tf_op jit(solution)/shard_map/ppermute | solution.py:146
  98.5 11.0 %collective-permute-start.9 = (bf16[32,4096]{1,0:T(8,128)(2,1)S(1)}, bf16[32,4096]{1,0:T(8,128)(2,1)S(1)}, u32[]{:S(2)}, u32[]{:S(2)}) collective-permute-start(bf16[32,4096]{1,0:T(8,128)(2,1)S(1)} %collective-permute-done.8), channel_id=1, source_target_pairs={{0,64},{2,450},{4,68},{6,454},{8,72},{10,458},{12,76},{14,462},{16... | collective-permute-start | bytes 786440 | tf_op jit(solution)/shard_map/ppermute | solution.py:146
  109.6 10.0 %collective-permute-start.12 = (bf16[32,4096]{1,0:T(8,128)(2,1)S(1)}, bf16[32,4096]{1,0:T(8,128)(2,1)S(1)}, u32[]{:S(2)}, u32[]{:S(2)}) collective-permute-start(bf16[32,4096]{1,0:T(8,128)(2,1)S(1)} %collective-permute-done.9), channel_id=1, source_target_pairs={{0,448},{2,66},{4,452},{6,70},{8,456},{10,74},{12,460},{14,78},{16... | collective-permute-start | bytes 786440 | tf_op jit(solution)/shard_map/ppermute | solution.py:146
  114.4 8.3 %collective-permute-start.11 = (bf16[32,4096]{1,0:T(8,128)(2,1)S(1)}, bf16[32,4096]{1,0:T(8,128)(2,1)S(1)}, u32[]{:S(2)}, u32[]{:S(2)}) collective-permute-start(bf16[32,4096]{1,0:T(8,128)(2,1)S(1)} %collective-permute-done.10), channel_id=1, source_target_pairs={{0,64},{2,450},{4,68},{6,454},{8,72},{10,458},{12,76},{14,462},{16... | collective-permute-start | bytes 786440 | tf_op jit(solution)/shard_map/ppermute | solution.py:146
  119.6 6.9 %collective-permute-start.13 = (bf16[16,4096]{1,0:T(8,128)(2,1)S(1)}, bf16[16,4096]{1,0:T(8,128)(2,1)S(1)}, u32[]{:S(2)}, u32[]{:S(2)}) collective-permute-start(bf16[16,4096]{1,0:T(8,128)(2,1)S(1)} %slice.118), channel_id=1, source_target_pairs={{0,64},{2,450},{4,68},{6,454},{8,72},{10,458},{12,76},{14,462},{16... | collective-permute-start | bytes 393224 | tf_op jit(solution)/shard_map/ppermute | solution.py:146
  122.7 8.1 %collective-permute-start.14 = (bf16[16,4096]{1,0:T(8,128)(2,1)S(1)}, bf16[16,4096]{1,0:T(8,128)(2,1)S(1)}, u32[]{:S(2)}, u32[]{:S(2)}) collective-permute-start(bf16[16,4096]{1,0:T(8,128)(2,1)S(1)} %slice.119), channel_id=1, source_target_pairs={{0,448},{2,66},{4,452},{6,70},{8,456},{10,74},{12,460},{14,78},{16... | collective-permute-start | bytes 393224 | tf_op jit(solution)/shard_map/ppermute | solution.py:146
  134.6 13.8 %all-to-all-start.2 = ((bf16[8,256,128]{2,1,0:T(8,128)(2,1)}), bf16[8,256,128]{2,1,0:T(8,128)(2,1)S(1)}, u32[]{:S(2)}, u32[]{:S(2)}) async-start(bf16[8,256,128]{2,1,0:T(8,128)(2,1)} %get-tuple-element.17), calls=%async_computation.2 | async-start | bytes 1048576 | tf_op jit(solution)/shard_map/all_to_all | solution.py:211
  148.3 13.8 %all-to-all-start.1 = ((bf16[8,256,128]{2,1,0:T(8,128)(2,1)}), bf16[8,256,128]{2,1,0:T(8,128)(2,1)S(1)}, u32[]{:S(2)}, u32[]{:S(2)}) async-start(bf16[8,256,128]{2,1,0:T(8,128)(2,1)} %get-tuple-element.16), calls=%async_computation.1 | async-start | bytes 1048576 | tf_op jit(solution)/shard_map/all_to_all | solution.py:211
  153.2 17.2 %collective-permute-start.16 = (bf16[256,128]{1,0:T(8,128)(2,1)S(1)}, bf16[256,128]{1,0:T(8,128)(2,1)S(1)}, u32[]{:S(2)}, u32[]{:S(2)}) collective-permute-start(bf16[256,128]{1,0:T(8,128)(2,1)S(1)} %fusion.13), channel_id=1, source_target_pairs={{0,1},{1,0},{2,3},{3,2},{4,5},{5,4},{6,7},{7,6},{8,9},{9,8},{10,11... | collective-permute-start | bytes 196616 | tf_op jit(solution)/shard_map/ppermute | solution.py:213
  162.2 10.5 %collective-permute-start.15 = (bf16[256,128]{1,0:T(8,128)(2,1)S(1)}, bf16[256,128]{1,0:T(8,128)(2,1)S(1)}, u32[]{:S(2)}, u32[]{:S(2)}) collective-permute-start(bf16[256,128]{1,0:T(8,128)(2,1)S(1)} %fusion.12), channel_id=1, source_target_pairs={{0,1},{1,0},{2,3},{3,2},{4,5},{5,4},{6,7},{7,6},{8,9},{9,8},{10,11... | collective-permute-start | bytes 196616 | tf_op jit(solution)/shard_map/ppermute | solution.py:213
  (5 other events, 31.1 us)
Sparse Core Ops, SparseCore 0:
  72.6 28.1 all-gather.1

commit v4 on v3

--- a/solution.py
+++ b/solution.py
@@ -18,23 +18,11 @@
 CORE_SWAP = swaps(N_X * N_CORE, lambda h: h ^ 1)
 X_EVEN = swaps(N_X * N_CORE, lambda h: h ^ 2)
 X_ODD = swaps(N_X * N_CORE, lambda h: h ^ 6)
-Z_NEAR = swaps(N_Y * N_Z, lambda n: n ^ 1)
-Z_FAR = swaps(N_Y * N_Z, lambda n: n ^ 2)
-DEVICES = N_Y * N_Z * N_X * N_CORE
-
-
-def y_partner(device, odd):
-    node, h = device // (N_X * N_CORE), device % (N_X * N_CORE)
-    y = ((node // N_Z + odd) ^ 1) - odd
-    return (y % N_Y * N_Z + node % N_Z) * N_X * N_CORE + h
-
-
-Y_FIRST = swaps(DEVICES, lambda i: y_partner(i, i % N_CORE))
-Y_SECOND = swaps(DEVICES, lambda i: y_partner(i, 1 - i % N_CORE))
+Y_EVEN = swaps(N_Y * N_Z, lambda n: n ^ N_Z)
+Y_ODD = swaps(N_Y * N_Z, lambda n: (((n // N_Z + 1) ^ 1) - 1) % N_Y * N_Z + n % N_Z)
+Y_GROUPS = [[N_Z * y + z for y in range(N_Y)] for z in range(N_Z)]
+Z_GROUPS = [[N_Z * y + z for z in range(N_Z)] for y in range(N_Y)]
 DP_SWAP = swaps(2, lambda d: d ^ 1)
-Y_DISTANCE = (0, 1, -1, 2, -2, 3, -3, 4)
-Y_SLOT = (0, 1, 3, 5, 7, 6, 4, 2)
-Z_STEP = (0, 2, 1, 3)
 
 
 def add(*terms):
@@ -93,7 +81,7 @@
         grid_spec=pltpu.PrefetchScalarGridSpec(
             num_scalar_prefetch=1, grid=(N_X,), in_specs=[theirs], out_specs=block
         ),
-        compiler_params=params,
+        compiler_params=pltpu.CompilerParams(vmem_limit_bytes=4 * VMEM),
         name="pack",
     )(h, flat)
     got = lax.ppermute(given, "hst", CORE_SWAP)
@@ -138,45 +126,37 @@
 
 
 def gather_nodes(block):
-    far = jnp.concatenate([block, lax.ppermute(block, "node", Z_FAR)], 0)
-    line = jnp.concatenate([far, lax.ppermute(far, "node", Z_NEAR)], 0)
-    half = line.shape[0] // 2
-
-    def step(rows, pairs):
-        return lax.ppermute(rows, ("node", "hst"), pairs)
-
-    first, second = line, line
-    blocks = [line]
-    for _ in range(3):
-        first, second = step(second, Y_FIRST), step(first, Y_SECOND)
-        blocks += [first, second]
-    blocks.append(step(second[:half], Y_FIRST))
-    blocks.append(step(first[half:], Y_SECOND))
-    return jnp.concatenate(blocks, 0)
-
-
-def node_order():
-    n = lax.axis_index("node")
-    y, z = n // N_Z, n % N_Z
-    sign = (1 - 2 * (y % 2)) * (1 - 2 * (lax.axis_index("hst") % N_CORE))
-    step = jnp.arange(N_Y * N_Z)
-    turn = jnp.array(Z_STEP)
-    nodes = (y + sign * jnp.array(Y_DISTANCE)[step // N_Z]) % N_Y * N_Z + (z ^ turn[step % N_Z])
-    slots = jnp.array(Y_SLOT)[sign * (step // N_Z - y) % N_Y] * N_Z + turn[z ^ (step % N_Z)]
-    return nodes, slots
+    copies = jnp.broadcast_to(block, (N_Z,) + block.shape)
+    line = lax.all_to_all(copies, "node", 0, 0, axis_index_groups=Z_GROUPS, tiled=True)
+    line = line.reshape(-1, block.shape[1])
+    rows, width = line.shape[0], line.shape[1] // 2
+    right = lax.all_gather(
+        line[:, width:], "node", axis_index_groups=Y_GROUPS, axis=0, tiled=True
+    )
+    y = lax.axis_index("node") // N_Z
+    sign = 1 - 2 * (y % 2)
+
+    def put(left, part, distance, first_row=0):
+        place = (y + sign * distance) % N_Y * rows + first_row
+        return lax.dynamic_update_slice(left, part, (place, 0))
+
+    even = odd = line[:, :width]
+    left = put(jnp.zeros((N_Y * rows, width), line.dtype), even, 0)
+    for distance in range(1, N_Y // 2):
+        even, odd = lax.ppermute(odd, "node", Y_EVEN), lax.ppermute(even, "node", Y_ODD)
+        left = put(put(left, even, distance), odd, -distance)
+    half = rows // 2
+    even = lax.ppermute(odd[:half], "node", Y_EVEN), lax.ppermute(even[half:], "node", Y_ODD)
+    left = put(put(left, even[0], N_Y // 2), even[1], N_Y // 2, half)
+    return left, right
 
 
 def local(partials, counts, perm, fm_proj, ln_gain, w_in, d_hidden):
     samples = counts.shape[2]
     group, hidden_here = d_hidden.shape[2], d_hidden.shape[3]
-    nodes, slots = node_order()
-    d_hid = jnp.take(d_hidden[0, 0].reshape(-1, samples, hidden_here), nodes, axis=0, mode="clip")
-    d_hid = d_hid.reshape(group, hidden_here)
-
+    w_full = lax.all_gather(w_in, "hst", axis=0, tiled=True)
     rows = partials.shape[2] * partials.shape[3]
     summed = sum_partials(partials[0].transpose(1, 2, 0).reshape(rows, -1))
-    summed, w_in = lax.optimization_barrier((summed, w_in))
-    w_full = lax.all_gather(w_in, "hst", axis=0, tiled=True)
     shard_rows = lax.all_to_all(
         summed.reshape(N_Y * N_Z, samples, rows), "node", split_axis=0, concat_axis=0, tiled=True
     )
@@ -193,25 +173,25 @@
     pairwise = jnp.einsum("sfe,sek->sfk", pooled, projected, preferred_element_type=jnp.float32)
     z_local = normalize(pairwise.reshape(samples, -1), ln_gain)
 
-    z_group = gather_nodes(z_local)
-    pre_act = jnp.dot(z_group, w_full, preferred_element_type=jnp.float32)
+    left, right = gather_nodes(z_local)
+    width = left.shape[1]
+    pre_act = jnp.dot(left, w_full[:width], preferred_element_type=jnp.float32)
+    pre_act = pre_act + jnp.dot(right, w_full[width:], preferred_element_type=jnp.float32)
     sigma = jax.nn.sigmoid(pre_act)
-    hidden = (pre_act * sigma).astype(jnp.bfloat16).reshape(-1, samples, hidden_here)
-    hidden = jnp.take(hidden, slots, axis=0, mode="clip")
-    d_pre = (d_hid.astype(jnp.float32) * sigma * (1.0 + pre_act * (1.0 - sigma))).astype(
+    hidden = (pre_act * sigma).astype(jnp.bfloat16)
+    d_pre = (d_hidden[0, 0].astype(jnp.float32) * sigma * (1.0 + pre_act * (1.0 - sigma))).astype(
         jnp.bfloat16
     )
-    term = lax.dot_general(
-        z_group, d_pre, (((0,), (0,)), ((), ())), preferred_element_type=jnp.float32
-    ).astype(jnp.bfloat16)
-    term = term.reshape(N_X * N_CORE, w_in.shape[0], hidden_here)
-    half = w_in.shape[0] // 2
-    shares, others = [], []
-    for rows in (slice(0, half), slice(half, None)):
-        terms = lax.all_to_all(term[:, rows], "hst", 0, 0, tiled=True)
-        shares.append(add(*[terms[i] for i in range(N_X * N_CORE)]).astype(jnp.bfloat16))
-        others.append(lax.ppermute(shares[-1], "dp", DP_SWAP))
-    grad_w = jnp.concatenate([add(*both) for both in zip(shares, others)], 0)
+    term = [
+        lax.dot_general(
+            part, d_pre, (((0,), (0,)), ((), ())), preferred_element_type=jnp.float32
+        ).astype(jnp.bfloat16)
+        for part in (left, right)
+    ]
+    term = jnp.concatenate(term, 0).reshape(N_X * N_CORE, w_in.shape[0], hidden_here)
+    terms = lax.all_to_all(term, "hst", 0, 0, tiled=True)
+    share = add(*[terms[i] for i in range(N_X * N_CORE)]).astype(jnp.bfloat16)
+    grad_w = add(share, lax.ppermute(share, "dp", DP_SWAP))
     return (hidden.reshape(1, 1, group, hidden_here), grad_w)
 
 

time: 183 us -> 178 us (0.973)
  blocking collectives: 0 us -> 19.9 us
  starting transfers between devices: 82.9 us -> 63.4 us
  waiting for transfers between devices: 66.5 us -> 61.5 us
  local copies, waits for them, and re-layouts: 8.74 us -> 5.92 us
    all_to_all x0 -> x1, blocking collectives: none -> 19.9 us  [local(): terms = lax.all_to_all(term, 'hst', 0, 0, tiled=True)]
    ppermute x12 -> x9, starting transfers between devices: 47.2 us -> 33 us  [the longest x3 12.6 us: gather_nodes(): lax.ppermute(even, 'node', Y_ODD)]
    ppermute x12 -> x9, waiting for transfers between devices: 31.6 us -> 21.3 us  [the longest x3 11.9 us: gather_nodes(): lax.ppermute(even, 'node', Y_ODD)]
    ppermute x1, waiting for transfers between devices: 0.01 us -> 7.45 us  [sum_partials(): b_one = lax.ppermute(b_send, 'hst', X_ODD)]
    all_gather x0 -> x1, waiting for transfers between devices: none -> 5.36 us  [gather_nodes(): lax.all_gather(line[:, width:], 'node', axis_index_groups=Y_GROUPS, axis=...]
    ppermute x1, waiting for transfers between devices: 5.57 us -> 0.92 us  [sum_partials(): a_one = lax.ppermute(a_send, 'hst', X_EVEN)]
    all_to_all x2 -> x1, starting transfers between devices: 6.98 us -> 3.41 us  [gather_nodes(): lax.all_to_all(copies, 'node', 0, 0, axis_index_groups=Z_GROUPS, tiled=True)]
    all_to_all x2 -> x1, waiting for transfers between devices: 10.2 us -> 6.65 us  [gather_nodes(): lax.all_to_all(copies, 'node', 0, 0, axis_index_groups=Z_GROUPS, tiled=True)]
  transfers between devices with their start and end apart: 21 -> 18, of which waited for: 17 -> 15; matrix products, arithmetic and copies ran while one was open for 2% -> 3% of each run, Pallas kernels for 0% -> 0%
where the time goes in v4:
time: 178 us; the launch traced here: 175 us
  starting transfers between devices  63.4 us (36%)
  waiting for transfers between devices  61.5 us (35%)
  blocking collectives  19.9 us (11%)
  between operations  14.7 us (8%)
  local copies, waits for them, and re-layouts  5.92 us (3%)
  matrix products  4.99 us (3%)
  Pallas kernels  2.55 us (1%)
  other arithmetic  2.2 us (1%)
    all_to_all x1, blocking collectives, local(): terms = lax.all_to_all(term, 'hst', 0, 0, tiled=True)  19.9 us
    ppermute x3, starting transfers between devices, gather_nodes(): lax.ppermute(even, 'node', Y_ODD)  12.6 us
    all_to_all x1, starting transfers between devices, local(): lax.all_to_all(summed.reshape(N_Y * N_Z, samples, rows), 'node', split_ax...  12.5 us
    ppermute x3, waiting for transfers between devices, gather_nodes(): lax.ppermute(even, 'node', Y_ODD)  11.9 us
    all_to_all x1, waiting for transfers between devices, local(): lax.all_to_all(summed.reshape(N_Y * N_Z, samples, rows), 'node', split_ax...  10.3 us
    ppermute x1, starting transfers between devices, local(): grad_w = add(share, lax.ppermute(share, 'dp', DP_SWAP))  7.85 us
    ppermute x1, waiting for transfers between devices, sum_partials(): b_one = lax.ppermute(b_send, 'hst', X_ODD)  7.45 us
    ppermute x3, starting transfers between devices, gather_nodes(): lax.ppermute(odd, 'node', Y_EVEN)  6.96 us
  transfers between devices with their start and end apart: 18, of which 15 were waited for; matrix products, arithmetic and copies ran while one was open for 3% of the time, Pallas kernels for 0%

profile of v4, /device:TPU:56, one launch (start us, length us, event | category | flops | bytes accessed | tf_op | source)
XLA Modules:
  0.0 175.2 jit_solution(751436135749807237)
XLA Ops:
  9.5 1.9 %collective-permute-start = (bf16[3072,256]{1,0:T(8,128)(2,1)S(1)}, bf16[3072,256]{1,0:T(8,128)(2,1)S(1)}, u32[]{:S(2)}, u32[]{:S(2)}) collective-permute-start(bf16[3072,256]{1,0:T(8,128)(2,1)S(1)} %pack.1), channel_id=1, source_target_pairs={{0,2},{2,0},{4,6},{6,4},{8,10},{10,8},{12,14},{14,12},{1,3},{3,1},... | collective-permute-start | bytes 4718600 | tf_op jit(solution)/shard_map/ppermute | solution.py:87
  11.5 3.4 %collective-permute-done.got_ref = bf16[3072,256]{1,0:T(8,128)(2,1)S(1)} collective-permute-done((bf16[3072,256]{1,0:T(8,128)(2,1)S(1)}, bf16[3072,256]{1,0:T(8,128)(2,1)S(1)}, u32[]{:S(2)}, u32[]{:S(2)}) %collective-permute-start) | collective-permute-done | bytes 1572896 | tf_op jit(solution)/shard_map/ppermute | solution.py:87
  16.0 4.7 %collective-permute-start.3 = (bf16[2,384,256]{2,1,0:T(8,128)(2,1)S(1)}, bf16[2,384,256]{2,1,0:T(8,128)(2,1)S(1)}, u32[]{:S(2)}, u32[]{:S(2)}) collective-permute-start(bf16[2,384,256]{2,1,0:T(8,128)(2,1)S(1)} %get-tuple-element.9), channel_id=1, source_target_pairs={{0,12},{2,14},{4,8},{6,10},{8,4},{10,6},{12,0},{14,2},{1,13},{3,15... | collective-permute-start | bytes 1179656 | tf_op jit(solution)/shard_map/ppermute | solution.py:110
  20.6 2.1 %collective-permute-start.1 = (bf16[2,384,256]{2,1,0:T(8,128)(2,1)S(1)}, bf16[2,384,256]{2,1,0:T(8,128)(2,1)S(1)}, u32[]{:S(2)}, u32[]{:S(2)}) collective-permute-start(bf16[2,384,256]{2,1,0:T(8,128)(2,1)S(1)} %get-tuple-element.7), channel_id=1, source_target_pairs={{0,4},{2,6},{4,0},{6,2},{8,12},{10,14},{12,8},{14,10},{1,5},{3,7},... | collective-permute-start | bytes 1179656 | tf_op jit(solution)/shard_map/ppermute | solution.py:109
  22.8 7.4 %collective-permute-done.3.b_one = bf16[2,384,256]{2,1,0:T(8,128)(2,1)S(1)} collective-permute-done((bf16[2,384,256]{2,1,0:T(8,128)(2,1)S(1)}, bf16[2,384,256]{2,1,0:T(8,128)(2,1)S(1)}, u32[]{:S(2)}, u32[]{:S(2)}) %collective-permute-start.3) | collective-permute-done | bytes 393248 | tf_op jit(solution)/shard_map/ppermute | solution.py:110
  30.3 2.2 %collective-permute-start.4 = (bf16[384,256]{1,0:T(8,128)(2,1)S(1)}, bf16[384,256]{1,0:T(8,128)(2,1)S(1)}, u32[]{:S(2)}, u32[]{:S(2)}) collective-permute-start(bf16[384,256]{1,0:T(8,128)(2,1)S(1)} %fusion.11), channel_id=1, source_target_pairs={{0,4},{2,6},{4,0},{6,2},{8,12},{10,14},{12,8},{14,10},{1,5},{3,7},... | collective-permute-start | bytes 589832 | tf_op jit(solution)/shard_map/ppermute | solution.py:112
  33.5 3.5 %collective-permute-start.2 = (bf16[384,256]{1,0:T(8,128)(2,1)S(1)}, bf16[384,256]{1,0:T(8,128)(2,1)S(1)}, u32[]{:S(2)}, u32[]{:S(2)}) collective-permute-start(bf16[384,256]{1,0:T(8,128)(2,1)S(1)} %fusion.10), channel_id=1, source_target_pairs={{0,12},{2,14},{4,8},{6,10},{8,4},{10,6},{12,0},{14,2},{1,13},{3,15... | collective-permute-start | bytes 589832 | tf_op jit(solution)/shard_map/ppermute | solution.py:111
  38.3 4.1 %collective-permute-done.2.a_two = bf16[384,256]{1,0:T(8,128)(2,1)S(1)} collective-permute-done((bf16[384,256]{1,0:T(8,128)(2,1)S(1)}, bf16[384,256]{1,0:T(8,128)(2,1)S(1)}, u32[]{:S(2)}, u32[]{:S(2)}) %collective-permute-start.2) | collective-permute-done | bytes 196640 | tf_op jit(solution)/shard_map/ppermute | solution.py:111
  43.3 12.5 %all-to-all-start = ((bf16[32,8,768]{2,1,0:T(8,128)(2,1)}), bf16[32,8,768]{2,1,0:T(8,128)(2,1)S(1)}, u32[]{:S(2)}, u32[]{:S(2)}) async-start(bf16[32,8,768]{2,1,0:T(8,128)(2,1)} %bitcast.9), calls=%async_computation | async-start | bytes 786432 | tf_op jit(solution)/shard_map/all_to_all | solution.py:160
  56.7 10.3 %all-to-all-done = bf16[32,8,768]{2,1,0:T(8,128)(2,1)S(1)} async-done(((bf16[32,8,768]{2,1,0:T(8,128)(2,1)}), bf16[32,8,768]{2,1,0:T(8,128)(2,1)S(1)}, u32[]{:S(2)}, u32[]{:S(2)}) %all-to-all-start) | async-done | bytes 393248 | tf_op jit(solution)/shard_map/all_to_all | solution.py:160
  71.1 3.4 %all-to-all-start.1 = ((bf16[4,8,4096]{2,1,0:T(8,128)(2,1)}), bf16[4,8,4096]{2,1,0:T(8,128)(2,1)S(1)}, u32[]{:S(2)}, u32[]{:S(2)}) async-start(bf16[4,8,4096]{2,1,0:T(8,128)(2,1)} %broadcast_in_dim.30), calls=%async_computation.1 | async-start | bytes 524288 | tf_op jit(solution)/shard_map/all_to_all | solution.py:130
  74.6 6.7 %all-to-all-done.1 = bf16[4,8,4096]{2,1,0:T(8,128)(2,1)S(1)} async-done(((bf16[4,8,4096]{2,1,0:T(8,128)(2,1)}), bf16[4,8,4096]{2,1,0:T(8,128)(2,1)S(1)}, u32[]{:S(2)}, u32[]{:S(2)}) %all-to-all-start.1) | async-done | bytes 262176 | tf_op jit(solution)/shard_map/all_to_all | solution.py:130
  82.0 5.6 %collective-permute-start.6 = (bf16[32,2048]{1,0:T(8,128)(2,1)S(1)}, bf16[32,2048]{1,0:T(8,128)(2,1)S(1)}, u32[]{:S(2)}, u32[]{:S(2)}) collective-permute-start(bf16[32,2048]{1,0:T(8,128)(2,1)S(1)} %get-tuple-element.10), channel_id=1, source_target_pairs={{0,448},{16,464},{32,480},{48,496},{64,128},{80,144},{96,160},{112... | collective-permute-start | bytes 393224 | tf_op jit(solution)/shard_map/ppermute | solution.py:146
  90.5 3.1 %collective-permute-start.7 = (bf16[32,2048]{1,0:T(8,128)(2,1)S(1)}, bf16[32,2048]{1,0:T(8,128)(2,1)S(1)}, u32[]{:S(2)}, u32[]{:S(2)}) collective-permute-start(bf16[32,2048]{1,0:T(8,128)(2,1)S(1)} %collective-permute-done.6), channel_id=1, source_target_pairs={{0,64},{16,80},{32,96},{48,112},{64,0},{80,16},{96,32},{112,48},{1... | collective-permute-start | bytes 393224 | tf_op jit(solution)/shard_map/ppermute | solution.py:146
  94.5 3.1 %collective-permute-start.8 = (bf16[32,2048]{1,0:T(8,128)(2,1)S(1)}, bf16[32,2048]{1,0:T(8,128)(2,1)S(1)}, u32[]{:S(2)}, u32[]{:S(2)}) collective-permute-start(bf16[32,2048]{1,0:T(8,128)(2,1)S(1)} %collective-permute-done.5), channel_id=1, source_target_pairs={{0,448},{16,464},{32,480},{48,496},{64,128},{80,144},{96,160},{112... | collective-permute-start | bytes 393224 | tf_op jit(solution)/shard_map/ppermute | solution.py:146
  97.7 5.1 %collective-permute-done.8 = bf16[32,2048]{1,0:T(8,128)(2,1)S(1)} collective-permute-done((bf16[32,2048]{1,0:T(8,128)(2,1)S(1)}, bf16[32,2048]{1,0:T(8,128)(2,1)S(1)}, u32[]{:S(2)}, u32[]{:S(2)}) %collective-permute-start.8) | collective-permute-done | bytes 131104 | tf_op jit(solution)/shard_map/ppermute | solution.py:146
  104.7 3.9 %collective-permute-start.10 = (bf16[32,2048]{1,0:T(8,128)(2,1)S(1)}, bf16[32,2048]{1,0:T(8,128)(2,1)S(1)}, u32[]{:S(2)}, u32[]{:S(2)}) collective-permute-start(bf16[32,2048]{1,0:T(8,128)(2,1)S(1)} %collective-permute-done.7), channel_id=1, source_target_pairs={{0,448},{16,464},{32,480},{48,496},{64,128},{80,144},{96,160},{112... | collective-permute-start | bytes 393224 | tf_op jit(solution)/shard_map/ppermute | solution.py:146
  108.6 6.0 %collective-permute-done.10 = bf16[32,2048]{1,0:T(8,128)(2,1)S(1)} collective-permute-done((bf16[32,2048]{1,0:T(8,128)(2,1)S(1)}, bf16[32,2048]{1,0:T(8,128)(2,1)S(1)}, u32[]{:S(2)}, u32[]{:S(2)}) %collective-permute-start.10) | collective-permute-done | bytes 131104 | tf_op jit(solution)/shard_map/ppermute | solution.py:146
  114.7 3.7 %collective-permute-start.11 = (bf16[16,2048]{1,0:T(8,128)(2,1)S(1)}, bf16[16,2048]{1,0:T(8,128)(2,1)S(1)}, u32[]{:S(2)}, u32[]{:S(2)}) collective-permute-start(bf16[16,2048]{1,0:T(8,128)(2,1)S(1)} %slice.77), channel_id=1, source_target_pairs={{0,64},{16,80},{32,96},{48,112},{64,0},{80,16},{96,32},{112,48},{1... | collective-permute-start | bytes 196616 | tf_op jit(solution)/shard_map/ppermute | solution.py:149
  121.2 5.3 %collective-permute-done.12 = bf16[16,2048]{1,0:T(8,128)(2,1)S(1)} collective-permute-done((bf16[16,2048]{1,0:T(8,128)(2,1)S(1)}, bf16[16,2048]{1,0:T(8,128)(2,1)S(1)}, u32[]{:S(2)}, u32[]{:S(2)}) %collective-permute-start.12) | collective-permute-done | bytes 65568 | tf_op jit(solution)/shard_map/ppermute | solution.py:149
  126.5 5.4 %all-gather.5.cloned.1.call-done = bf16[256,2048]{1,0:T(8,128)(2,1)} async-done(((bf16[32,2048]{1,0:T(8,128)(2,1)}), bf16[256,2048]{1,0:T(8,128)(2,1)}) %all-gather.5.cloned.1.call-update) | async-done | bytes 1048592 | tf_op jit(solution)/shard_map/all_gather | solution.py:133
  136.4 19.9 %all_to_all.15 = bf16[8,512,128]{2,1,0:T(8,128)(2,1)S(1)} all-to-all(bf16[8,512,128]{2,1,0:T(8,128)(2,1)S(1)} %bitcast.53), channel_id=1, replica_groups=mesh['node'=32,'hst'=8,'dp'=2] {'hst'}, dimensions={0} | all-to-all | bytes 2097152 | tf_op jit(solution)/shard_map/all_to_all | solution.py:192
  156.4 7.8 %collective-permute-start.13 = (bf16[512,128]{1,0:T(8,128)(2,1)S(1)}, bf16[512,128]{1,0:T(8,128)(2,1)S(1)}, u32[]{:S(2)}, u32[]{:S(2)}) collective-permute-start(bf16[512,128]{1,0:T(8,128)(2,1)S(1)} %fusion.12), channel_id=1, source_target_pairs={{0,1},{1,0},{2,3},{3,2},{4,5},{5,4},{6,7},{7,6},{8,9},{9,8},{10,11... | collective-permute-start | bytes 393224 | tf_op jit(solution)/shard_map/ppermute | solution.py:194
  164.9 2.5 %collective-permute-done.13 = bf16[512,128]{1,0:T(8,128)(2,1)S(1)} collective-permute-done((bf16[512,128]{1,0:T(8,128)(2,1)S(1)}, bf16[512,128]{1,0:T(8,128)(2,1)S(1)}, u32[]{:S(2)}, u32[]{:S(2)}) %collective-permute-start.13) | collective-permute-done | bytes 131104 | tf_op jit(solution)/shard_map/ppermute | solution.py:194
  (70 shorter events, 26.9 us)
Async XLA Ops:
  7.2 61.8 %copy-start = (bf16[128,32]{0,1:T(8,128)(2,1)S(1)}, bf16[128,32]{0,1:T(8,128)(2,1)}, u32[]{:S(2)}) copy-start(bf16[128,32]{0,1:T(8,128)(2,1)} %param.10) | copy-start | bytes 24580
  7.2 1.9 %copy-start.1 = (bf16[1,2048,4,192]{1,3,2,0:T(8,128)(2,1)S(1)}, bf16[1,2048,4,192]{1,3,2,0:T(8,128)(2,1)}, u32[]{:S(2)}) copy-start(bf16[1,2048,4,192]{1,3,2,0:T(8,128)(2,1)} %param.7) | copy-start | bytes 9437188
  9.5 5.3 %collective-permute-start = (bf16[3072,256]{1,0:T(8,128)(2,1)S(1)}, bf16[3072,256]{1,0:T(8,128)(2,1)S(1)}, u32[]{:S(2)}, u32[]{:S(2)}) collective-permute-start(bf16[3072,256]{1,0:T(8,128)(2,1)S(1)} %pack.1), channel_id=1, source_target_pairs={{0,2},{2,0},{4,6},{6,4},{8,10},{10,8},{12,14},{14,12},{1,3},{3,1},... | collective-permute-start | bytes 4718600 | tf_op jit(solution)/shard_map/ppermute | solution.py:87
  16.0 14.3 %collective-permute-start.3 = (bf16[2,384,256]{2,1,0:T(8,128)(2,1)S(1)}, bf16[2,384,256]{2,1,0:T(8,128)(2,1)S(1)}, u32[]{:S(2)}, u32[]{:S(2)}) collective-permute-start(bf16[2,384,256]{2,1,0:T(8,128)(2,1)S(1)} %get-tuple-element.9), channel_id=1, source_target_pairs={{0,12},{2,14},{4,8},{6,10},{8,4},{10,6},{12,0},{14,2},{1,13},{3,15... | collective-permute-start | bytes 1179656 | tf_op jit(solution)/shard_map/ppermute | solution.py:110
  20.6 12.8 %collective-permute-start.1 = (bf16[2,384,256]{2,1,0:T(8,128)(2,1)S(1)}, bf16[2,384,256]{2,1,0:T(8,128)(2,1)S(1)}, u32[]{:S(2)}, u32[]{:S(2)}) collective-permute-start(bf16[2,384,256]{2,1,0:T(8,128)(2,1)S(1)} %get-tuple-element.7), channel_id=1, source_target_pairs={{0,4},{2,6},{4,0},{6,2},{8,12},{10,14},{12,8},{14,10},{1,5},{3,7},... | collective-permute-start | bytes 1179656 | tf_op jit(solution)/shard_map/ppermute | solution.py:109
  30.2 26.4 %copy-start.4 = (s32[128]{0:T(128)S(1)}, s32[128]{0:T(128)}, u32[]{:S(2)}) copy-start(s32[128]{0:T(128)} %param.9) | copy-start | bytes 1540
  30.2 26.4 %copy-start.2 = (s32[1,1,8,128]{3,2,1,0:T(8,128)S(1)}, s32[1,1,8,128]{3,2,1,0:T(8,128)}, u32[]{:S(2)}) copy-start(s32[1,1,8,128]{3,2,1,0:T(8,128)} %param.8) | copy-start | bytes 12292
  30.3 8.0 %collective-permute-start.4 = (bf16[384,256]{1,0:T(8,128)(2,1)S(1)}, bf16[384,256]{1,0:T(8,128)(2,1)S(1)}, u32[]{:S(2)}, u32[]{:S(2)}) collective-permute-start(bf16[384,256]{1,0:T(8,128)(2,1)S(1)} %fusion.11), channel_id=1, source_target_pairs={{0,4},{2,6},{4,0},{6,2},{8,12},{10,14},{12,8},{14,10},{1,5},{3,7},... | collective-permute-start | bytes 589832 | tf_op jit(solution)/shard_map/ppermute | solution.py:112
  33.5 8.9 %collective-permute-start.2 = (bf16[384,256]{1,0:T(8,128)(2,1)S(1)}, bf16[384,256]{1,0:T(8,128)(2,1)S(1)}, u32[]{:S(2)}, u32[]{:S(2)}) collective-permute-start(bf16[384,256]{1,0:T(8,128)(2,1)S(1)} %fusion.10), channel_id=1, source_target_pairs={{0,12},{2,14},{4,8},{6,10},{8,4},{10,6},{12,0},{14,2},{1,13},{3,15... | collective-permute-start | bytes 589832 | tf_op jit(solution)/shard_map/ppermute | solution.py:111
  43.3 23.6 %all-to-all-start = ((bf16[32,8,768]{2,1,0:T(8,128)(2,1)}), bf16[32,8,768]{2,1,0:T(8,128)(2,1)S(1)}, u32[]{:S(2)}, u32[]{:S(2)}) async-start(bf16[32,8,768]{2,1,0:T(8,128)(2,1)} %bitcast.9), calls=%async_computation | async-start | bytes 786432 | tf_op jit(solution)/shard_map/all_to_all | solution.py:160
  55.9 70.6 %all-gather.3.cloned.1.call-start = ((), (), s32[]{:S(2)}) async-start(), calls=%async_computation.3 | async-start | bytes 1179648 | tf_op jit(solution)/shard_map/all_gather | solution.py:157
  71.1 10.2 %all-to-all-start.1 = ((bf16[4,8,4096]{2,1,0:T(8,128)(2,1)}), bf16[4,8,4096]{2,1,0:T(8,128)(2,1)S(1)}, u32[]{:S(2)}, u32[]{:S(2)}) async-start(bf16[4,8,4096]{2,1,0:T(8,128)(2,1)} %broadcast_in_dim.30), calls=%async_computation.1 | async-start | bytes 524288 | tf_op jit(solution)/shard_map/all_to_all | solution.py:130
  74.5 57.4 %all-gather.5.cloned.1.call-start = ((), (), s32[]{:S(2)}) async-start(), calls=%async_computation.4 | async-start | bytes 1179648 | tf_op jit(solution)/shard_map/all_gather | solution.py:133
  82.0 8.5 %collective-permute-start.6 = (bf16[32,2048]{1,0:T(8,128)(2,1)S(1)}, bf16[32,2048]{1,0:T(8,128)(2,1)S(1)}, u32[]{:S(2)}, u32[]{:S(2)}) collective-permute-start(bf16[32,2048]{1,0:T(8,128)(2,1)S(1)} %get-tuple-element.10), channel_id=1, source_target_pairs={{0,448},{16,464},{32,480},{48,496},{64,128},{80,144},{96,160},{112... | collective-permute-start | bytes 393224 | tf_op jit(solution)/shard_map/ppermute | solution.py:146
  87.6 6.9 %collective-permute-start.5 = (bf16[32,2048]{1,0:T(8,128)(2,1)S(1)}, bf16[32,2048]{1,0:T(8,128)(2,1)S(1)}, u32[]{:S(2)}, u32[]{:S(2)}) collective-permute-start(bf16[32,2048]{1,0:T(8,128)(2,1)S(1)} %get-tuple-element.10), channel_id=1, source_target_pairs={{0,64},{16,80},{32,96},{48,112},{64,0},{80,16},{96,32},{112,48},{1... | collective-permute-start | bytes 393224 | tf_op jit(solution)/shard_map/ppermute | solution.py:146
  90.5 14.1 %collective-permute-start.7 = (bf16[32,2048]{1,0:T(8,128)(2,1)S(1)}, bf16[32,2048]{1,0:T(8,128)(2,1)S(1)}, u32[]{:S(2)}, u32[]{:S(2)}) collective-permute-start(bf16[32,2048]{1,0:T(8,128)(2,1)S(1)} %collective-permute-done.6), channel_id=1, source_target_pairs={{0,64},{16,80},{32,96},{48,112},{64,0},{80,16},{96,32},{112,48},{1... | collective-permute-start | bytes 393224 | tf_op jit(solution)/shard_map/ppermute | solution.py:146
  94.5 8.3 %collective-permute-start.8 = (bf16[32,2048]{1,0:T(8,128)(2,1)S(1)}, bf16[32,2048]{1,0:T(8,128)(2,1)S(1)}, u32[]{:S(2)}, u32[]{:S(2)}) collective-permute-start(bf16[32,2048]{1,0:T(8,128)(2,1)S(1)} %collective-permute-done.5), channel_id=1, source_target_pairs={{0,448},{16,464},{32,480},{48,496},{64,128},{80,144},{96,160},{112... | collective-permute-start | bytes 393224 | tf_op jit(solution)/shard_map/ppermute | solution.py:146
  102.7 15.6 %collective-permute-start.9 = (bf16[32,2048]{1,0:T(8,128)(2,1)S(1)}, bf16[32,2048]{1,0:T(8,128)(2,1)S(1)}, u32[]{:S(2)}, u32[]{:S(2)}) collective-permute-start(bf16[32,2048]{1,0:T(8,128)(2,1)S(1)} %collective-permute-done.8), channel_id=1, source_target_pairs={{0,64},{16,80},{32,96},{48,112},{64,0},{80,16},{96,32},{112,48},{1... | collective-permute-start | bytes 393224 | tf_op jit(solution)/shard_map/ppermute | solution.py:146
  104.7 10.0 %collective-permute-start.10 = (bf16[32,2048]{1,0:T(8,128)(2,1)S(1)}, bf16[32,2048]{1,0:T(8,128)(2,1)S(1)}, u32[]{:S(2)}, u32[]{:S(2)}) collective-permute-start(bf16[32,2048]{1,0:T(8,128)(2,1)S(1)} %collective-permute-done.7), channel_id=1, source_target_pairs={{0,448},{16,464},{32,480},{48,496},{64,128},{80,144},{96,160},{112... | collective-permute-start | bytes 393224 | tf_op jit(solution)/shard_map/ppermute | solution.py:146
  114.7 6.5 %collective-permute-start.11 = (bf16[16,2048]{1,0:T(8,128)(2,1)S(1)}, bf16[16,2048]{1,0:T(8,128)(2,1)S(1)}, u32[]{:S(2)}, u32[]{:S(2)}) collective-permute-start(bf16[16,2048]{1,0:T(8,128)(2,1)S(1)} %slice.77), channel_id=1, source_target_pairs={{0,64},{16,80},{32,96},{48,112},{64,0},{80,16},{96,32},{112,48},{1... | collective-permute-start | bytes 196616 | tf_op jit(solution)/shard_map/ppermute | solution.py:149
  118.4 8.1 %collective-permute-start.12 = (bf16[16,2048]{1,0:T(8,128)(2,1)S(1)}, bf16[16,2048]{1,0:T(8,128)(2,1)S(1)}, u32[]{:S(2)}, u32[]{:S(2)}) collective-permute-start(bf16[16,2048]{1,0:T(8,128)(2,1)S(1)} %slice.78), channel_id=1, source_target_pairs={{0,448},{16,464},{32,480},{48,496},{64,128},{80,144},{96,160},{112... | collective-permute-start | bytes 196616 | tf_op jit(solution)/shard_map/ppermute | solution.py:149
  120.3 14.9 %copy-start.6 = (bf16[1,1,256,128]{3,2,1,0:T(8,128)(2,1)S(1)}, bf16[1,1,256,128]{3,2,1,0:T(8,128)(2,1)}, u32[]{:S(2)}) copy-start(bf16[1,1,256,128]{3,2,1,0:T(8,128)(2,1)} %param.13) | copy-start | bytes 196612
  133.6 2.1 %copy-start.5 = (bf16[256,2048]{1,0:T(8,128)(2,1)S(1)}, bf16[256,2048]{1,0:T(8,128)(2,1)}, u32[]{:S(2)}) copy-start(bf16[256,2048]{1,0:T(8,128)(2,1)} %all-gather.5.cloned.1.call-done) | copy-start | bytes 3145732
  156.4 11.1 %collective-permute-start.13 = (bf16[512,128]{1,0:T(8,128)(2,1)S(1)}, bf16[512,128]{1,0:T(8,128)(2,1)S(1)}, u32[]{:S(2)}, u32[]{:S(2)}) collective-permute-start(bf16[512,128]{1,0:T(8,128)(2,1)S(1)} %fusion.12), channel_id=1, source_target_pairs={{0,1},{1,0},{2,3},{3,2},{4,5},{5,4},{6,7},{7,6},{8,9},{9,8},{10,11... | collective-permute-start | bytes 393224 | tf_op jit(solution)/shard_map/ppermute | solution.py:194
  (1 other events, 1.3 us)
Sparse Core Ops, SparseCore 0:
  58.9 29.1 all-gather.2
  90.7 41.1 all-gather.4

commit v5 on v4

v5 whole, which is shorter than its diff:
```python
import jax
import jax.numpy as jnp
from jax import lax
from jax.experimental import pallas as pl
from jax.experimental.pallas import tpu as pltpu
from jax.sharding import PartitionSpec as P

N_X = 4
N_CORE = 2
N_Y = 8
N_Z = 4
VMEM = 12 * 2**20

def swaps(size, partner):
    return [(i, partner(i)) for i in range(size)]


CORE_SWAP = swaps(N_X * N_CORE, lambda h: h ^ 1)
X_EVEN = swaps(N_X * N_CORE, lambda h: h ^ 2)
X_ODD = swaps(N_X * N_CORE, lambda h: h ^ 6)
Y_EVEN = swaps(N_Y * N_Z, lambda n: n ^ N_Z)
Y_ODD = swaps(N_Y * N_Z, lambda n: (((n // N_Z + 1) ^ 1) - 1) % N_Y * N_Z + n % N_Z)
Z_GROUPS = [[N_Z * y + z for z in range(N_Z)] for y in range(N_Y)]
X_GROUPS = [[N_CORE * x + c for x in range(N_X)] for c in range(N_CORE)]
DP_SWAP = swaps(2, lambda d: d ^ 1)


def add(*terms):
    total = terms[0].astype(jnp.float32)
    for term in terms[1:]:
        total = total + term.astype(jnp.float32)
    return total


def pack_kernel(h_ref, rows_ref, out_ref):
    out_ref[...] = rows_ref[...]


def pair_kernel(h_ref, rows_ref, got_ref, *out_refs):
    total = add(rows_ref[...], got_ref[...]).astype(rows_ref.dtype)
    half = total.shape[0] // 2
    for j in range(N_X):

        @pl.when(pl.program_id(0) == j)
        def _(away=-j % N_X):
            out_refs[away][...] = total[:half]
            out_refs[N_X + away][...] = total[half:]


def turn_kernel(*refs):
    out_ref = refs[-1]
    half = refs[0].shape[0]
    for first, parts in ((0, refs[:3]), (half, refs[3:6])):
        for row in range(0, half, 128):
            total = add(*[part[row : row + 128] for part in parts])
            out_ref[:, first + row : first + row + 128] = total.T.astype(out_ref.dtype)


def sum_partials(flat):
    rows, samples = flat.shape[0], flat.shape[1] // (N_X * N_CORE)
    half = rows // 2
    h = lax.axis_index("hst").astype(jnp.int32).reshape(1)
    params = pltpu.CompilerParams(vmem_limit_bytes=VMEM)
    block = pl.BlockSpec((rows, samples), lambda j, h: (j, 0))
    theirs = pl.BlockSpec((rows, samples), lambda j, h: (0, h[0] ^ 1 ^ (6 * j % 8)))
    mine = pl.BlockSpec((rows, samples), lambda j, h: (0, h[0] ^ (6 * j % 8)))
    given = pl.pallas_call(
        pack_kernel,
        out_shape=jax.ShapeDtypeStruct((N_X * rows, samples), flat.dtype),
        grid_spec=pltpu.PrefetchScalarGridSpec(
            num_scalar_prefetch=1, grid=(N_X,), in_specs=[theirs], out_specs=block
        ),
        compiler_params=pltpu.CompilerParams(vmem_limit_bytes=4 * VMEM),
        name="pack",
    )(h, flat)
    got = lax.ppermute(given, "hst", CORE_SWAP)

    out = pl.pallas_call(
        pair_kernel,
        out_shape=[jax.ShapeDtypeStruct((half, samples), flat.dtype)] * (2 * N_X),
        grid_spec=pltpu.PrefetchScalarGridSpec(
            num_scalar_prefetch=1,
            grid=(N_X,),
            in_specs=[mine, block],
            out_specs=[pl.BlockSpec((half, samples), lambda j, h: (0, 0))] * (2 * N_X),
        ),
        compiler_params=params,
        name="pair",
    )(h, flat, got)
    a, b = out[:N_X], out[N_X:]
    a_far = lax.ppermute(a[2], "hst", X_EVEN)
    b_far = lax.ppermute(b[2], "hst", X_ODD)
    a_one = lax.ppermute(a[1], "hst", X_EVEN)
    b_one = lax.ppermute(b[3], "hst", X_ODD)
    a_two = lax.ppermute(add(a[3], a_far).astype(flat.dtype), "hst", X_ODD)
    b_two = lax.ppermute(add(b[1], b_far).astype(flat.dtype), "hst", X_EVEN)
    return pl.pallas_call(
        turn_kernel,
        out_shape=jax.ShapeDtypeStruct((samples, rows), flat.dtype),
        compiler_params=params,
        name="turn",
    )(a[0], a_one, a_two, b[0], b_one, b_two)


def normalize(flat_rows, ln_gain):
    middle = jnp.mean(flat_rows, axis=-1, keepdims=True)
    centered = flat_rows - middle
    variance = jnp.mean(centered * centered, axis=-1, keepdims=True)
    return (centered * lax.rsqrt(variance + 1e-05) * ln_gain).astype(jnp.bfloat16)


def gather_nodes(block):
    copies = jnp.broadcast_to(block, (N_Z,) + block.shape)
    line = lax.all_to_all(copies, "node", 0, 0, axis_index_groups=Z_GROUPS, tiled=True)
    line = line.reshape(-1, block.shape[1])
    rows, half = line.shape[0], line.shape[0] // 2
    y = lax.axis_index("node") // N_Z
    sign = 1 - 2 * (y % 2)

    def put(group, part, distance, first_row=0):
        place = (y + sign * distance) % N_Y * rows + first_row
        return lax.dynamic_update_slice(group, part, (place, 0))

    even = odd = line
    group = put(jnp.zeros((N_Y * rows, line.shape[1]), line.dtype), line, 0)
    for distance in range(1, N_Y // 2):
        even, odd = lax.ppermute(odd, "node", Y_EVEN), lax.ppermute(even, "node", Y_ODD)
        group = put(put(group, even, distance), odd, -distance)
    even, odd = lax.ppermute(odd[:half], "node", Y_EVEN), lax.ppermute(even[half:], "node", Y_ODD)
    return put(put(group, even, N_Y // 2), odd, N_Y // 2, half)


def local(partials, counts, perm, fm_proj, ln_gain, w_in, d_hidden):
    samples = counts.shape[2]
    group, hidden_here = d_hidden.shape[2], d_hidden.shape[3]
    w_full = lax.all_gather(w_in, "hst", axis=0, tiled=True)
    rows = partials.shape[2] * partials.shape[3]
    summed = sum_partials(partials[0].transpose(1, 2, 0).reshape(rows, -1))
    shard_rows = lax.all_to_all(
        summed.reshape(N_Y * N_Z, samples, rows), "node", split_axis=0, concat_axis=0, tiled=True
    )
    shard_rows = shard_rows.transpose(1, 0, 2).reshape(samples, -1, partials.shape[3])
    ordered = jnp.take(shard_rows, perm, axis=1, mode="clip")
    counts_here = counts[0, 0]
    divisor = jnp.maximum(counts_here, 1).astype(jnp.float32)[:, :, None]
    pooled = jnp.where(
        counts_here[:, :, None] > 0, ordered.astype(jnp.float32) / divisor, 0.0
    ).astype(jnp.bfloat16)
    projected = jnp.einsum(
        "sfe,fk->sek", pooled, fm_proj, preferred_element_type=jnp.float32
    ).astype(jnp.bfloat16)
    pairwise = jnp.einsum("sfe,sek->sfk", pooled, projected, preferred_element_type=jnp.float32)
    z_local = normalize(pairwise.reshape(samples, -1), ln_gain)

    z_group = gather_nodes(z_local)
    pre_act = jnp.dot(z_group, w_full, preferred_element_type=jnp.float32)
    sigma = jax.nn.sigmoid(pre_act)
    hidden = (pre_act * sigma).astype(jnp.bfloat16)
    d_pre = (d_hidden[0, 0].astype(jnp.float32) * sigma * (1.0 + pre_act * (1.0 - sigma))).astype(
        jnp.bfloat16
    )
    term = lax.dot_general(
        z_group, d_pre, (((0,), (0,)), ((), ())), preferred_element_type=jnp.float32
    ).astype(jnp.bfloat16)
    term = term.reshape(N_X, N_CORE, w_in.shape[0], hidden_here)
    core = lax.axis_index("hst") % N_CORE
    given = lax.dynamic_index_in_dim(term, 1 - core, 1, keepdims=False)
    kept = lax.dynamic_index_in_dim(term, core, 1, keepdims=False)
    pair = add(kept, lax.ppermute(given, "hst", CORE_SWAP)).astype(jnp.bfloat16)
    terms = lax.all_to_all(pair, "hst", 0, 0, axis_index_groups=X_GROUPS, tiled=True)
    share = add(*[terms[i] for i in range(N_X)]).astype(jnp.bfloat16)
    grad_w = add(share, lax.ppermute(share, "dp", DP_SWAP))
    return (hidden.reshape(1, 1, group, hidden_here), grad_w)


def solution(mesh):
    in_specs = (
        P("hst", "dp", "node", None),
        P("dp", "hst", "node", None),
        P(),
        P(),
        P(),
        P("hst", "node"),
        P("dp", "hst", None, "node"),
    )
    out_specs = (P("dp", "hst", None, "node"), P("hst", "node"))
    return jax.shard_map(local, mesh=mesh, in_specs=in_specs, out_specs=out_specs, check_vma=False)
```

time: 178 us -> 172 us (0.966)
  the two profiles are of different devices: /device:TPU:56 before, /device:TPU:64 now
where the time goes in v5:
time: 172 us; the launch traced here: 171 us
  starting transfers between devices  68.5 us (40%)
  waiting for transfers between devices  60.3 us (35%)
  between operations  14.7 us (9%)
  blocking collectives  13.7 us (8%)
  local copies, waits for them, and re-layouts  5.48 us (3%)
  matrix products  3.34 us (2%)
  Pallas kernels  2.56 us (1%)
  other arithmetic  2.12 us (1%)
    ppermute x3, waiting for transfers between devices, gather_nodes(): lax.ppermute(even, 'node', Y_ODD)  22.3 us
    all_to_all x1, blocking collectives, local(): lax.all_to_all(pair, 'hst', 0, 0, axis_index_groups=X_GROUPS, tiled=True)  13.7 us
    all_to_all x1, starting transfers between devices, local(): lax.all_to_all(summed.reshape(N_Y * N_Z, samples, rows), 'node', split_ax...  12.3 us
    all_to_all x1, waiting for transfers between devices, local(): lax.all_to_all(summed.reshape(N_Y * N_Z, samples, rows), 'node', split_ax...  11.8 us
    ppermute x1, starting transfers between devices, local(): grad_w = add(share, lax.ppermute(share, 'dp', DP_SWAP))  8.1 us
    ppermute x3, starting transfers between devices, gather_nodes(): lax.ppermute(odd, 'node', Y_EVEN)  7.68 us
    ppermute x3, starting transfers between devices, gather_nodes(): lax.ppermute(even, 'node', Y_ODD)  7.2 us
    all_to_all x1, starting transfers between devices, gather_nodes(): lax.all_to_all(copies, 'node', 0, 0, axis_index_groups=Z_GROUPS, tiled=True)  5.97 us
  transfers between devices with their start and end apart: 20, of which 13 were waited for; matrix products, arithmetic and copies ran while one was open for 1% of the time, Pallas kernels for 0%

profile of v5, /device:TPU:64, one launch (start us, length us, event | category | flops | bytes accessed | tf_op | source)
XLA Modules:
  0.0 170.7 jit_solution(15990386757293266395)
XLA Ops:
  11.5 3.4 %collective-permute-done.got_ref = bf16[3072,256]{1,0:T(8,128)(2,1)S(1)} collective-permute-done((bf16[3072,256]{1,0:T(8,128)(2,1)S(1)}, bf16[3072,256]{1,0:T(8,128)(2,1)S(1)}, u32[]{:S(2)}, u32[]{:S(2)}) %collective-permute-start) | collective-permute-done | bytes 1572896 | tf_op jit(solution)/shard_map/ppermute | solution.py:76
  16.0 4.7 %collective-permute-start.5 = (bf16[384,256]{1,0:T(8,128)(2,1)S(1)}, bf16[384,256]{1,0:T(8,128)(2,1)S(1)}, u32[]{:S(2)}, u32[]{:S(2)}) collective-permute-start(bf16[384,256]{1,0:T(8,128)(2,1)S(1)} %get-tuple-element.17), channel_id=1, source_target_pairs={{0,12},{2,14},{4,8},{6,10},{8,4},{10,6},{12,0},{14,2},{1,13},{3,15... | collective-permute-start | bytes 589832 | tf_op jit(solution)/shard_map/ppermute | solution.py:92
  20.7 2.1 %collective-permute-start.2 = (bf16[384,256]{1,0:T(8,128)(2,1)S(1)}, bf16[384,256]{1,0:T(8,128)(2,1)S(1)}, u32[]{:S(2)}, u32[]{:S(2)}) collective-permute-start(bf16[384,256]{1,0:T(8,128)(2,1)S(1)} %get-tuple-element.13), channel_id=1, source_target_pairs={{0,4},{2,6},{4,0},{6,2},{8,12},{10,14},{12,8},{14,10},{1,5},{3,7},... | collective-permute-start | bytes 589832 | tf_op jit(solution)/shard_map/ppermute | solution.py:91
  22.8 3.7 %collective-permute-start.1 = (bf16[384,256]{1,0:T(8,128)(2,1)S(1)}, bf16[384,256]{1,0:T(8,128)(2,1)S(1)}, u32[]{:S(2)}, u32[]{:S(2)}) collective-permute-start(bf16[384,256]{1,0:T(8,128)(2,1)S(1)} %get-tuple-element.11), channel_id=1, source_target_pairs={{0,4},{2,6},{4,0},{6,2},{8,12},{10,14},{12,8},{14,10},{1,5},{3,7},... | collective-permute-start | bytes 589832 | tf_op jit(solution)/shard_map/ppermute | solution.py:93
  26.5 2.4 %collective-permute-start.4 = (bf16[384,256]{1,0:T(8,128)(2,1)S(1)}, bf16[384,256]{1,0:T(8,128)(2,1)S(1)}, u32[]{:S(2)}, u32[]{:S(2)}) collective-permute-start(bf16[384,256]{1,0:T(8,128)(2,1)S(1)} %get-tuple-element.15), channel_id=1, source_target_pairs={{0,12},{2,14},{4,8},{6,10},{8,4},{10,6},{12,0},{14,2},{1,13},{3,15... | collective-permute-start | bytes 589832 | tf_op jit(solution)/shard_map/ppermute | solution.py:94
  29.0 2.2 %collective-permute-start.6 = (bf16[384,256]{1,0:T(8,128)(2,1)S(1)}, bf16[384,256]{1,0:T(8,128)(2,1)S(1)}, u32[]{:S(2)}, u32[]{:S(2)}) collective-permute-start(bf16[384,256]{1,0:T(8,128)(2,1)S(1)} %add_convert_fusion), channel_id=1, source_target_pairs={{0,4},{2,6},{4,0},{6,2},{8,12},{10,14},{12,8},{14,10},{1,5},{3,7},... | collective-permute-start | bytes 589832 | tf_op jit(solution)/shard_map/ppermute | solution.py:96
  31.3 4.4 %collective-permute-start.3 = (bf16[384,256]{1,0:T(8,128)(2,1)S(1)}, bf16[384,256]{1,0:T(8,128)(2,1)S(1)}, u32[]{:S(2)}, u32[]{:S(2)}) collective-permute-start(bf16[384,256]{1,0:T(8,128)(2,1)S(1)} %add_convert_fusion.1), channel_id=1, source_target_pairs={{0,12},{2,14},{4,8},{6,10},{8,4},{10,6},{12,0},{14,2},{1,13},{3,15... | collective-permute-start | bytes 589832 | tf_op jit(solution)/shard_map/ppermute | solution.py:95
  37.7 2.4 %collective-permute-done.3.refs_2_ = bf16[384,256]{1,0:T(8,128)(2,1)S(1)} collective-permute-done((bf16[384,256]{1,0:T(8,128)(2,1)S(1)}, bf16[384,256]{1,0:T(8,128)(2,1)S(1)}, u32[]{:S(2)}, u32[]{:S(2)}) %collective-permute-start.3) | collective-permute-done | bytes 196640 | tf_op jit(solution)/shard_map/ppermute | solution.py:95
  41.0 12.3 %all-to-all-start = ((bf16[32,8,768]{2,1,0:T(8,128)(2,1)}), bf16[32,8,768]{2,1,0:T(8,128)(2,1)S(1)}, u32[]{:S(2)}, u32[]{:S(2)}) async-start(bf16[32,8,768]{2,1,0:T(8,128)(2,1)} %bitcast.7), calls=%async_computation | async-start | bytes 786432 | tf_op jit(solution)/shard_map/all_to_all | solution.py:139
  53.4 11.8 %all-to-all-done = bf16[32,8,768]{2,1,0:T(8,128)(2,1)S(1)} async-done(((bf16[32,8,768]{2,1,0:T(8,128)(2,1)}), bf16[32,8,768]{2,1,0:T(8,128)(2,1)S(1)}, u32[]{:S(2)}, u32[]{:S(2)}) %all-to-all-start) | async-done | bytes 393248 | tf_op jit(solution)/shard_map/all_to_all | solution.py:139
  69.3 6.0 %all-to-all-start.1 = ((bf16[4,8,4096]{2,1,0:T(8,128)(2,1)}), bf16[4,8,4096]{2,1,0:T(8,128)(2,1)S(1)}, u32[]{:S(2)}, u32[]{:S(2)}) async-start(bf16[4,8,4096]{2,1,0:T(8,128)(2,1)} %broadcast_in_dim.30), calls=%async_computation.1 | async-start | bytes 524288 | tf_op jit(solution)/shard_map/all_to_all | solution.py:114
  76.2 5.3 %all-to-all-done.1 = bf16[4,8,4096]{2,1,0:T(8,128)(2,1)S(1)} async-done(((bf16[4,8,4096]{2,1,0:T(8,128)(2,1)}), bf16[4,8,4096]{2,1,0:T(8,128)(2,1)S(1)}, u32[]{:S(2)}, u32[]{:S(2)}) %all-to-all-start.1) | async-done | bytes 262176 | tf_op jit(solution)/shard_map/all_to_all | solution.py:114
  81.4 2.5 %collective-permute-start.7 = (bf16[32,4096]{1,0:T(8,128)(2,1)S(1)}, bf16[32,4096]{1,0:T(8,128)(2,1)S(1)}, u32[]{:S(2)}, u32[]{:S(2)}) collective-permute-start(bf16[32,4096]{1,0:T(8,128)(2,1)S(1)} %bitcast.60), channel_id=1, source_target_pairs={{0,64},{16,80},{32,96},{48,112},{64,0},{80,16},{96,32},{112,48},{1... | collective-permute-start | bytes 786440 | tf_op jit(solution)/shard_map/ppermute | solution.py:127
  84.0 2.7 %collective-permute-start.8 = (bf16[32,4096]{1,0:T(8,128)(2,1)S(1)}, bf16[32,4096]{1,0:T(8,128)(2,1)S(1)}, u32[]{:S(2)}, u32[]{:S(2)}) collective-permute-start(bf16[32,4096]{1,0:T(8,128)(2,1)S(1)} %bitcast.61), channel_id=1, source_target_pairs={{0,448},{16,464},{32,480},{48,496},{64,128},{80,144},{96,160},{112... | collective-permute-start | bytes 786440 | tf_op jit(solution)/shard_map/ppermute | solution.py:127
  86.9 6.5 %collective-permute-done.8 = bf16[32,4096]{1,0:T(8,128)(2,1)S(1)} collective-permute-done((bf16[32,4096]{1,0:T(8,128)(2,1)S(1)}, bf16[32,4096]{1,0:T(8,128)(2,1)S(1)}, u32[]{:S(2)}, u32[]{:S(2)}) %collective-permute-start.8) | collective-permute-done | bytes 262176 | tf_op jit(solution)/shard_map/ppermute | solution.py:127
  95.6 2.5 %collective-permute-start.10 = (bf16[32,4096]{1,0:T(8,128)(2,1)S(1)}, bf16[32,4096]{1,0:T(8,128)(2,1)S(1)}, u32[]{:S(2)}, u32[]{:S(2)}) collective-permute-start(bf16[32,4096]{1,0:T(8,128)(2,1)S(1)} %collective-permute-done.7), channel_id=1, source_target_pairs={{0,448},{16,464},{32,480},{48,496},{64,128},{80,144},{96,160},{112... | collective-permute-start | bytes 786440 | tf_op jit(solution)/shard_map/ppermute | solution.py:127
  98.1 7.0 %collective-permute-done.10 = bf16[32,4096]{1,0:T(8,128)(2,1)S(1)} collective-permute-done((bf16[32,4096]{1,0:T(8,128)(2,1)S(1)}, bf16[32,4096]{1,0:T(8,128)(2,1)S(1)}, u32[]{:S(2)}, u32[]{:S(2)}) %collective-permute-start.10) | collective-permute-done | bytes 262176 | tf_op jit(solution)/shard_map/ppermute | solution.py:127
  105.1 3.1 %collective-permute-start.11 = (bf16[32,4096]{1,0:T(8,128)(2,1)S(1)}, bf16[32,4096]{1,0:T(8,128)(2,1)S(1)}, u32[]{:S(2)}, u32[]{:S(2)}) collective-permute-start(bf16[32,4096]{1,0:T(8,128)(2,1)S(1)} %collective-permute-done.10), channel_id=1, source_target_pairs={{0,64},{16,80},{32,96},{48,112},{64,0},{80,16},{96,32},{112,48},{1... | collective-permute-start | bytes 786440 | tf_op jit(solution)/shard_map/ppermute | solution.py:127
  110.3 8.8 %collective-permute-done.12 = bf16[32,4096]{1,0:T(8,128)(2,1)S(1)} collective-permute-done((bf16[32,4096]{1,0:T(8,128)(2,1)S(1)}, bf16[32,4096]{1,0:T(8,128)(2,1)S(1)}, u32[]{:S(2)}, u32[]{:S(2)}) %collective-permute-start.12) | collective-permute-done | bytes 262176 | tf_op jit(solution)/shard_map/ppermute | solution.py:127
  123.1 2.9 %collective-permute-done.13 = bf16[16,4096]{1,0:T(8,128)(2,1)S(1)} collective-permute-done((bf16[16,4096]{1,0:T(8,128)(2,1)S(1)}, bf16[16,4096]{1,0:T(8,128)(2,1)S(1)}, u32[]{:S(2)}, u32[]{:S(2)}) %collective-permute-start.13) | collective-permute-done | bytes 131104 | tf_op jit(solution)/shard_map/ppermute | solution.py:129
  126.0 3.2 %collective-permute-done.14 = bf16[16,4096]{1,0:T(8,128)(2,1)S(1)} collective-permute-done((bf16[16,4096]{1,0:T(8,128)(2,1)S(1)}, bf16[16,4096]{1,0:T(8,128)(2,1)S(1)}, u32[]{:S(2)}, u32[]{:S(2)}) %collective-permute-start.14) | collective-permute-done | bytes 131104 | tf_op jit(solution)/shard_map/ppermute | solution.py:129
  136.0 13.7 %all_to_all.15 = bf16[4,512,128]{2,1,0:T(8,128)(2,1)S(1)} all-to-all(bf16[4,512,128]{2,1,0:T(8,128)(2,1)S(1)} %fusion.1), channel_id=1, replica_groups={{0,4,8,12},{2,6,10,14},{1,5,9,13},{3,7,11,15},{16,20,24,28},{18,22,26,3..., dimensions={0} | all-to-all | bytes 1048576 | tf_op jit(solution)/shard_map/all_to_all | solution.py:170
  149.7 8.1 %collective-permute-start.16 = (bf16[512,128]{1,0:T(8,128)(2,1)S(1)}, bf16[512,128]{1,0:T(8,128)(2,1)S(1)}, u32[]{:S(2)}, u32[]{:S(2)}) collective-permute-start(bf16[512,128]{1,0:T(8,128)(2,1)S(1)} %fusion.8), channel_id=1, source_target_pairs={{0,1},{1,0},{2,3},{3,2},{4,5},{5,4},{6,7},{7,6},{8,9},{9,8},{10,11... | collective-permute-start | bytes 393224 | tf_op jit(solution)/shard_map/ppermute | solution.py:172
  158.5 4.6 %collective-permute-done.16 = bf16[512,128]{1,0:T(8,128)(2,1)S(1)} collective-permute-done((bf16[512,128]{1,0:T(8,128)(2,1)S(1)}, bf16[512,128]{1,0:T(8,128)(2,1)S(1)}, u32[]{:S(2)}, u32[]{:S(2)}) %collective-permute-start.16) | collective-permute-done | bytes 131104 | tf_op jit(solution)/shard_map/ppermute | solution.py:172
  (70 shorter events, 29.9 us)
Async XLA Ops:
  7.2 60.0 %copy-start = (bf16[128,32]{0,1:T(8,128)(2,1)S(1)}, bf16[128,32]{0,1:T(8,128)(2,1)}, u32[]{:S(2)}) copy-start(bf16[128,32]{0,1:T(8,128)(2,1)} %param.10) | copy-start | bytes 24580
  9.5 5.3 %collective-permute-start = (bf16[3072,256]{1,0:T(8,128)(2,1)S(1)}, bf16[3072,256]{1,0:T(8,128)(2,1)S(1)}, u32[]{:S(2)}, u32[]{:S(2)}) collective-permute-start(bf16[3072,256]{1,0:T(8,128)(2,1)S(1)} %pack.1), channel_id=1, source_target_pairs={{0,2},{2,0},{4,6},{6,4},{8,10},{10,8},{12,14},{14,12},{1,3},{3,1},... | collective-permute-start | bytes 4718600 | tf_op jit(solution)/shard_map/ppermute | solution.py:76
  16.0 37.4 %copy-start.5 = (s32[128]{0:T(128)S(1)}, s32[128]{0:T(128)}, u32[]{:S(2)}) copy-start(s32[128]{0:T(128)} %param.9) | copy-start | bytes 1540
  16.0 37.4 %copy-start.3 = (s32[1,1,8,128]{3,2,1,0:T(8,128)S(1)}, s32[1,1,8,128]{3,2,1,0:T(8,128)}, u32[]{:S(2)}) copy-start(s32[1,1,8,128]{3,2,1,0:T(8,128)} %param.8) | copy-start | bytes 12292
  16.0 12.9 %collective-permute-start.5 = (bf16[384,256]{1,0:T(8,128)(2,1)S(1)}, bf16[384,256]{1,0:T(8,128)(2,1)S(1)}, u32[]{:S(2)}, u32[]{:S(2)}) collective-permute-start(bf16[384,256]{1,0:T(8,128)(2,1)S(1)} %get-tuple-element.17), channel_id=1, source_target_pairs={{0,12},{2,14},{4,8},{6,10},{8,4},{10,6},{12,0},{14,2},{1,13},{3,15... | collective-permute-start | bytes 589832 | tf_op jit(solution)/shard_map/ppermute | solution.py:92
  20.7 10.5 %collective-permute-start.2 = (bf16[384,256]{1,0:T(8,128)(2,1)S(1)}, bf16[384,256]{1,0:T(8,128)(2,1)S(1)}, u32[]{:S(2)}, u32[]{:S(2)}) collective-permute-start(bf16[384,256]{1,0:T(8,128)(2,1)S(1)} %get-tuple-element.13), channel_id=1, source_target_pairs={{0,4},{2,6},{4,0},{6,2},{8,12},{10,14},{12,8},{14,10},{1,5},{3,7},... | collective-permute-start | bytes 589832 | tf_op jit(solution)/shard_map/ppermute | solution.py:91
  22.8 12.9 %collective-permute-start.1 = (bf16[384,256]{1,0:T(8,128)(2,1)S(1)}, bf16[384,256]{1,0:T(8,128)(2,1)S(1)}, u32[]{:S(2)}, u32[]{:S(2)}) collective-permute-start(bf16[384,256]{1,0:T(8,128)(2,1)S(1)} %get-tuple-element.11), channel_id=1, source_target_pairs={{0,4},{2,6},{4,0},{6,2},{8,12},{10,14},{12,8},{14,10},{1,5},{3,7},... | collective-permute-start | bytes 589832 | tf_op jit(solution)/shard_map/ppermute | solution.py:93
  26.5 9.2 %collective-permute-start.4 = (bf16[384,256]{1,0:T(8,128)(2,1)S(1)}, bf16[384,256]{1,0:T(8,128)(2,1)S(1)}, u32[]{:S(2)}, u32[]{:S(2)}) collective-permute-start(bf16[384,256]{1,0:T(8,128)(2,1)S(1)} %get-tuple-element.15), channel_id=1, source_target_pairs={{0,12},{2,14},{4,8},{6,10},{8,4},{10,6},{12,0},{14,2},{1,13},{3,15... | collective-permute-start | bytes 589832 | tf_op jit(solution)/shard_map/ppermute | solution.py:94
  29.0 8.7 %collective-permute-start.6 = (bf16[384,256]{1,0:T(8,128)(2,1)S(1)}, bf16[384,256]{1,0:T(8,128)(2,1)S(1)}, u32[]{:S(2)}, u32[]{:S(2)}) collective-permute-start(bf16[384,256]{1,0:T(8,128)(2,1)S(1)} %add_convert_fusion), channel_id=1, source_target_pairs={{0,4},{2,6},{4,0},{6,2},{8,12},{10,14},{12,8},{14,10},{1,5},{3,7},... | collective-permute-start | bytes 589832 | tf_op jit(solution)/shard_map/ppermute | solution.py:96
  31.3 8.8 %collective-permute-start.3 = (bf16[384,256]{1,0:T(8,128)(2,1)S(1)}, bf16[384,256]{1,0:T(8,128)(2,1)S(1)}, u32[]{:S(2)}, u32[]{:S(2)}) collective-permute-start(bf16[384,256]{1,0:T(8,128)(2,1)S(1)} %add_convert_fusion.1), channel_id=1, source_target_pairs={{0,12},{2,14},{4,8},{6,10},{8,4},{10,6},{12,0},{14,2},{1,13},{3,15... | collective-permute-start | bytes 589832 | tf_op jit(solution)/shard_map/ppermute | solution.py:95
  41.0 24.2 %all-to-all-start = ((bf16[32,8,768]{2,1,0:T(8,128)(2,1)}), bf16[32,8,768]{2,1,0:T(8,128)(2,1)S(1)}, u32[]{:S(2)}, u32[]{:S(2)}) async-start(bf16[32,8,768]{2,1,0:T(8,128)(2,1)} %bitcast.7), calls=%async_computation | async-start | bytes 786432 | tf_op jit(solution)/shard_map/all_to_all | solution.py:139
  69.3 12.2 %all-to-all-start.1 = ((bf16[4,8,4096]{2,1,0:T(8,128)(2,1)}), bf16[4,8,4096]{2,1,0:T(8,128)(2,1)S(1)}, u32[]{:S(2)}, u32[]{:S(2)}) async-start(bf16[4,8,4096]{2,1,0:T(8,128)(2,1)} %broadcast_in_dim.30), calls=%async_computation.1 | async-start | bytes 524288 | tf_op jit(solution)/shard_map/all_to_all | solution.py:114
  75.2 54.0 %all-gather.2.cloned.1.call-start = ((), (), s32[]{:S(2)}) async-start(), calls=%async_computation.3 | async-start | bytes 1179648 | tf_op jit(solution)/shard_map/all_gather | solution.py:136
  81.4 14.1 %collective-permute-start.7 = (bf16[32,4096]{1,0:T(8,128)(2,1)S(1)}, bf16[32,4096]{1,0:T(8,128)(2,1)S(1)}, u32[]{:S(2)}, u32[]{:S(2)}) collective-permute-start(bf16[32,4096]{1,0:T(8,128)(2,1)S(1)} %bitcast.60), channel_id=1, source_target_pairs={{0,64},{16,80},{32,96},{48,112},{64,0},{80,16},{96,32},{112,48},{1... | collective-permute-start | bytes 786440 | tf_op jit(solution)/shard_map/ppermute | solution.py:127
  84.0 9.5 %collective-permute-start.8 = (bf16[32,4096]{1,0:T(8,128)(2,1)S(1)}, bf16[32,4096]{1,0:T(8,128)(2,1)S(1)}, u32[]{:S(2)}, u32[]{:S(2)}) collective-permute-start(bf16[32,4096]{1,0:T(8,128)(2,1)S(1)} %bitcast.61), channel_id=1, source_target_pairs={{0,448},{16,464},{32,480},{48,496},{64,128},{80,144},{96,160},{112... | collective-permute-start | bytes 786440 | tf_op jit(solution)/shard_map/ppermute | solution.py:127
  93.4 14.8 %collective-permute-start.9 = (bf16[32,4096]{1,0:T(8,128)(2,1)S(1)}, bf16[32,4096]{1,0:T(8,128)(2,1)S(1)}, u32[]{:S(2)}, u32[]{:S(2)}) collective-permute-start(bf16[32,4096]{1,0:T(8,128)(2,1)S(1)} %collective-permute-done.8), channel_id=1, source_target_pairs={{0,64},{16,80},{32,96},{48,112},{64,0},{80,16},{96,32},{112,48},{1... | collective-permute-start | bytes 786440 | tf_op jit(solution)/shard_map/ppermute | solution.py:127
  95.6 9.6 %collective-permute-start.10 = (bf16[32,4096]{1,0:T(8,128)(2,1)S(1)}, bf16[32,4096]{1,0:T(8,128)(2,1)S(1)}, u32[]{:S(2)}, u32[]{:S(2)}) collective-permute-start(bf16[32,4096]{1,0:T(8,128)(2,1)S(1)} %collective-permute-done.7), channel_id=1, source_target_pairs={{0,448},{16,464},{32,480},{48,496},{64,128},{80,144},{96,160},{112... | collective-permute-start | bytes 786440 | tf_op jit(solution)/shard_map/ppermute | solution.py:127
  105.1 15.9 %collective-permute-start.11 = (bf16[32,4096]{1,0:T(8,128)(2,1)S(1)}, bf16[32,4096]{1,0:T(8,128)(2,1)S(1)}, u32[]{:S(2)}, u32[]{:S(2)}) collective-permute-start(bf16[32,4096]{1,0:T(8,128)(2,1)S(1)} %collective-permute-done.10), channel_id=1, source_target_pairs={{0,64},{16,80},{32,96},{48,112},{64,0},{80,16},{96,32},{112,48},{1... | collective-permute-start | bytes 786440 | tf_op jit(solution)/shard_map/ppermute | solution.py:127
  108.2 10.9 %collective-permute-start.12 = (bf16[32,4096]{1,0:T(8,128)(2,1)S(1)}, bf16[32,4096]{1,0:T(8,128)(2,1)S(1)}, u32[]{:S(2)}, u32[]{:S(2)}) collective-permute-start(bf16[32,4096]{1,0:T(8,128)(2,1)S(1)} %collective-permute-done.9), channel_id=1, source_target_pairs={{0,448},{16,464},{32,480},{48,496},{64,128},{80,144},{96,160},{112... | collective-permute-start | bytes 786440 | tf_op jit(solution)/shard_map/ppermute | solution.py:127
  119.1 6.9 %collective-permute-start.13 = (bf16[16,4096]{1,0:T(8,128)(2,1)S(1)}, bf16[16,4096]{1,0:T(8,128)(2,1)S(1)}, u32[]{:S(2)}, u32[]{:S(2)}) collective-permute-start(bf16[16,4096]{1,0:T(8,128)(2,1)S(1)} %slice.26), channel_id=1, source_target_pairs={{0,64},{16,80},{32,96},{48,112},{64,0},{80,16},{96,32},{112,48},{1... | collective-permute-start | bytes 393224 | tf_op jit(solution)/shard_map/ppermute | solution.py:129
  121.1 8.1 %collective-permute-start.14 = (bf16[16,4096]{1,0:T(8,128)(2,1)S(1)}, bf16[16,4096]{1,0:T(8,128)(2,1)S(1)}, u32[]{:S(2)}, u32[]{:S(2)}) collective-permute-start(bf16[16,4096]{1,0:T(8,128)(2,1)S(1)} %slice.27), channel_id=1, source_target_pairs={{0,448},{16,464},{32,480},{48,496},{64,128},{80,144},{96,160},{112... | collective-permute-start | bytes 393224 | tf_op jit(solution)/shard_map/ppermute | solution.py:129
  123.1 8.1 %copy-start.2 = (bf16[1,1,256,128]{3,2,1,0:T(8,128)(2,1)S(1)}, bf16[1,1,256,128]{3,2,1,0:T(8,128)(2,1)}, u32[]{:S(2)}) copy-start(bf16[1,1,256,128]{3,2,1,0:T(8,128)(2,1)} %param.13) | copy-start | bytes 196612
  132.0 3.8 %collective-permute-start.15 = (bf16[4,512,128]{2,1,0:T(8,128)(2,1)S(1)}, bf16[4,512,128]{2,1,0:T(8,128)(2,1)S(1)}, u32[]{:S(2)}, u32[]{:S(2)}) collective-permute-start(bf16[4,512,128]{2,1,0:T(8,128)(2,1)S(1)} %dynamic-slice_bitcast_fusion), channel_id=1, source_target_pairs={{0,2},{2,0},{4,6},{6,4},{8,10},{10,8},{12,14},{14,12},{1,3},{3,1},... | collective-permute-start | bytes 1572872 | tf_op jit(solution)/shard_map/ppermute | solution.py:169
  149.7 13.4 %collective-permute-start.16 = (bf16[512,128]{1,0:T(8,128)(2,1)S(1)}, bf16[512,128]{1,0:T(8,128)(2,1)S(1)}, u32[]{:S(2)}, u32[]{:S(2)}) collective-permute-start(bf16[512,128]{1,0:T(8,128)(2,1)S(1)} %fusion.8), channel_id=1, source_target_pairs={{0,1},{1,0},{2,3},{3,2},{4,5},{5,4},{6,7},{7,6},{8,9},{9,8},{10,11... | collective-permute-start | bytes 393224 | tf_op jit(solution)/shard_map/ppermute | solution.py:172
  (2 other events, 3.2 us)
Sparse Core Ops, SparseCore 0:
  78.2 26.1 all-gather.1

commit v6 on v5

--- a/solution.py
+++ b/solution.py
@@ -18,8 +18,17 @@
 CORE_SWAP = swaps(N_X * N_CORE, lambda h: h ^ 1)
 X_EVEN = swaps(N_X * N_CORE, lambda h: h ^ 2)
 X_ODD = swaps(N_X * N_CORE, lambda h: h ^ 6)
-Y_EVEN = swaps(N_Y * N_Z, lambda n: n ^ N_Z)
-Y_ODD = swaps(N_Y * N_Z, lambda n: (((n // N_Z + 1) ^ 1) - 1) % N_Y * N_Z + n % N_Z)
+DEVICES = N_Y * N_Z * N_X * N_CORE
+
+
+def y_partner(device, odd):
+    node, h = device // (N_X * N_CORE), device % (N_X * N_CORE)
+    y = ((node // N_Z + odd) ^ 1) - odd
+    return (y % N_Y * N_Z + node % N_Z) * N_X * N_CORE + h
+
+
+Y_FIRST = swaps(DEVICES, lambda i: y_partner(i, i % N_CORE))
+Y_SECOND = swaps(DEVICES, lambda i: y_partner(i, 1 - i % N_CORE))
 Z_GROUPS = [[N_Z * y + z for z in range(N_Z)] for y in range(N_Y)]
 X_GROUPS = [[N_CORE * x + c for x in range(N_X)] for c in range(N_CORE)]
 DP_SWAP = swaps(2, lambda d: d ^ 1)
@@ -109,25 +118,32 @@
     return (centered * lax.rsqrt(variance + 1e-05) * ln_gain).astype(jnp.bfloat16)
 
 
-def gather_nodes(block):
+def gather_nodes(block, early):
     copies = jnp.broadcast_to(block, (N_Z,) + block.shape)
     line = lax.all_to_all(copies, "node", 0, 0, axis_index_groups=Z_GROUPS, tiled=True)
     line = line.reshape(-1, block.shape[1])
-    rows, half = line.shape[0], line.shape[0] // 2
-    y = lax.axis_index("node") // N_Z
-    sign = 1 - 2 * (y % 2)
-
-    def put(group, part, distance, first_row=0):
-        place = (y + sign * distance) % N_Y * rows + first_row
-        return lax.dynamic_update_slice(group, part, (place, 0))
-
-    even = odd = line
+    rows = line.shape[0]
+    y, core = lax.axis_index("node") // N_Z, lax.axis_index("hst") % N_CORE
+    sign = (1 - 2 * (y % 2)) * (1 - 2 * core)
+
+    def put(group, part, distance):
+        return lax.dynamic_update_slice(group, part, ((y + sign * distance) % N_Y * rows, 0))
+
     group = put(jnp.zeros((N_Y * rows, line.shape[1]), line.dtype), line, 0)
-    for distance in range(1, N_Y // 2):
-        even, odd = lax.ppermute(odd, "node", Y_EVEN), lax.ppermute(even, "node", Y_ODD)
-        group = put(put(group, even, distance), odd, -distance)
-    even, odd = lax.ppermute(odd[:half], "node", Y_EVEN), lax.ppermute(even[half:], "node", Y_ODD)
-    return put(put(group, even, N_Y // 2), odd, N_Y // 2, half)
+    both = jnp.concatenate([line, lax.ppermute(line, "hst", CORE_SWAP)], 0)
+    handed = []
+    for step in range(1, N_Y // 2):
+        both = lax.ppermute(both, ("node", "hst"), Y_FIRST if step % 2 else Y_SECOND)
+        group = put(group, both[:rows], step if step % 2 else -step)
+        handed.append(both[rows:])
+        if step == 1:
+            both, early = lax.optimization_barrier((both, early))
+    last = lax.ppermute(both[:rows], ("node", "hst"), Y_SECOND)
+    handed = lax.ppermute(jnp.concatenate(handed, 0), "hst", CORE_SWAP)
+    for step in range(1, N_Y // 2):
+        part = handed[(step - 1) * rows : step * rows]
+        group = put(group, part, -step if step % 2 else step)
+    return put(group, last, N_Y // 2), early
 
 
 def local(partials, counts, perm, fm_proj, ln_gain, w_in, d_hidden):
@@ -152,7 +168,7 @@
     pairwise = jnp.einsum("sfe,sek->sfk", pooled, projected, preferred_element_type=jnp.float32)
     z_local = normalize(pairwise.reshape(samples, -1), ln_gain)
 
-    z_group = gather_nodes(z_local)
+    z_group, w_full = gather_nodes(z_local, w_full)
     pre_act = jnp.dot(z_group, w_full, preferred_element_type=jnp.float32)
     sigma = jax.nn.sigmoid(pre_act)
     hidden = (pre_act * sigma).astype(jnp.bfloat16)

time: 172 us -> 180 us (1.047)
  the two profiles are of different devices: /device:TPU:64 before, /device:TPU:56 now
where the time goes in v6:
time: 180 us; the launch traced here: 179 us
  waiting for transfers between devices  73.9 us (41%)
  starting transfers between devices  61.4 us (34%)
  between operations  14.7 us (8%)
  blocking collectives  12.5 us (7%)
  local copies, waits for them, and re-layouts  8.4 us (5%)
  other arithmetic  3.1 us (2%)
  Pallas kernels  2.57 us (1%)
  matrix products  2.09 us (1%)
    ppermute x3, waiting for transfers between devices, gather_nodes(): lax.ppermute(both, ('node', 'hst'), Y_FIRST if step % 2 else Y_SECOND)  18.8 us
    all_gather x1, waiting for transfers between devices, local(): w_full = lax.all_gather(w_in, 'hst', axis=0, tiled=True)  18.6 us
    all_to_all x1, starting transfers between devices, local(): lax.all_to_all(summed.reshape(N_Y * N_Z, samples, rows), 'node', split_ax...  12.5 us
    all_to_all x1, blocking collectives, local(): lax.all_to_all(pair, 'hst', 0, 0, axis_index_groups=X_GROUPS, tiled=True)  12.5 us
    all_to_all x1, waiting for transfers between devices, local(): lax.all_to_all(summed.reshape(N_Y * N_Z, samples, rows), 'node', split_ax...  10.8 us
    ppermute x1, starting transfers between devices, local(): grad_w = add(share, lax.ppermute(share, 'dp', DP_SWAP))  8.01 us
    ppermute x3, starting transfers between devices, gather_nodes(): lax.ppermute(both, ('node', 'hst'), Y_FIRST if step % 2 else Y_SECOND)  7.94 us
    all_to_all x1, waiting for transfers between devices, gather_nodes(): lax.all_to_all(copies, 'node', 0, 0, axis_index_groups=Z_GROUPS, tiled=True)  6 us
  transfers between devices with their start and end apart: 18, of which 14 were waited for; matrix products, arithmetic and copies ran while one was open for 2% of the time, Pallas kernels for 0%

profile of v6, /device:TPU:56, one launch (start us, length us, event | category | flops | bytes accessed | tf_op | source)
XLA Modules:
  0.0 178.6 jit_solution(10980150212687904925)
XLA Ops:
  9.5 1.9 %collective-permute-start = (bf16[3072,256]{1,0:T(8,128)(2,1)S(1)}, bf16[3072,256]{1,0:T(8,128)(2,1)S(1)}, u32[]{:S(2)}, u32[]{:S(2)}) collective-permute-start(bf16[3072,256]{1,0:T(8,128)(2,1)S(1)} %pack.1), channel_id=1, source_target_pairs={{0,2},{2,0},{4,6},{6,4},{8,10},{10,8},{12,14},{14,12},{1,3},{3,1},... | collective-permute-start | bytes 4718600 | tf_op jit(solution)/shard_map/ppermute | solution.py:85
  11.5 3.4 %collective-permute-done.got_ref = bf16[3072,256]{1,0:T(8,128)(2,1)S(1)} collective-permute-done((bf16[3072,256]{1,0:T(8,128)(2,1)S(1)}, bf16[3072,256]{1,0:T(8,128)(2,1)S(1)}, u32[]{:S(2)}, u32[]{:S(2)}) %collective-permute-start) | collective-permute-done | bytes 1572896 | tf_op jit(solution)/shard_map/ppermute | solution.py:85
  16.0 4.7 %collective-permute-start.5 = (bf16[384,256]{1,0:T(8,128)(2,1)S(1)}, bf16[384,256]{1,0:T(8,128)(2,1)S(1)}, u32[]{:S(2)}, u32[]{:S(2)}) collective-permute-start(bf16[384,256]{1,0:T(8,128)(2,1)S(1)} %get-tuple-element.19), channel_id=1, source_target_pairs={{0,12},{2,14},{4,8},{6,10},{8,4},{10,6},{12,0},{14,2},{1,13},{3,15... | collective-permute-start | bytes 589832 | tf_op jit(solution)/shard_map/ppermute | solution.py:101
  20.7 2.1 %collective-permute-start.2 = (bf16[384,256]{1,0:T(8,128)(2,1)S(1)}, bf16[384,256]{1,0:T(8,128)(2,1)S(1)}, u32[]{:S(2)}, u32[]{:S(2)}) collective-permute-start(bf16[384,256]{1,0:T(8,128)(2,1)S(1)} %get-tuple-element.15), channel_id=1, source_target_pairs={{0,4},{2,6},{4,0},{6,2},{8,12},{10,14},{12,8},{14,10},{1,5},{3,7},... | collective-permute-start | bytes 589832 | tf_op jit(solution)/shard_map/ppermute | solution.py:100
  22.8 3.7 %collective-permute-start.1 = (bf16[384,256]{1,0:T(8,128)(2,1)S(1)}, bf16[384,256]{1,0:T(8,128)(2,1)S(1)}, u32[]{:S(2)}, u32[]{:S(2)}) collective-permute-start(bf16[384,256]{1,0:T(8,128)(2,1)S(1)} %get-tuple-element.13), channel_id=1, source_target_pairs={{0,4},{2,6},{4,0},{6,2},{8,12},{10,14},{12,8},{14,10},{1,5},{3,7},... | collective-permute-start | bytes 589832 | tf_op jit(solution)/shard_map/ppermute | solution.py:102
  26.5 2.4 %collective-permute-start.4 = (bf16[384,256]{1,0:T(8,128)(2,1)S(1)}, bf16[384,256]{1,0:T(8,128)(2,1)S(1)}, u32[]{:S(2)}, u32[]{:S(2)}) collective-permute-start(bf16[384,256]{1,0:T(8,128)(2,1)S(1)} %get-tuple-element.17), channel_id=1, source_target_pairs={{0,12},{2,14},{4,8},{6,10},{8,4},{10,6},{12,0},{14,2},{1,13},{3,15... | collective-permute-start | bytes 589832 | tf_op jit(solution)/shard_map/ppermute | solution.py:103
  29.0 2.2 %collective-permute-start.6 = (bf16[384,256]{1,0:T(8,128)(2,1)S(1)}, bf16[384,256]{1,0:T(8,128)(2,1)S(1)}, u32[]{:S(2)}, u32[]{:S(2)}) collective-permute-start(bf16[384,256]{1,0:T(8,128)(2,1)S(1)} %add_convert_fusion), channel_id=1, source_target_pairs={{0,4},{2,6},{4,0},{6,2},{8,12},{10,14},{12,8},{14,10},{1,5},{3,7},... | collective-permute-start | bytes 589832 | tf_op jit(solution)/shard_map/ppermute | solution.py:105
  31.3 4.4 %collective-permute-start.3 = (bf16[384,256]{1,0:T(8,128)(2,1)S(1)}, bf16[384,256]{1,0:T(8,128)(2,1)S(1)}, u32[]{:S(2)}, u32[]{:S(2)}) collective-permute-start(bf16[384,256]{1,0:T(8,128)(2,1)S(1)} %add_convert_fusion.1), channel_id=1, source_target_pairs={{0,12},{2,14},{4,8},{6,10},{8,4},{10,6},{12,0},{14,2},{1,13},{3,15... | collective-permute-start | bytes 589832 | tf_op jit(solution)/shard_map/ppermute | solution.py:104
  37.7 2.4 %collective-permute-done.3.refs_2_ = bf16[384,256]{1,0:T(8,128)(2,1)S(1)} collective-permute-done((bf16[384,256]{1,0:T(8,128)(2,1)S(1)}, bf16[384,256]{1,0:T(8,128)(2,1)S(1)}, u32[]{:S(2)}, u32[]{:S(2)}) %collective-permute-start.3) | collective-permute-done | bytes 196640 | tf_op jit(solution)/shard_map/ppermute | solution.py:104
  41.0 12.5 %all-to-all-start = ((bf16[32,8,768]{2,1,0:T(8,128)(2,1)}), bf16[32,8,768]{2,1,0:T(8,128)(2,1)S(1)}, u32[]{:S(2)}, u32[]{:S(2)}) async-start(bf16[32,8,768]{2,1,0:T(8,128)(2,1)} %bitcast.7), calls=%async_computation | async-start | bytes 786432 | tf_op jit(solution)/shard_map/all_to_all | solution.py:155
  53.6 10.8 %all-to-all-done = bf16[32,8,768]{2,1,0:T(8,128)(2,1)S(1)} async-done(((bf16[32,8,768]{2,1,0:T(8,128)(2,1)}), bf16[32,8,768]{2,1,0:T(8,128)(2,1)S(1)}, u32[]{:S(2)}, u32[]{:S(2)}) %all-to-all-start) | async-done | bytes 393248 | tf_op jit(solution)/shard_map/all_to_all | solution.py:155
  68.5 3.4 %all-to-all-start.1 = ((bf16[4,8,4096]{2,1,0:T(8,128)(2,1)}), bf16[4,8,4096]{2,1,0:T(8,128)(2,1)S(1)}, u32[]{:S(2)}, u32[]{:S(2)}) async-start(bf16[4,8,4096]{2,1,0:T(8,128)(2,1)} %broadcast_in_dim.30), calls=%async_computation.1 | async-start | bytes 524288 | tf_op jit(solution)/shard_map/all_to_all | solution.py:123
  72.7 6.0 %all-to-all-done.1 = bf16[4,8,4096]{2,1,0:T(8,128)(2,1)S(1)} async-done(((bf16[4,8,4096]{2,1,0:T(8,128)(2,1)}), bf16[4,8,4096]{2,1,0:T(8,128)(2,1)S(1)}, u32[]{:S(2)}, u32[]{:S(2)}) %all-to-all-start.1) | async-done | bytes 262176 | tf_op jit(solution)/shard_map/all_to_all | solution.py:123
  82.1 3.5 %collective-permute-start.8 = (bf16[64,4096]{1,0:T(8,128)(2,1)S(1)}, bf16[64,4096]{1,0:T(8,128)(2,1)S(1)}, u32[]{:S(2)}, u32[]{:S(2)}) collective-permute-start(bf16[64,4096]{1,0:T(8,128)(2,1)S(1)} %pad_maximum_fusion.1), channel_id=1, source_target_pairs={{0,64},{2,450},{4,68},{6,454},{8,72},{10,458},{12,76},{14,462},{16... | collective-permute-start | bytes 1572872 | tf_op jit(solution)/shard_map/ppermute | solution.py:136
  85.9 18.6 %all-gather.2.cloned.1.call-done = bf16[4096,128]{1,0:T(8,128)(2,1)} async-done(((bf16[512,128]{1,0:T(8,128)(2,1)}), bf16[4096,128]{1,0:T(8,128)(2,1)}) %all-gather.2.cloned.1.call-update) | async-done | bytes 1048592 | tf_op jit(solution)/shard_map/all_gather | solution.py:152
  104.5 2.3 %collective-permute-start.9 = (bf16[64,4096]{1,0:T(8,128)(2,1)S(1)}, bf16[64,4096]{1,0:T(8,128)(2,1)S(1)}, u32[]{:S(2)}, u32[]{:S(2)}) collective-permute-start(bf16[64,4096]{1,0:T(8,128)(2,1)S(1)} %collective-permute-done.8), channel_id=1, source_target_pairs={{0,448},{2,66},{4,452},{6,70},{8,456},{10,74},{12,460},{14,78},{16... | collective-permute-start | bytes 1572872 | tf_op jit(solution)/shard_map/ppermute | solution.py:136
  106.9 9.9 %collective-permute-done.9 = bf16[64,4096]{1,0:T(8,128)(2,1)S(1)} collective-permute-done((bf16[64,4096]{1,0:T(8,128)(2,1)S(1)}, bf16[64,4096]{1,0:T(8,128)(2,1)S(1)}, u32[]{:S(2)}, u32[]{:S(2)}) %collective-permute-start.9) | collective-permute-done | bytes 524320 | tf_op jit(solution)/shard_map/ppermute | solution.py:136
  116.8 2.1 %collective-permute-start.10 = (bf16[64,4096]{1,0:T(8,128)(2,1)S(1)}, bf16[64,4096]{1,0:T(8,128)(2,1)S(1)}, u32[]{:S(2)}, u32[]{:S(2)}) collective-permute-start(bf16[64,4096]{1,0:T(8,128)(2,1)S(1)} %collective-permute-done.9), channel_id=1, source_target_pairs={{0,64},{2,450},{4,68},{6,454},{8,72},{10,458},{12,76},{14,462},{16... | collective-permute-start | bytes 1572872 | tf_op jit(solution)/shard_map/ppermute | solution.py:136
  119.0 8.9 %collective-permute-done.10 = bf16[64,4096]{1,0:T(8,128)(2,1)S(1)} collective-permute-done((bf16[64,4096]{1,0:T(8,128)(2,1)S(1)}, bf16[64,4096]{1,0:T(8,128)(2,1)S(1)}, u32[]{:S(2)}, u32[]{:S(2)}) %collective-permute-start.10) | collective-permute-done | bytes 524320 | tf_op jit(solution)/shard_map/ppermute | solution.py:136
  130.9 2.3 %collective-permute-start.12 = (bf16[32,4096]{1,0:T(8,128)(2,1)S(1)}, bf16[32,4096]{1,0:T(8,128)(2,1)S(1)}, u32[]{:S(2)}, u32[]{:S(2)}) collective-permute-start(bf16[32,4096]{1,0:T(8,128)(2,1)S(1)} %get-tuple-element.22), channel_id=1, source_target_pairs={{0,448},{2,66},{4,452},{6,70},{8,456},{10,74},{12,460},{14,78},{16... | collective-permute-start | bytes 786440 | tf_op jit(solution)/shard_map/ppermute | solution.py:141
  136.4 4.0 %collective-permute-done.12 = bf16[32,4096]{1,0:T(8,128)(2,1)S(1)} collective-permute-done((bf16[32,4096]{1,0:T(8,128)(2,1)S(1)}, bf16[32,4096]{1,0:T(8,128)(2,1)S(1)}, u32[]{:S(2)}, u32[]{:S(2)}) %collective-permute-start.12) | collective-permute-done | bytes 262176 | tf_op jit(solution)/shard_map/ppermute | solution.py:141
  145.9 12.5 %all_to_all.15 = bf16[4,512,128]{2,1,0:T(8,128)(2,1)S(1)} all-to-all(bf16[4,512,128]{2,1,0:T(8,128)(2,1)S(1)} %fusion.1), channel_id=1, replica_groups={{0,4,8,12},{2,6,10,14},{1,5,9,13},{3,7,11,15},{16,20,24,28},{18,22,26,3..., dimensions={0} | all-to-all | bytes 1048576 | tf_op jit(solution)/shard_map/all_to_all | solution.py:186
  158.4 8.0 %collective-permute-start.14 = (bf16[512,128]{1,0:T(8,128)(2,1)S(1)}, bf16[512,128]{1,0:T(8,128)(2,1)S(1)}, u32[]{:S(2)}, u32[]{:S(2)}) collective-permute-start(bf16[512,128]{1,0:T(8,128)(2,1)S(1)} %fusion.8), channel_id=1, source_target_pairs={{0,1},{1,0},{2,3},{3,2},{4,5},{5,4},{6,7},{7,6},{8,9},{9,8},{10,11... | collective-permute-start | bytes 393224 | tf_op jit(solution)/shard_map/ppermute | solution.py:188
  167.1 3.9 %collective-permute-done.14 = bf16[512,128]{1,0:T(8,128)(2,1)S(1)} collective-permute-done((bf16[512,128]{1,0:T(8,128)(2,1)S(1)}, bf16[512,128]{1,0:T(8,128)(2,1)S(1)}, u32[]{:S(2)}, u32[]{:S(2)}) %collective-permute-start.14) | collective-permute-done | bytes 131104 | tf_op jit(solution)/shard_map/ppermute | solution.py:188
  (67 shorter events, 28.0 us)
Async XLA Ops:
  7.2 59.2 %copy-start = (bf16[128,32]{0,1:T(8,128)(2,1)S(1)}, bf16[128,32]{0,1:T(8,128)(2,1)}, u32[]{:S(2)}) copy-start(bf16[128,32]{0,1:T(8,128)(2,1)} %param.10) | copy-start | bytes 24580
  7.2 1.9 %copy-start.1 = (bf16[1,2048,4,192]{1,3,2,0:T(8,128)(2,1)S(1)}, bf16[1,2048,4,192]{1,3,2,0:T(8,128)(2,1)}, u32[]{:S(2)}) copy-start(bf16[1,2048,4,192]{1,3,2,0:T(8,128)(2,1)} %param.7) | copy-start | bytes 9437188
  9.5 5.3 %collective-permute-start = (bf16[3072,256]{1,0:T(8,128)(2,1)S(1)}, bf16[3072,256]{1,0:T(8,128)(2,1)S(1)}, u32[]{:S(2)}, u32[]{:S(2)}) collective-permute-start(bf16[3072,256]{1,0:T(8,128)(2,1)S(1)} %pack.1), channel_id=1, source_target_pairs={{0,2},{2,0},{4,6},{6,4},{8,10},{10,8},{12,14},{14,12},{1,3},{3,1},... | collective-permute-start | bytes 4718600 | tf_op jit(solution)/shard_map/ppermute | solution.py:85
  16.0 37.6 %copy-start.6 = (s32[128]{0:T(128)S(1)}, s32[128]{0:T(128)}, u32[]{:S(2)}) copy-start(s32[128]{0:T(128)} %param.9) | copy-start | bytes 1540
  16.0 37.6 %copy-start.4 = (s32[1,1,8,128]{3,2,1,0:T(8,128)S(1)}, s32[1,1,8,128]{3,2,1,0:T(8,128)}, u32[]{:S(2)}) copy-start(s32[1,1,8,128]{3,2,1,0:T(8,128)} %param.8) | copy-start | bytes 12292
  16.0 12.9 %collective-permute-start.5 = (bf16[384,256]{1,0:T(8,128)(2,1)S(1)}, bf16[384,256]{1,0:T(8,128)(2,1)S(1)}, u32[]{:S(2)}, u32[]{:S(2)}) collective-permute-start(bf16[384,256]{1,0:T(8,128)(2,1)S(1)} %get-tuple-element.19), channel_id=1, source_target_pairs={{0,12},{2,14},{4,8},{6,10},{8,4},{10,6},{12,0},{14,2},{1,13},{3,15... | collective-permute-start | bytes 589832 | tf_op jit(solution)/shard_map/ppermute | solution.py:101
  20.7 10.5 %collective-permute-start.2 = (bf16[384,256]{1,0:T(8,128)(2,1)S(1)}, bf16[384,256]{1,0:T(8,128)(2,1)S(1)}, u32[]{:S(2)}, u32[]{:S(2)}) collective-permute-start(bf16[384,256]{1,0:T(8,128)(2,1)S(1)} %get-tuple-element.15), channel_id=1, source_target_pairs={{0,4},{2,6},{4,0},{6,2},{8,12},{10,14},{12,8},{14,10},{1,5},{3,7},... | collective-permute-start | bytes 589832 | tf_op jit(solution)/shard_map/ppermute | solution.py:100
  22.8 12.9 %collective-permute-start.1 = (bf16[384,256]{1,0:T(8,128)(2,1)S(1)}, bf16[384,256]{1,0:T(8,128)(2,1)S(1)}, u32[]{:S(2)}, u32[]{:S(2)}) collective-permute-start(bf16[384,256]{1,0:T(8,128)(2,1)S(1)} %get-tuple-element.13), channel_id=1, source_target_pairs={{0,4},{2,6},{4,0},{6,2},{8,12},{10,14},{12,8},{14,10},{1,5},{3,7},... | collective-permute-start | bytes 589832 | tf_op jit(solution)/shard_map/ppermute | solution.py:102
  26.5 9.2 %collective-permute-start.4 = (bf16[384,256]{1,0:T(8,128)(2,1)S(1)}, bf16[384,256]{1,0:T(8,128)(2,1)S(1)}, u32[]{:S(2)}, u32[]{:S(2)}) collective-permute-start(bf16[384,256]{1,0:T(8,128)(2,1)S(1)} %get-tuple-element.17), channel_id=1, source_target_pairs={{0,12},{2,14},{4,8},{6,10},{8,4},{10,6},{12,0},{14,2},{1,13},{3,15... | collective-permute-start | bytes 589832 | tf_op jit(solution)/shard_map/ppermute | solution.py:103
  29.0 8.7 %collective-permute-start.6 = (bf16[384,256]{1,0:T(8,128)(2,1)S(1)}, bf16[384,256]{1,0:T(8,128)(2,1)S(1)}, u32[]{:S(2)}, u32[]{:S(2)}) collective-permute-start(bf16[384,256]{1,0:T(8,128)(2,1)S(1)} %add_convert_fusion), channel_id=1, source_target_pairs={{0,4},{2,6},{4,0},{6,2},{8,12},{10,14},{12,8},{14,10},{1,5},{3,7},... | collective-permute-start | bytes 589832 | tf_op jit(solution)/shard_map/ppermute | solution.py:105
  31.3 8.8 %collective-permute-start.3 = (bf16[384,256]{1,0:T(8,128)(2,1)S(1)}, bf16[384,256]{1,0:T(8,128)(2,1)S(1)}, u32[]{:S(2)}, u32[]{:S(2)}) collective-permute-start(bf16[384,256]{1,0:T(8,128)(2,1)S(1)} %add_convert_fusion.1), channel_id=1, source_target_pairs={{0,12},{2,14},{4,8},{6,10},{8,4},{10,6},{12,0},{14,2},{1,13},{3,15... | collective-permute-start | bytes 589832 | tf_op jit(solution)/shard_map/ppermute | solution.py:104
  41.0 23.4 %all-to-all-start = ((bf16[32,8,768]{2,1,0:T(8,128)(2,1)}), bf16[32,8,768]{2,1,0:T(8,128)(2,1)S(1)}, u32[]{:S(2)}, u32[]{:S(2)}) async-start(bf16[32,8,768]{2,1,0:T(8,128)(2,1)} %bitcast.7), calls=%async_computation | async-start | bytes 786432 | tf_op jit(solution)/shard_map/all_to_all | solution.py:155
  68.5 10.2 %all-to-all-start.1 = ((bf16[4,8,4096]{2,1,0:T(8,128)(2,1)}), bf16[4,8,4096]{2,1,0:T(8,128)(2,1)S(1)}, u32[]{:S(2)}, u32[]{:S(2)}) async-start(bf16[4,8,4096]{2,1,0:T(8,128)(2,1)} %broadcast_in_dim.30), calls=%async_computation.1 | async-start | bytes 524288 | tf_op jit(solution)/shard_map/all_to_all | solution.py:123
  71.9 32.6 %all-gather.2.cloned.1.call-start = ((), (), s32[]{:S(2)}) async-start(), calls=%async_computation.3 | async-start | bytes 1179648 | tf_op jit(solution)/shard_map/all_gather | solution.py:152
  78.7 3.4 %collective-permute-start.7 = (bf16[32,4096]{1,0:T(8,128)(2,1)S(1)}, bf16[32,4096]{1,0:T(8,128)(2,1)S(1)}, u32[]{:S(2)}, u32[]{:S(2)}) collective-permute-start(bf16[32,4096]{1,0:T(8,128)(2,1)S(1)} %bitcast.59), channel_id=1, source_target_pairs={{0,2},{2,0},{4,6},{6,4},{8,10},{10,8},{12,14},{14,12},{1,3},{3,1},... | collective-permute-start | bytes 786440 | tf_op jit(solution)/shard_map/ppermute | solution.py:133
  82.1 22.4 %collective-permute-start.8 = (bf16[64,4096]{1,0:T(8,128)(2,1)S(1)}, bf16[64,4096]{1,0:T(8,128)(2,1)S(1)}, u32[]{:S(2)}, u32[]{:S(2)}) collective-permute-start(bf16[64,4096]{1,0:T(8,128)(2,1)S(1)} %pad_maximum_fusion.1), channel_id=1, source_target_pairs={{0,64},{2,450},{4,68},{6,454},{8,72},{10,458},{12,76},{14,462},{16... | collective-permute-start | bytes 1572872 | tf_op jit(solution)/shard_map/ppermute | solution.py:136
  104.5 12.3 %collective-permute-start.9 = (bf16[64,4096]{1,0:T(8,128)(2,1)S(1)}, bf16[64,4096]{1,0:T(8,128)(2,1)S(1)}, u32[]{:S(2)}, u32[]{:S(2)}) collective-permute-start(bf16[64,4096]{1,0:T(8,128)(2,1)S(1)} %collective-permute-done.8), channel_id=1, source_target_pairs={{0,448},{2,66},{4,452},{6,70},{8,456},{10,74},{12,460},{14,78},{16... | collective-permute-start | bytes 1572872 | tf_op jit(solution)/shard_map/ppermute | solution.py:136
  116.8 11.1 %collective-permute-start.10 = (bf16[64,4096]{1,0:T(8,128)(2,1)S(1)}, bf16[64,4096]{1,0:T(8,128)(2,1)S(1)}, u32[]{:S(2)}, u32[]{:S(2)}) collective-permute-start(bf16[64,4096]{1,0:T(8,128)(2,1)S(1)} %collective-permute-done.9), channel_id=1, source_target_pairs={{0,64},{2,450},{4,68},{6,454},{8,72},{10,458},{12,76},{14,462},{16... | collective-permute-start | bytes 1572872 | tf_op jit(solution)/shard_map/ppermute | solution.py:136
  127.9 12.5 %copy-start.2 = (bf16[4096,128]{1,0:T(8,128)(2,1)S(1)}, bf16[4096,128]{1,0:T(8,128)(2,1)}, u32[]{:S(2)}) copy-start(bf16[4096,128]{1,0:T(8,128)(2,1)} %all-gather.2.cloned.1.call-done) | copy-start | bytes 3145732
  128.9 4.5 %collective-permute-start.11 = (bf16[96,4096]{1,0:T(8,128)(2,1)}, bf16[96,4096]{1,0:T(8,128)(2,1)}, u32[]{:S(2)}, u32[]{:S(2)}) collective-permute-start(bf16[96,4096]{1,0:T(8,128)(2,1)} %pad_maximum_fusion), channel_id=1, source_target_pairs={{0,2},{2,0},{4,6},{6,4},{8,10},{10,8},{12,14},{14,12},{1,3},{3,1},... | collective-permute-start | bytes 2359304 | tf_op jit(solution)/shard_map/ppermute | solution.py:142
  130.9 9.5 %collective-permute-start.12 = (bf16[32,4096]{1,0:T(8,128)(2,1)S(1)}, bf16[32,4096]{1,0:T(8,128)(2,1)S(1)}, u32[]{:S(2)}, u32[]{:S(2)}) collective-permute-start(bf16[32,4096]{1,0:T(8,128)(2,1)S(1)} %get-tuple-element.22), channel_id=1, source_target_pairs={{0,448},{2,66},{4,452},{6,70},{8,456},{10,74},{12,460},{14,78},{16... | collective-permute-start | bytes 786440 | tf_op jit(solution)/shard_map/ppermute | solution.py:141
  135.3 5.8 %copy-start.3 = (bf16[1,1,256,128]{3,2,1,0:T(8,128)(2,1)S(1)}, bf16[1,1,256,128]{3,2,1,0:T(8,128)(2,1)}, u32[]{:S(2)}) copy-start(bf16[1,1,256,128]{3,2,1,0:T(8,128)(2,1)} %param.13) | copy-start | bytes 196612
  142.0 3.8 %collective-permute-start.13 = (bf16[4,512,128]{2,1,0:T(8,128)(2,1)S(1)}, bf16[4,512,128]{2,1,0:T(8,128)(2,1)S(1)}, u32[]{:S(2)}, u32[]{:S(2)}) collective-permute-start(bf16[4,512,128]{2,1,0:T(8,128)(2,1)S(1)} %dynamic-slice_bitcast_fusion), channel_id=1, source_target_pairs={{0,2},{2,0},{4,6},{6,4},{8,10},{10,8},{12,14},{14,12},{1,3},{3,1},... | collective-permute-start | bytes 1572872 | tf_op jit(solution)/shard_map/ppermute | solution.py:185
  158.4 12.5 %collective-permute-start.14 = (bf16[512,128]{1,0:T(8,128)(2,1)S(1)}, bf16[512,128]{1,0:T(8,128)(2,1)S(1)}, u32[]{:S(2)}, u32[]{:S(2)}) collective-permute-start(bf16[512,128]{1,0:T(8,128)(2,1)S(1)} %fusion.8), channel_id=1, source_target_pairs={{0,1},{1,0},{2,3},{3,2},{4,5},{5,4},{6,7},{7,6},{8,9},{9,8},{10,11... | collective-permute-start | bytes 393224 | tf_op jit(solution)/shard_map/ppermute | solution.py:188
  (1 other events, 1.3 us)
Sparse Core Ops, SparseCore 0:
  74.9 29.5 all-gather.1

commit v7 on v5

--- a/solution.py
+++ b/solution.py
@@ -121,13 +121,18 @@
         place = (y + sign * distance) % N_Y * rows + first_row
         return lax.dynamic_update_slice(group, part, (place, 0))
 
-    even = odd = line
     group = put(jnp.zeros((N_Y * rows, line.shape[1]), line.dtype), line, 0)
-    for distance in range(1, N_Y // 2):
-        even, odd = lax.ppermute(odd, "node", Y_EVEN), lax.ppermute(even, "node", Y_ODD)
-        group = put(put(group, even, distance), odd, -distance)
-    even, odd = lax.ppermute(odd[:half], "node", Y_EVEN), lax.ppermute(even[half:], "node", Y_ODD)
-    return put(put(group, even, N_Y // 2), odd, N_Y // 2, half)
+    pairs = (Y_EVEN, Y_ODD)
+    lead = lax.ppermute(line, "node", pairs[0])
+    trail = lax.ppermute(line, "node", pairs[1])
+    for step in range(1, N_Y // 2):
+        pairs = pairs[::-1]
+        way = step if step % 2 else -step
+        group = put(put(group, lead, way), trail, -way)
+        if step == N_Y // 2 - 1:
+            lead, trail = lead[half:], trail[:half]
+        lead, trail = lax.ppermute(lead, "node", pairs[0]), lax.ppermute(trail, "node", pairs[1])
+    return put(put(group, lead, N_Y // 2, half), trail, N_Y // 2)
 
 
 def local(partials, counts, perm, fm_proj, ln_gain, w_in, d_hidden):

time: 172 us -> 162 us (0.942)
  the two profiles are of different devices: /device:TPU:64 before, /device:TPU:96 now
where the time goes in v7:
time: 162 us; the launch traced here: 161 us
  starting transfers between devices  73.6 us (45%)
  waiting for transfers between devices  44.9 us (28%)
  between operations  14.7 us (9%)
  blocking collectives  14 us (9%)
  local copies, waits for them, and re-layouts  5.49 us (3%)
  matrix products  3.33 us (2%)
  Pallas kernels  2.56 us (2%)
  other arithmetic  2.12 us (1%)
    all_to_all x1, blocking collectives, local(): lax.all_to_all(pair, 'hst', 0, 0, axis_index_groups=X_GROUPS, tiled=True)  14 us
    ppermute x3, waiting for transfers between devices, gather_nodes(): lax.ppermute(trail, 'node', pairs[1])  12.1 us
    all_to_all x1, starting transfers between devices, local(): lax.all_to_all(summed.reshape(N_Y * N_Z, samples, rows), 'node', split_ax...  11.9 us
    ppermute x3, starting transfers between devices, gather_nodes(): lax.ppermute(lead, 'node', pairs[0])  11.3 us
    ppermute x1, starting transfers between devices, local(): grad_w = add(share, lax.ppermute(share, 'dp', DP_SWAP))  8.25 us
    all_to_all x1, waiting for transfers between devices, local(): lax.all_to_all(summed.reshape(N_Y * N_Z, samples, rows), 'node', split_ax...  8.25 us
    ppermute x3, starting transfers between devices, gather_nodes(): lax.ppermute(trail, 'node', pairs[1])  5.74 us
    all_to_all x1, waiting for transfers between devices, gather_nodes(): lax.all_to_all(copies, 'node', 0, 0, axis_index_groups=Z_GROUPS, tiled=True)  5.37 us
  transfers between devices with their start and end apart: 20, of which 15 were waited for; matrix products, arithmetic and copies ran while one was open for 1% of the time, Pallas kernels for 0%

profile of v7, /device:TPU:96, one launch (start us, length us, event | category | flops | bytes accessed | tf_op | source)
XLA Modules:
  0.0 160.7 jit_solution(1053449046534644668)
XLA Ops:
  11.5 3.4 %collective-permute-done.got_ref = bf16[3072,256]{1,0:T(8,128)(2,1)S(1)} collective-permute-done((bf16[3072,256]{1,0:T(8,128)(2,1)S(1)}, bf16[3072,256]{1,0:T(8,128)(2,1)S(1)}, u32[]{:S(2)}, u32[]{:S(2)}) %collective-permute-start) | collective-permute-done | bytes 1572896 | tf_op jit(solution)/shard_map/ppermute | solution.py:76
  16.0 4.7 %collective-permute-start.5 = (bf16[384,256]{1,0:T(8,128)(2,1)S(1)}, bf16[384,256]{1,0:T(8,128)(2,1)S(1)}, u32[]{:S(2)}, u32[]{:S(2)}) collective-permute-start(bf16[384,256]{1,0:T(8,128)(2,1)S(1)} %get-tuple-element.17), channel_id=1, source_target_pairs={{0,12},{2,14},{4,8},{6,10},{8,4},{10,6},{12,0},{14,2},{1,13},{3,15... | collective-permute-start | bytes 589832 | tf_op jit(solution)/shard_map/ppermute | solution.py:92
  20.7 2.1 %collective-permute-start.2 = (bf16[384,256]{1,0:T(8,128)(2,1)S(1)}, bf16[384,256]{1,0:T(8,128)(2,1)S(1)}, u32[]{:S(2)}, u32[]{:S(2)}) collective-permute-start(bf16[384,256]{1,0:T(8,128)(2,1)S(1)} %get-tuple-element.13), channel_id=1, source_target_pairs={{0,4},{2,6},{4,0},{6,2},{8,12},{10,14},{12,8},{14,10},{1,5},{3,7},... | collective-permute-start | bytes 589832 | tf_op jit(solution)/shard_map/ppermute | solution.py:91
  22.8 3.7 %collective-permute-start.1 = (bf16[384,256]{1,0:T(8,128)(2,1)S(1)}, bf16[384,256]{1,0:T(8,128)(2,1)S(1)}, u32[]{:S(2)}, u32[]{:S(2)}) collective-permute-start(bf16[384,256]{1,0:T(8,128)(2,1)S(1)} %get-tuple-element.11), channel_id=1, source_target_pairs={{0,4},{2,6},{4,0},{6,2},{8,12},{10,14},{12,8},{14,10},{1,5},{3,7},... | collective-permute-start | bytes 589832 | tf_op jit(solution)/shard_map/ppermute | solution.py:93
  26.5 2.4 %collective-permute-start.4 = (bf16[384,256]{1,0:T(8,128)(2,1)S(1)}, bf16[384,256]{1,0:T(8,128)(2,1)S(1)}, u32[]{:S(2)}, u32[]{:S(2)}) collective-permute-start(bf16[384,256]{1,0:T(8,128)(2,1)S(1)} %get-tuple-element.15), channel_id=1, source_target_pairs={{0,12},{2,14},{4,8},{6,10},{8,4},{10,6},{12,0},{14,2},{1,13},{3,15... | collective-permute-start | bytes 589832 | tf_op jit(solution)/shard_map/ppermute | solution.py:94
  29.0 2.2 %collective-permute-start.6 = (bf16[384,256]{1,0:T(8,128)(2,1)S(1)}, bf16[384,256]{1,0:T(8,128)(2,1)S(1)}, u32[]{:S(2)}, u32[]{:S(2)}) collective-permute-start(bf16[384,256]{1,0:T(8,128)(2,1)S(1)} %add_convert_fusion), channel_id=1, source_target_pairs={{0,4},{2,6},{4,0},{6,2},{8,12},{10,14},{12,8},{14,10},{1,5},{3,7},... | collective-permute-start | bytes 589832 | tf_op jit(solution)/shard_map/ppermute | solution.py:96
  31.3 4.4 %collective-permute-start.3 = (bf16[384,256]{1,0:T(8,128)(2,1)S(1)}, bf16[384,256]{1,0:T(8,128)(2,1)S(1)}, u32[]{:S(2)}, u32[]{:S(2)}) collective-permute-start(bf16[384,256]{1,0:T(8,128)(2,1)S(1)} %add_convert_fusion.1), channel_id=1, source_target_pairs={{0,12},{2,14},{4,8},{6,10},{8,4},{10,6},{12,0},{14,2},{1,13},{3,15... | collective-permute-start | bytes 589832 | tf_op jit(solution)/shard_map/ppermute | solution.py:95
  37.7 2.4 %collective-permute-done.3.refs_2_ = bf16[384,256]{1,0:T(8,128)(2,1)S(1)} collective-permute-done((bf16[384,256]{1,0:T(8,128)(2,1)S(1)}, bf16[384,256]{1,0:T(8,128)(2,1)S(1)}, u32[]{:S(2)}, u32[]{:S(2)}) %collective-permute-start.3) | collective-permute-done | bytes 196640 | tf_op jit(solution)/shard_map/ppermute | solution.py:95
  41.0 11.9 %all-to-all-start = ((bf16[32,8,768]{2,1,0:T(8,128)(2,1)}), bf16[32,8,768]{2,1,0:T(8,128)(2,1)S(1)}, u32[]{:S(2)}, u32[]{:S(2)}) async-start(bf16[32,8,768]{2,1,0:T(8,128)(2,1)} %bitcast.7), calls=%async_computation | async-start | bytes 786432 | tf_op jit(solution)/shard_map/all_to_all | solution.py:144
  53.0 8.2 %all-to-all-done = bf16[32,8,768]{2,1,0:T(8,128)(2,1)S(1)} async-done(((bf16[32,8,768]{2,1,0:T(8,128)(2,1)}), bf16[32,8,768]{2,1,0:T(8,128)(2,1)S(1)}, u32[]{:S(2)}, u32[]{:S(2)}) %all-to-all-start) | async-done | bytes 393248 | tf_op jit(solution)/shard_map/all_to_all | solution.py:144
  65.3 5.3 %all-to-all-start.1 = ((bf16[4,8,4096]{2,1,0:T(8,128)(2,1)}), bf16[4,8,4096]{2,1,0:T(8,128)(2,1)S(1)}, u32[]{:S(2)}, u32[]{:S(2)}) async-start(bf16[4,8,4096]{2,1,0:T(8,128)(2,1)} %broadcast_in_dim.30), calls=%async_computation.1 | async-start | bytes 524288 | tf_op jit(solution)/shard_map/all_to_all | solution.py:114
  71.5 5.4 %all-to-all-done.1 = bf16[4,8,4096]{2,1,0:T(8,128)(2,1)S(1)} async-done(((bf16[4,8,4096]{2,1,0:T(8,128)(2,1)}), bf16[4,8,4096]{2,1,0:T(8,128)(2,1)S(1)}, u32[]{:S(2)}, u32[]{:S(2)}) %all-to-all-start.1) | async-done | bytes 262176 | tf_op jit(solution)/shard_map/all_to_all | solution.py:114
  76.9 2.6 %collective-permute-start.7 = (bf16[32,4096]{1,0:T(8,128)(2,1)S(1)}, bf16[32,4096]{1,0:T(8,128)(2,1)S(1)}, u32[]{:S(2)}, u32[]{:S(2)}) collective-permute-start(bf16[32,4096]{1,0:T(8,128)(2,1)S(1)} %bitcast.60), channel_id=1, source_target_pairs={{0,64},{16,80},{32,96},{48,112},{64,0},{80,16},{96,32},{112,48},{1... | collective-permute-start | bytes 786440 | tf_op jit(solution)/shard_map/ppermute | solution.py:126
  79.4 5.3 %collective-permute-start.8 = (bf16[32,4096]{1,0:T(8,128)(2,1)S(1)}, bf16[32,4096]{1,0:T(8,128)(2,1)S(1)}, u32[]{:S(2)}, u32[]{:S(2)}) collective-permute-start(bf16[32,4096]{1,0:T(8,128)(2,1)S(1)} %bitcast.61), channel_id=1, source_target_pairs={{0,448},{16,464},{32,480},{48,496},{64,128},{80,144},{96,160},{112... | collective-permute-start | bytes 786440 | tf_op jit(solution)/shard_map/ppermute | solution.py:127
  85.1 4.3 %collective-permute-start.9 = (bf16[32,4096]{1,0:T(8,128)(2,1)S(1)}, bf16[32,4096]{1,0:T(8,128)(2,1)S(1)}, u32[]{:S(2)}, u32[]{:S(2)}) collective-permute-start(bf16[32,4096]{1,0:T(8,128)(2,1)S(1)} %collective-permute-done.7), channel_id=1, source_target_pairs={{0,448},{16,464},{32,480},{48,496},{64,128},{80,144},{96,160},{112... | collective-permute-start | bytes 786440 | tf_op jit(solution)/shard_map/ppermute | solution.py:134
  89.4 2.1 %collective-permute-done.8 = bf16[32,4096]{1,0:T(8,128)(2,1)S(1)} collective-permute-done((bf16[32,4096]{1,0:T(8,128)(2,1)S(1)}, bf16[32,4096]{1,0:T(8,128)(2,1)S(1)}, u32[]{:S(2)}, u32[]{:S(2)}) %collective-permute-start.8) | collective-permute-done | bytes 262176 | tf_op jit(solution)/shard_map/ppermute | solution.py:127
  94.7 2.7 %collective-permute-start.11 = (bf16[32,4096]{1,0:T(8,128)(2,1)S(1)}, bf16[32,4096]{1,0:T(8,128)(2,1)S(1)}, u32[]{:S(2)}, u32[]{:S(2)}) collective-permute-start(bf16[32,4096]{1,0:T(8,128)(2,1)S(1)} %collective-permute-done.9), channel_id=1, source_target_pairs={{0,64},{16,80},{32,96},{48,112},{64,0},{80,16},{96,32},{112,48},{1... | collective-permute-start | bytes 786440 | tf_op jit(solution)/shard_map/ppermute | solution.py:134
  97.4 4.7 %collective-permute-done.10 = bf16[32,4096]{1,0:T(8,128)(2,1)S(1)} collective-permute-done((bf16[32,4096]{1,0:T(8,128)(2,1)S(1)}, bf16[32,4096]{1,0:T(8,128)(2,1)S(1)}, u32[]{:S(2)}, u32[]{:S(2)}) %collective-permute-start.10) | collective-permute-done | bytes 262176 | tf_op jit(solution)/shard_map/ppermute | solution.py:134
  104.9 4.3 %collective-permute-start.13 = (bf16[16,4096]{1,0:T(8,128)(2,1)S(1)}, bf16[16,4096]{1,0:T(8,128)(2,1)S(1)}, u32[]{:S(2)}, u32[]{:S(2)}) collective-permute-start(bf16[16,4096]{1,0:T(8,128)(2,1)S(1)} %slice.26), channel_id=1, source_target_pairs={{0,448},{16,464},{32,480},{48,496},{64,128},{80,144},{96,160},{112... | collective-permute-start | bytes 393224 | tf_op jit(solution)/shard_map/ppermute | solution.py:134
  109.2 2.6 %collective-permute-done.12 = bf16[32,4096]{1,0:T(8,128)(2,1)S(1)} collective-permute-done((bf16[32,4096]{1,0:T(8,128)(2,1)S(1)}, bf16[32,4096]{1,0:T(8,128)(2,1)S(1)}, u32[]{:S(2)}, u32[]{:S(2)}) %collective-permute-start.12) | collective-permute-done | bytes 262176 | tf_op jit(solution)/shard_map/ppermute | solution.py:134
  113.9 4.8 %collective-permute-done.14 = bf16[16,4096]{1,0:T(8,128)(2,1)S(1)} collective-permute-done((bf16[16,4096]{1,0:T(8,128)(2,1)S(1)}, bf16[16,4096]{1,0:T(8,128)(2,1)S(1)}, u32[]{:S(2)}, u32[]{:S(2)}) %collective-permute-start.14) | collective-permute-done | bytes 131104 | tf_op jit(solution)/shard_map/ppermute | solution.py:134
  125.5 14.0 %all_to_all.15 = bf16[4,512,128]{2,1,0:T(8,128)(2,1)S(1)} all-to-all(bf16[4,512,128]{2,1,0:T(8,128)(2,1)S(1)} %fusion.1), channel_id=1, replica_groups={{0,4,8,12},{2,6,10,14},{1,5,9,13},{3,7,11,15},{16,20,24,28},{18,22,26,3..., dimensions={0} | all-to-all | bytes 1048576 | tf_op jit(solution)/shard_map/all_to_all | solution.py:175
  139.5 8.3 %collective-permute-start.16 = (bf16[512,128]{1,0:T(8,128)(2,1)S(1)}, bf16[512,128]{1,0:T(8,128)(2,1)S(1)}, u32[]{:S(2)}, u32[]{:S(2)}) collective-permute-start(bf16[512,128]{1,0:T(8,128)(2,1)S(1)} %fusion.8), channel_id=1, source_target_pairs={{0,1},{1,0},{2,3},{3,2},{4,5},{5,4},{6,7},{7,6},{8,9},{9,8},{10,11... | collective-permute-start | bytes 393224 | tf_op jit(solution)/shard_map/ppermute | solution.py:177
  148.5 4.6 %collective-permute-done.16 = bf16[512,128]{1,0:T(8,128)(2,1)S(1)} collective-permute-done((bf16[512,128]{1,0:T(8,128)(2,1)S(1)}, bf16[512,128]{1,0:T(8,128)(2,1)S(1)}, u32[]{:S(2)}, u32[]{:S(2)}) %collective-permute-start.16) | collective-permute-done | bytes 131104 | tf_op jit(solution)/shard_map/ppermute | solution.py:177
  (70 shorter events, 29.8 us)
Async XLA Ops:
  7.2 56.0 %copy-start = (bf16[128,32]{0,1:T(8,128)(2,1)S(1)}, bf16[128,32]{0,1:T(8,128)(2,1)}, u32[]{:S(2)}) copy-start(bf16[128,32]{0,1:T(8,128)(2,1)} %param.10) | copy-start | bytes 24580
  9.5 5.3 %collective-permute-start = (bf16[3072,256]{1,0:T(8,128)(2,1)S(1)}, bf16[3072,256]{1,0:T(8,128)(2,1)S(1)}, u32[]{:S(2)}, u32[]{:S(2)}) collective-permute-start(bf16[3072,256]{1,0:T(8,128)(2,1)S(1)} %pack.1), channel_id=1, source_target_pairs={{0,2},{2,0},{4,6},{6,4},{8,10},{10,8},{12,14},{14,12},{1,3},{3,1},... | collective-permute-start | bytes 4718600 | tf_op jit(solution)/shard_map/ppermute | solution.py:76
  16.0 36.9 %copy-start.5 = (s32[128]{0:T(128)S(1)}, s32[128]{0:T(128)}, u32[]{:S(2)}) copy-start(s32[128]{0:T(128)} %param.9) | copy-start | bytes 1540
  16.0 36.9 %copy-start.3 = (s32[1,1,8,128]{3,2,1,0:T(8,128)S(1)}, s32[1,1,8,128]{3,2,1,0:T(8,128)}, u32[]{:S(2)}) copy-start(s32[1,1,8,128]{3,2,1,0:T(8,128)} %param.8) | copy-start | bytes 12292
  16.0 12.9 %collective-permute-start.5 = (bf16[384,256]{1,0:T(8,128)(2,1)S(1)}, bf16[384,256]{1,0:T(8,128)(2,1)S(1)}, u32[]{:S(2)}, u32[]{:S(2)}) collective-permute-start(bf16[384,256]{1,0:T(8,128)(2,1)S(1)} %get-tuple-element.17), channel_id=1, source_target_pairs={{0,12},{2,14},{4,8},{6,10},{8,4},{10,6},{12,0},{14,2},{1,13},{3,15... | collective-permute-start | bytes 589832 | tf_op jit(solution)/shard_map/ppermute | solution.py:92
  20.7 10.5 %collective-permute-start.2 = (bf16[384,256]{1,0:T(8,128)(2,1)S(1)}, bf16[384,256]{1,0:T(8,128)(2,1)S(1)}, u32[]{:S(2)}, u32[]{:S(2)}) collective-permute-start(bf16[384,256]{1,0:T(8,128)(2,1)S(1)} %get-tuple-element.13), channel_id=1, source_target_pairs={{0,4},{2,6},{4,0},{6,2},{8,12},{10,14},{12,8},{14,10},{1,5},{3,7},... | collective-permute-start | bytes 589832 | tf_op jit(solution)/shard_map/ppermute | solution.py:91
  22.8 12.9 %collective-permute-start.1 = (bf16[384,256]{1,0:T(8,128)(2,1)S(1)}, bf16[384,256]{1,0:T(8,128)(2,1)S(1)}, u32[]{:S(2)}, u32[]{:S(2)}) collective-permute-start(bf16[384,256]{1,0:T(8,128)(2,1)S(1)} %get-tuple-element.11), channel_id=1, source_target_pairs={{0,4},{2,6},{4,0},{6,2},{8,12},{10,14},{12,8},{14,10},{1,5},{3,7},... | collective-permute-start | bytes 589832 | tf_op jit(solution)/shard_map/ppermute | solution.py:93
  26.5 9.2 %collective-permute-start.4 = (bf16[384,256]{1,0:T(8,128)(2,1)S(1)}, bf16[384,256]{1,0:T(8,128)(2,1)S(1)}, u32[]{:S(2)}, u32[]{:S(2)}) collective-permute-start(bf16[384,256]{1,0:T(8,128)(2,1)S(1)} %get-tuple-element.15), channel_id=1, source_target_pairs={{0,12},{2,14},{4,8},{6,10},{8,4},{10,6},{12,0},{14,2},{1,13},{3,15... | collective-permute-start | bytes 589832 | tf_op jit(solution)/shard_map/ppermute | solution.py:94
  29.0 8.7 %collective-permute-start.6 = (bf16[384,256]{1,0:T(8,128)(2,1)S(1)}, bf16[384,256]{1,0:T(8,128)(2,1)S(1)}, u32[]{:S(2)}, u32[]{:S(2)}) collective-permute-start(bf16[384,256]{1,0:T(8,128)(2,1)S(1)} %add_convert_fusion), channel_id=1, source_target_pairs={{0,4},{2,6},{4,0},{6,2},{8,12},{10,14},{12,8},{14,10},{1,5},{3,7},... | collective-permute-start | bytes 589832 | tf_op jit(solution)/shard_map/ppermute | solution.py:96
  31.3 8.8 %collective-permute-start.3 = (bf16[384,256]{1,0:T(8,128)(2,1)S(1)}, bf16[384,256]{1,0:T(8,128)(2,1)S(1)}, u32[]{:S(2)}, u32[]{:S(2)}) collective-permute-start(bf16[384,256]{1,0:T(8,128)(2,1)S(1)} %add_convert_fusion.1), channel_id=1, source_target_pairs={{0,12},{2,14},{4,8},{6,10},{8,4},{10,6},{12,0},{14,2},{1,13},{3,15... | collective-permute-start | bytes 589832 | tf_op jit(solution)/shard_map/ppermute | solution.py:95
  41.0 20.2 %all-to-all-start = ((bf16[32,8,768]{2,1,0:T(8,128)(2,1)}), bf16[32,8,768]{2,1,0:T(8,128)(2,1)S(1)}, u32[]{:S(2)}, u32[]{:S(2)}) async-start(bf16[32,8,768]{2,1,0:T(8,128)(2,1)} %bitcast.7), calls=%async_computation | async-start | bytes 786432 | tf_op jit(solution)/shard_map/all_to_all | solution.py:144
  65.3 11.6 %all-to-all-start.1 = ((bf16[4,8,4096]{2,1,0:T(8,128)(2,1)}), bf16[4,8,4096]{2,1,0:T(8,128)(2,1)S(1)}, u32[]{:S(2)}, u32[]{:S(2)}) async-start(bf16[4,8,4096]{2,1,0:T(8,128)(2,1)} %broadcast_in_dim.30), calls=%async_computation.1 | async-start | bytes 524288 | tf_op jit(solution)/shard_map/all_to_all | solution.py:114
  70.6 48.2 %all-gather.2.cloned.1.call-start = ((), (), s32[]{:S(2)}) async-start(), calls=%async_computation.3 | async-start | bytes 1179648 | tf_op jit(solution)/shard_map/all_gather | solution.py:141
  76.9 8.3 %collective-permute-start.7 = (bf16[32,4096]{1,0:T(8,128)(2,1)S(1)}, bf16[32,4096]{1,0:T(8,128)(2,1)S(1)}, u32[]{:S(2)}, u32[]{:S(2)}) collective-permute-start(bf16[32,4096]{1,0:T(8,128)(2,1)S(1)} %bitcast.60), channel_id=1, source_target_pairs={{0,64},{16,80},{32,96},{48,112},{64,0},{80,16},{96,32},{112,48},{1... | collective-permute-start | bytes 786440 | tf_op jit(solution)/shard_map/ppermute | solution.py:126
  79.4 12.0 %collective-permute-start.8 = (bf16[32,4096]{1,0:T(8,128)(2,1)S(1)}, bf16[32,4096]{1,0:T(8,128)(2,1)S(1)}, u32[]{:S(2)}, u32[]{:S(2)}) collective-permute-start(bf16[32,4096]{1,0:T(8,128)(2,1)S(1)} %bitcast.61), channel_id=1, source_target_pairs={{0,448},{16,464},{32,480},{48,496},{64,128},{80,144},{96,160},{112... | collective-permute-start | bytes 786440 | tf_op jit(solution)/shard_map/ppermute | solution.py:127
  85.1 9.5 %collective-permute-start.9 = (bf16[32,4096]{1,0:T(8,128)(2,1)S(1)}, bf16[32,4096]{1,0:T(8,128)(2,1)S(1)}, u32[]{:S(2)}, u32[]{:S(2)}) collective-permute-start(bf16[32,4096]{1,0:T(8,128)(2,1)S(1)} %collective-permute-done.7), channel_id=1, source_target_pairs={{0,448},{16,464},{32,480},{48,496},{64,128},{80,144},{96,160},{112... | collective-permute-start | bytes 786440 | tf_op jit(solution)/shard_map/ppermute | solution.py:134
  91.5 10.6 %collective-permute-start.10 = (bf16[32,4096]{1,0:T(8,128)(2,1)S(1)}, bf16[32,4096]{1,0:T(8,128)(2,1)S(1)}, u32[]{:S(2)}, u32[]{:S(2)}) collective-permute-start(bf16[32,4096]{1,0:T(8,128)(2,1)S(1)} %collective-permute-done.8), channel_id=1, source_target_pairs={{0,64},{16,80},{32,96},{48,112},{64,0},{80,16},{96,32},{112,48},{1... | collective-permute-start | bytes 786440 | tf_op jit(solution)/shard_map/ppermute | solution.py:134
  94.7 10.2 %collective-permute-start.11 = (bf16[32,4096]{1,0:T(8,128)(2,1)S(1)}, bf16[32,4096]{1,0:T(8,128)(2,1)S(1)}, u32[]{:S(2)}, u32[]{:S(2)}) collective-permute-start(bf16[32,4096]{1,0:T(8,128)(2,1)S(1)} %collective-permute-done.9), channel_id=1, source_target_pairs={{0,64},{16,80},{32,96},{48,112},{64,0},{80,16},{96,32},{112,48},{1... | collective-permute-start | bytes 786440 | tf_op jit(solution)/shard_map/ppermute | solution.py:134
  102.1 9.8 %collective-permute-start.12 = (bf16[32,4096]{1,0:T(8,128)(2,1)S(1)}, bf16[32,4096]{1,0:T(8,128)(2,1)S(1)}, u32[]{:S(2)}, u32[]{:S(2)}) collective-permute-start(bf16[32,4096]{1,0:T(8,128)(2,1)S(1)} %collective-permute-done.10), channel_id=1, source_target_pairs={{0,448},{16,464},{32,480},{48,496},{64,128},{80,144},{96,160},{112... | collective-permute-start | bytes 786440 | tf_op jit(solution)/shard_map/ppermute | solution.py:134
  104.9 9.0 %collective-permute-start.13 = (bf16[16,4096]{1,0:T(8,128)(2,1)S(1)}, bf16[16,4096]{1,0:T(8,128)(2,1)S(1)}, u32[]{:S(2)}, u32[]{:S(2)}) collective-permute-start(bf16[16,4096]{1,0:T(8,128)(2,1)S(1)} %slice.26), channel_id=1, source_target_pairs={{0,448},{16,464},{32,480},{48,496},{64,128},{80,144},{96,160},{112... | collective-permute-start | bytes 393224 | tf_op jit(solution)/shard_map/ppermute | solution.py:134
  111.8 6.9 %collective-permute-start.14 = (bf16[16,4096]{1,0:T(8,128)(2,1)S(1)}, bf16[16,4096]{1,0:T(8,128)(2,1)S(1)}, u32[]{:S(2)}, u32[]{:S(2)}) collective-permute-start(bf16[16,4096]{1,0:T(8,128)(2,1)S(1)} %slice.27), channel_id=1, source_target_pairs={{0,64},{16,80},{32,96},{48,112},{64,0},{80,16},{96,32},{112,48},{1... | collective-permute-start | bytes 393224 | tf_op jit(solution)/shard_map/ppermute | solution.py:134
  113.8 6.9 %copy-start.2 = (bf16[1,1,256,128]{3,2,1,0:T(8,128)(2,1)S(1)}, bf16[1,1,256,128]{3,2,1,0:T(8,128)(2,1)}, u32[]{:S(2)}) copy-start(bf16[1,1,256,128]{3,2,1,0:T(8,128)(2,1)} %param.13) | copy-start | bytes 196612
  121.5 3.8 %collective-permute-start.15 = (bf16[4,512,128]{2,1,0:T(8,128)(2,1)S(1)}, bf16[4,512,128]{2,1,0:T(8,128)(2,1)S(1)}, u32[]{:S(2)}, u32[]{:S(2)}) collective-permute-start(bf16[4,512,128]{2,1,0:T(8,128)(2,1)S(1)} %dynamic-slice_bitcast_fusion), channel_id=1, source_target_pairs={{0,2},{2,0},{4,6},{6,4},{8,10},{10,8},{12,14},{14,12},{1,3},{3,1},... | collective-permute-start | bytes 1572872 | tf_op jit(solution)/shard_map/ppermute | solution.py:174
  139.5 13.5 %collective-permute-start.16 = (bf16[512,128]{1,0:T(8,128)(2,1)S(1)}, bf16[512,128]{1,0:T(8,128)(2,1)S(1)}, u32[]{:S(2)}, u32[]{:S(2)}) collective-permute-start(bf16[512,128]{1,0:T(8,128)(2,1)S(1)} %fusion.8), channel_id=1, source_target_pairs={{0,1},{1,0},{2,3},{3,2},{4,5},{5,4},{6,7},{7,6},{8,9},{9,8},{10,11... | collective-permute-start | bytes 393224 | tf_op jit(solution)/shard_map/ppermute | solution.py:177
  (2 other events, 3.2 us)
Sparse Core Ops, SparseCore 0:
  73.5 30.4 all-gather.1

commit v8 on v7

--- a/solution.py
+++ b/solution.py
@@ -21,7 +21,6 @@
 Y_EVEN = swaps(N_Y * N_Z, lambda n: n ^ N_Z)
 Y_ODD = swaps(N_Y * N_Z, lambda n: (((n // N_Z + 1) ^ 1) - 1) % N_Y * N_Z + n % N_Z)
 Z_GROUPS = [[N_Z * y + z for z in range(N_Z)] for y in range(N_Y)]
-X_GROUPS = [[N_CORE * x + c for x in range(N_X)] for c in range(N_CORE)]
 DP_SWAP = swaps(2, lambda d: d ^ 1)
 
 
@@ -32,8 +31,27 @@
     return total
 
 
-def pack_kernel(h_ref, rows_ref, out_ref):
-    out_ref[...] = rows_ref[...]
+def sum_over_x(a, b):
+    a_far = lax.ppermute(a[2], "hst", X_EVEN)
+    b_far = lax.ppermute(b[2], "hst", X_ODD)
+    a_one = lax.ppermute(a[1], "hst", X_EVEN)
+    b_one = lax.ppermute(b[3], "hst", X_ODD)
+    a_two = lax.ppermute(add(a[3], a_far).astype(a_far.dtype), "hst", X_ODD)
+    b_two = lax.ppermute(add(b[1], b_far).astype(b_far.dtype), "hst", X_EVEN)
+    return (a[0], a_one, a_two), (b[0], b_one, b_two)
+
+
+def pack_kernel(h_ref, rows_ref, out_ref, sems):
+    rows, samples = rows_ref.shape[0], out_ref.shape[1]
+    copies = []
+    for j in range(N_X):
+        first = pl.multiple_of((h_ref[0] ^ 1 ^ (6 * j % 8)) * samples, samples)
+        source = rows_ref.at[:, pl.ds(first, samples)]
+        target = out_ref.at[pl.ds(j * rows, rows), :]
+        copies.append(pltpu.make_async_copy(source, target, sems.at[j]))
+        copies[-1].start()
+    for copy in copies:
+        copy.wait()
 
 
 def pair_kernel(h_ref, rows_ref, got_ref, *out_refs):
@@ -62,15 +80,18 @@
     h = lax.axis_index("hst").astype(jnp.int32).reshape(1)
     params = pltpu.CompilerParams(vmem_limit_bytes=VMEM)
     block = pl.BlockSpec((rows, samples), lambda j, h: (j, 0))
-    theirs = pl.BlockSpec((rows, samples), lambda j, h: (0, h[0] ^ 1 ^ (6 * j % 8)))
     mine = pl.BlockSpec((rows, samples), lambda j, h: (0, h[0] ^ (6 * j % 8)))
     given = pl.pallas_call(
         pack_kernel,
         out_shape=jax.ShapeDtypeStruct((N_X * rows, samples), flat.dtype),
         grid_spec=pltpu.PrefetchScalarGridSpec(
-            num_scalar_prefetch=1, grid=(N_X,), in_specs=[theirs], out_specs=block
+            num_scalar_prefetch=1,
+            grid=(1,),
+            in_specs=[pl.BlockSpec(memory_space=pltpu.HBM)],
+            out_specs=pl.BlockSpec(memory_space=pl.ANY),
+            scratch_shapes=[pltpu.SemaphoreType.DMA((N_X,))],
         ),
-        compiler_params=pltpu.CompilerParams(vmem_limit_bytes=4 * VMEM),
+        compiler_params=params,
         name="pack",
     )(h, flat)
     got = lax.ppermute(given, "hst", CORE_SWAP)
@@ -87,19 +108,13 @@
         compiler_params=params,
         name="pair",
     )(h, flat, got)
-    a, b = out[:N_X], out[N_X:]
-    a_far = lax.ppermute(a[2], "hst", X_EVEN)
-    b_far = lax.ppermute(b[2], "hst", X_ODD)
-    a_one = lax.ppermute(a[1], "hst", X_EVEN)
-    b_one = lax.ppermute(b[3], "hst", X_ODD)
-    a_two = lax.ppermute(add(a[3], a_far).astype(flat.dtype), "hst", X_ODD)
-    b_two = lax.ppermute(add(b[1], b_far).astype(flat.dtype), "hst", X_EVEN)
+    a_parts, b_parts = sum_over_x(out[:N_X], out[N_X:])
     return pl.pallas_call(
         turn_kernel,
         out_shape=jax.ShapeDtypeStruct((samples, rows), flat.dtype),
         compiler_params=params,
         name="turn",
-    )(a[0], a_one, a_two, b[0], b_one, b_two)
+    )(*a_parts, *b_parts)
 
 
 def normalize(flat_rows, ln_gain):
@@ -172,9 +187,13 @@
     given = lax.dynamic_index_in_dim(term, 1 - core, 1, keepdims=False)
     kept = lax.dynamic_index_in_dim(term, core, 1, keepdims=False)
     pair = add(kept, lax.ppermute(given, "hst", CORE_SWAP)).astype(jnp.bfloat16)
-    terms = lax.all_to_all(pair, "hst", 0, 0, axis_index_groups=X_GROUPS, tiled=True)
-    share = add(*[terms[i] for i in range(N_X)]).astype(jnp.bfloat16)
-    grad_w = add(share, lax.ppermute(share, "dp", DP_SWAP))
+    x, half = lax.axis_index("hst") // N_CORE, w_in.shape[0] // 2
+    away = [lax.dynamic_index_in_dim(pair, x ^ r, 0, keepdims=False) for r in range(N_X)]
+    a, b = [piece[:half] for piece in away], [piece[half:] for piece in away]
+    sums = sum_over_x(a, b)
+    shares = [add(*parts).astype(jnp.bfloat16) for parts in sums]
+    grad_w = [add(share, lax.ppermute(share, "dp", DP_SWAP)) for share in shares]
+    grad_w = jnp.concatenate(grad_w, 0)
     return (hidden.reshape(1, 1, group, hidden_here), grad_w)
 
 

time: 162 us -> 175 us (1.080)
  the two profiles are of different devices: /device:TPU:96 before, /device:TPU:56 now
where the time goes in v8:
time: 175 us; the launch traced here: 172 us
  starting transfers between devices  102 us (58%)
  waiting for transfers between devices  41.8 us (24%)
  between operations  14.9 us (9%)
  local copies, waits for them, and re-layouts  5.52 us (3%)
  matrix products  3.34 us (2%)
  Pallas kernels  2.38 us (1%)
  other arithmetic  2.13 us (1%)
    ppermute x3, starting transfers between devices, gather_nodes(): lax.ppermute(lead, 'node', pairs[0])  12.7 us
    all_to_all x1, starting transfers between devices, local(): lax.all_to_all(summed.reshape(N_Y * N_Z, samples, rows), 'node', split_ax...  12.5 us
    ppermute x2, starting transfers between devices, local(): lax.ppermute(share, 'dp', DP_SWAP)  11.7 us
    all_to_all x1, waiting for transfers between devices, local(): lax.all_to_all(summed.reshape(N_Y * N_Z, samples, rows), 'node', split_ax...  10.8 us
    ppermute x2, starting transfers between devices, sum_over_x(): b_far = lax.ppermute(b[2], 'hst', X_ODD)  10.3 us
    ppermute x3, starting transfers between devices, gather_nodes(): lax.ppermute(trail, 'node', pairs[1])  9.93 us
    ppermute x2, starting transfers between devices, sum_over_x(): b_one = lax.ppermute(b[3], 'hst', X_ODD)  7.52 us
    ppermute x2, waiting for transfers between devices, local(): lax.ppermute(share, 'dp', DP_SWAP)  6.89 us
  transfers between devices with their start and end apart: 27, of which 13 were waited for; matrix products, arithmetic and copies ran while one was open for 1% of the time, Pallas kernels for 0%

profile of v8, /device:TPU:56, one launch (start us, length us, event | category | flops | bytes accessed | tf_op | source)
XLA Modules:
  0.0 172.1 jit_solution(5879327708218877868)
XLA Ops:
  11.3 3.4 %collective-permute-done.got_ref = bf16[3072,256]{1,0:T(8,128)(2,1)S(1)} collective-permute-done((bf16[3072,256]{1,0:T(8,128)(2,1)S(1)}, bf16[3072,256]{1,0:T(8,128)(2,1)S(1)}, u32[]{:S(2)}, u32[]{:S(2)}) %collective-permute-start) | collective-permute-done | bytes 1572896 | tf_op jit(solution)/shard_map/ppermute | solution.py:97
  15.8 4.7 %collective-permute-start.5 = (bf16[384,256]{1,0:T(8,128)(2,1)S(1)}, bf16[384,256]{1,0:T(8,128)(2,1)S(1)}, u32[]{:S(2)}, u32[]{:S(2)}) collective-permute-start(bf16[384,256]{1,0:T(8,128)(2,1)S(1)} %get-tuple-element.17), channel_id=1, source_target_pairs={{0,12},{2,14},{4,8},{6,10},{8,4},{10,6},{12,0},{14,2},{1,13},{3,15... | collective-permute-start | bytes 589832 | tf_op jit(solution)/shard_map/ppermute | solution.py:36
  22.6 3.7 %collective-permute-start.1 = (bf16[384,256]{1,0:T(8,128)(2,1)S(1)}, bf16[384,256]{1,0:T(8,128)(2,1)S(1)}, u32[]{:S(2)}, u32[]{:S(2)}) collective-permute-start(bf16[384,256]{1,0:T(8,128)(2,1)S(1)} %get-tuple-element.11), channel_id=1, source_target_pairs={{0,4},{2,6},{4,0},{6,2},{8,12},{10,14},{12,8},{14,10},{1,5},{3,7},... | collective-permute-start | bytes 589832 | tf_op jit(solution)/shard_map/ppermute | solution.py:37
  26.4 2.4 %collective-permute-start.4 = (bf16[384,256]{1,0:T(8,128)(2,1)S(1)}, bf16[384,256]{1,0:T(8,128)(2,1)S(1)}, u32[]{:S(2)}, u32[]{:S(2)}) collective-permute-start(bf16[384,256]{1,0:T(8,128)(2,1)S(1)} %get-tuple-element.15), channel_id=1, source_target_pairs={{0,12},{2,14},{4,8},{6,10},{8,4},{10,6},{12,0},{14,2},{1,13},{3,15... | collective-permute-start | bytes 589832 | tf_op jit(solution)/shard_map/ppermute | solution.py:38
  31.1 4.4 %collective-permute-start.3 = (bf16[384,256]{1,0:T(8,128)(2,1)S(1)}, bf16[384,256]{1,0:T(8,128)(2,1)S(1)}, u32[]{:S(2)}, u32[]{:S(2)}) collective-permute-start(bf16[384,256]{1,0:T(8,128)(2,1)S(1)} %add_convert_fusion.1), channel_id=1, source_target_pairs={{0,12},{2,14},{4,8},{6,10},{8,4},{10,6},{12,0},{14,2},{1,13},{3,15... | collective-permute-start | bytes 589832 | tf_op jit(solution)/shard_map/ppermute | solution.py:39
  37.5 2.4 %collective-permute-done.3.refs_2_ = bf16[384,256]{1,0:T(8,128)(2,1)S(1)} collective-permute-done((bf16[384,256]{1,0:T(8,128)(2,1)S(1)}, bf16[384,256]{1,0:T(8,128)(2,1)S(1)}, u32[]{:S(2)}, u32[]{:S(2)}) %collective-permute-start.3) | collective-permute-done | bytes 196640 | tf_op jit(solution)/shard_map/ppermute | solution.py:39
  40.8 12.5 %all-to-all-start = ((bf16[32,8,768]{2,1,0:T(8,128)(2,1)}), bf16[32,8,768]{2,1,0:T(8,128)(2,1)S(1)}, u32[]{:S(2)}, u32[]{:S(2)}) async-start(bf16[32,8,768]{2,1,0:T(8,128)(2,1)} %bitcast.7), calls=%async_computation | async-start | bytes 786432 | tf_op jit(solution)/shard_map/all_to_all | solution.py:159
  53.4 10.8 %all-to-all-done = bf16[32,8,768]{2,1,0:T(8,128)(2,1)S(1)} async-done(((bf16[32,8,768]{2,1,0:T(8,128)(2,1)}), bf16[32,8,768]{2,1,0:T(8,128)(2,1)S(1)}, u32[]{:S(2)}, u32[]{:S(2)}) %all-to-all-start) | async-done | bytes 393248 | tf_op jit(solution)/shard_map/all_to_all | solution.py:159
  68.3 3.4 %all-to-all-start.1 = ((bf16[4,8,4096]{2,1,0:T(8,128)(2,1)}), bf16[4,8,4096]{2,1,0:T(8,128)(2,1)S(1)}, u32[]{:S(2)}, u32[]{:S(2)}) async-start(bf16[4,8,4096]{2,1,0:T(8,128)(2,1)} %broadcast_in_dim.30), calls=%async_computation.1 | async-start | bytes 524288 | tf_op jit(solution)/shard_map/all_to_all | solution.py:129
  72.7 5.8 %all-to-all-done.1 = bf16[4,8,4096]{2,1,0:T(8,128)(2,1)S(1)} async-done(((bf16[4,8,4096]{2,1,0:T(8,128)(2,1)}), bf16[4,8,4096]{2,1,0:T(8,128)(2,1)S(1)}, u32[]{:S(2)}, u32[]{:S(2)}) %all-to-all-start.1) | async-done | bytes 262176 | tf_op jit(solution)/shard_map/all_to_all | solution.py:129
  78.5 3.5 %collective-permute-start.7 = (bf16[32,4096]{1,0:T(8,128)(2,1)S(1)}, bf16[32,4096]{1,0:T(8,128)(2,1)S(1)}, u32[]{:S(2)}, u32[]{:S(2)}) collective-permute-start(bf16[32,4096]{1,0:T(8,128)(2,1)S(1)} %bitcast.84), channel_id=1, source_target_pairs={{0,64},{16,80},{32,96},{48,112},{64,0},{80,16},{96,32},{112,48},{1... | collective-permute-start | bytes 786440 | tf_op jit(solution)/shard_map/ppermute | solution.py:141
  82.0 4.4 %collective-permute-start.8 = (bf16[32,4096]{1,0:T(8,128)(2,1)S(1)}, bf16[32,4096]{1,0:T(8,128)(2,1)S(1)}, u32[]{:S(2)}, u32[]{:S(2)}) collective-permute-start(bf16[32,4096]{1,0:T(8,128)(2,1)S(1)} %bitcast.85), channel_id=1, source_target_pairs={{0,448},{16,464},{32,480},{48,496},{64,128},{80,144},{96,160},{112... | collective-permute-start | bytes 786440 | tf_op jit(solution)/shard_map/ppermute | solution.py:142
  86.7 5.4 %collective-permute-start.9 = (bf16[32,4096]{1,0:T(8,128)(2,1)S(1)}, bf16[32,4096]{1,0:T(8,128)(2,1)S(1)}, u32[]{:S(2)}, u32[]{:S(2)}) collective-permute-start(bf16[32,4096]{1,0:T(8,128)(2,1)S(1)} %collective-permute-done.7), channel_id=1, source_target_pairs={{0,448},{16,464},{32,480},{48,496},{64,128},{80,144},{96,160},{112... | collective-permute-start | bytes 786440 | tf_op jit(solution)/shard_map/ppermute | solution.py:149
  92.1 2.2 %collective-permute-start.10 = (bf16[32,4096]{1,0:T(8,128)(2,1)S(1)}, bf16[32,4096]{1,0:T(8,128)(2,1)S(1)}, u32[]{:S(2)}, u32[]{:S(2)}) collective-permute-start(bf16[32,4096]{1,0:T(8,128)(2,1)S(1)} %collective-permute-done.8), channel_id=1, source_target_pairs={{0,64},{16,80},{32,96},{48,112},{64,0},{80,16},{96,32},{112,48},{1... | collective-permute-start | bytes 786440 | tf_op jit(solution)/shard_map/ppermute | solution.py:149
  100.4 4.2 %collective-permute-start.12 = (bf16[32,4096]{1,0:T(8,128)(2,1)S(1)}, bf16[32,4096]{1,0:T(8,128)(2,1)S(1)}, u32[]{:S(2)}, u32[]{:S(2)}) collective-permute-start(bf16[32,4096]{1,0:T(8,128)(2,1)S(1)} %collective-permute-done.10), channel_id=1, source_target_pairs={{0,448},{16,464},{32,480},{48,496},{64,128},{80,144},{96,160},{112... | collective-permute-start | bytes 786440 | tf_op jit(solution)/shard_map/ppermute | solution.py:149
  104.7 5.3 %collective-permute-start.13 = (bf16[16,4096]{1,0:T(8,128)(2,1)S(1)}, bf16[16,4096]{1,0:T(8,128)(2,1)S(1)}, u32[]{:S(2)}, u32[]{:S(2)}) collective-permute-start(bf16[16,4096]{1,0:T(8,128)(2,1)S(1)} %slice.62), channel_id=1, source_target_pairs={{0,448},{16,464},{32,480},{48,496},{64,128},{80,144},{96,160},{112... | collective-permute-start | bytes 393224 | tf_op jit(solution)/shard_map/ppermute | solution.py:149
  110.0 3.5 %collective-permute-start.14 = (bf16[16,4096]{1,0:T(8,128)(2,1)S(1)}, bf16[16,4096]{1,0:T(8,128)(2,1)S(1)}, u32[]{:S(2)}, u32[]{:S(2)}) collective-permute-start(bf16[16,4096]{1,0:T(8,128)(2,1)S(1)} %slice.63), channel_id=1, source_target_pairs={{0,64},{16,80},{32,96},{48,112},{64,0},{80,16},{96,32},{112,48},{1... | collective-permute-start | bytes 393224 | tf_op jit(solution)/shard_map/ppermute | solution.py:149
  113.6 3.3 %collective-permute-done.14 = bf16[16,4096]{1,0:T(8,128)(2,1)S(1)} collective-permute-done((bf16[16,4096]{1,0:T(8,128)(2,1)S(1)}, bf16[16,4096]{1,0:T(8,128)(2,1)S(1)}, u32[]{:S(2)}, u32[]{:S(2)}) %collective-permute-start.14) | collective-permute-done | bytes 131104 | tf_op jit(solution)/shard_map/ppermute | solution.py:149
  123.7 3.9 %collective-permute-start.17 = (bf16[256,128]{1,0:T(8,128)(2,1)S(1)}, bf16[256,128]{1,0:T(8,128)(2,1)S(1)}, u32[]{:S(2)}, u32[]{:S(2)}) collective-permute-start(bf16[256,128]{1,0:T(8,128)(2,1)S(1)} %get-tuple-element.21), channel_id=1, source_target_pairs={{0,4},{2,6},{4,0},{6,2},{8,12},{10,14},{12,8},{14,10},{1,5},{3,7},... | collective-permute-start | bytes 196616 | tf_op jit(solution)/shard_map/ppermute | solution.py:35
  129.6 5.7 %collective-permute-start.21 = (bf16[256,128]{1,0:T(8,128)(2,1)S(1)}, bf16[256,128]{1,0:T(8,128)(2,1)S(1)}, u32[]{:S(2)}, u32[]{:S(2)}) collective-permute-start(bf16[256,128]{1,0:T(8,128)(2,1)S(1)} %get-tuple-element.22), channel_id=1, source_target_pairs={{0,12},{2,14},{4,8},{6,10},{8,4},{10,6},{12,0},{14,2},{1,13},{3,15... | collective-permute-start | bytes 196616 | tf_op jit(solution)/shard_map/ppermute | solution.py:36
  137.2 5.1 %collective-permute-start.20 = (bf16[256,128]{1,0:T(8,128)(2,1)S(1)}, bf16[256,128]{1,0:T(8,128)(2,1)S(1)}, u32[]{:S(2)}, u32[]{:S(2)}) collective-permute-start(bf16[256,128]{1,0:T(8,128)(2,1)S(1)} %get-tuple-element.23), channel_id=1, source_target_pairs={{0,12},{2,14},{4,8},{6,10},{8,4},{10,6},{12,0},{14,2},{1,13},{3,15... | collective-permute-start | bytes 196616 | tf_op jit(solution)/shard_map/ppermute | solution.py:38
  145.8 8.2 %collective-permute-start.19 = (bf16[256,128]{1,0:T(8,128)(2,1)S(1)}, bf16[256,128]{1,0:T(8,128)(2,1)S(1)}, u32[]{:S(2)}, u32[]{:S(2)}) collective-permute-start(bf16[256,128]{1,0:T(8,128)(2,1)S(1)} %get-tuple-element.18), channel_id=1, source_target_pairs={{0,1},{1,0},{2,3},{3,2},{4,5},{5,4},{6,7},{7,6},{8,9},{9,8},{10,11... | collective-permute-start | bytes 196616 | tf_op jit(solution)/shard_map/ppermute | solution.py:195
  154.1 3.5 %collective-permute-start.23 = (bf16[256,128]{1,0:T(8,128)(2,1)S(1)}, bf16[256,128]{1,0:T(8,128)(2,1)S(1)}, u32[]{:S(2)}, u32[]{:S(2)}) collective-permute-start(bf16[256,128]{1,0:T(8,128)(2,1)S(1)} %fusion.10), channel_id=1, source_target_pairs={{0,1},{1,0},{2,3},{3,2},{4,5},{5,4},{6,7},{7,6},{8,9},{9,8},{10,11... | collective-permute-start | bytes 196616 | tf_op jit(solution)/shard_map/ppermute | solution.py:195
  157.6 6.9 %collective-permute-done.23 = bf16[256,128]{1,0:T(8,128)(2,1)S(1)} collective-permute-done((bf16[256,128]{1,0:T(8,128)(2,1)S(1)}, bf16[256,128]{1,0:T(8,128)(2,1)S(1)}, u32[]{:S(2)}, u32[]{:S(2)}) %collective-permute-start.23) | collective-permute-done | bytes 65568 | tf_op jit(solution)/shard_map/ppermute | solution.py:195
  (88 shorter events, 38.7 us)
Async XLA Ops:
  15.8 12.9 %collective-permute-start.5 = (bf16[384,256]{1,0:T(8,128)(2,1)S(1)}, bf16[384,256]{1,0:T(8,128)(2,1)S(1)}, u32[]{:S(2)}, u32[]{:S(2)}) collective-permute-start(bf16[384,256]{1,0:T(8,128)(2,1)S(1)} %get-tuple-element.17), channel_id=1, source_target_pairs={{0,12},{2,14},{4,8},{6,10},{8,4},{10,6},{12,0},{14,2},{1,13},{3,15... | collective-permute-start | bytes 589832 | tf_op jit(solution)/shard_map/ppermute | solution.py:36
  20.5 10.5 %collective-permute-start.2 = (bf16[384,256]{1,0:T(8,128)(2,1)S(1)}, bf16[384,256]{1,0:T(8,128)(2,1)S(1)}, u32[]{:S(2)}, u32[]{:S(2)}) collective-permute-start(bf16[384,256]{1,0:T(8,128)(2,1)S(1)} %get-tuple-element.13), channel_id=1, source_target_pairs={{0,4},{2,6},{4,0},{6,2},{8,12},{10,14},{12,8},{14,10},{1,5},{3,7},... | collective-permute-start | bytes 589832 | tf_op jit(solution)/shard_map/ppermute | solution.py:35
  22.6 12.9 %collective-permute-start.1 = (bf16[384,256]{1,0:T(8,128)(2,1)S(1)}, bf16[384,256]{1,0:T(8,128)(2,1)S(1)}, u32[]{:S(2)}, u32[]{:S(2)}) collective-permute-start(bf16[384,256]{1,0:T(8,128)(2,1)S(1)} %get-tuple-element.11), channel_id=1, source_target_pairs={{0,4},{2,6},{4,0},{6,2},{8,12},{10,14},{12,8},{14,10},{1,5},{3,7},... | collective-permute-start | bytes 589832 | tf_op jit(solution)/shard_map/ppermute | solution.py:37
  26.4 9.2 %collective-permute-start.4 = (bf16[384,256]{1,0:T(8,128)(2,1)S(1)}, bf16[384,256]{1,0:T(8,128)(2,1)S(1)}, u32[]{:S(2)}, u32[]{:S(2)}) collective-permute-start(bf16[384,256]{1,0:T(8,128)(2,1)S(1)} %get-tuple-element.15), channel_id=1, source_target_pairs={{0,12},{2,14},{4,8},{6,10},{8,4},{10,6},{12,0},{14,2},{1,13},{3,15... | collective-permute-start | bytes 589832 | tf_op jit(solution)/shard_map/ppermute | solution.py:38
  28.8 8.7 %collective-permute-start.6 = (bf16[384,256]{1,0:T(8,128)(2,1)S(1)}, bf16[384,256]{1,0:T(8,128)(2,1)S(1)}, u32[]{:S(2)}, u32[]{:S(2)}) collective-permute-start(bf16[384,256]{1,0:T(8,128)(2,1)S(1)} %add_convert_fusion), channel_id=1, source_target_pairs={{0,4},{2,6},{4,0},{6,2},{8,12},{10,14},{12,8},{14,10},{1,5},{3,7},... | collective-permute-start | bytes 589832 | tf_op jit(solution)/shard_map/ppermute | solution.py:40
  31.1 8.8 %collective-permute-start.3 = (bf16[384,256]{1,0:T(8,128)(2,1)S(1)}, bf16[384,256]{1,0:T(8,128)(2,1)S(1)}, u32[]{:S(2)}, u32[]{:S(2)}) collective-permute-start(bf16[384,256]{1,0:T(8,128)(2,1)S(1)} %add_convert_fusion.1), channel_id=1, source_target_pairs={{0,12},{2,14},{4,8},{6,10},{8,4},{10,6},{12,0},{14,2},{1,13},{3,15... | collective-permute-start | bytes 589832 | tf_op jit(solution)/shard_map/ppermute | solution.py:39
  40.8 23.4 %all-to-all-start = ((bf16[32,8,768]{2,1,0:T(8,128)(2,1)}), bf16[32,8,768]{2,1,0:T(8,128)(2,1)S(1)}, u32[]{:S(2)}, u32[]{:S(2)}) async-start(bf16[32,8,768]{2,1,0:T(8,128)(2,1)} %bitcast.7), calls=%async_computation | async-start | bytes 786432 | tf_op jit(solution)/shard_map/all_to_all | solution.py:159
  68.3 10.2 %all-to-all-start.1 = ((bf16[4,8,4096]{2,1,0:T(8,128)(2,1)}), bf16[4,8,4096]{2,1,0:T(8,128)(2,1)S(1)}, u32[]{:S(2)}, u32[]{:S(2)}) async-start(bf16[4,8,4096]{2,1,0:T(8,128)(2,1)} %broadcast_in_dim.30), calls=%async_computation.1 | async-start | bytes 524288 | tf_op jit(solution)/shard_map/all_to_all | solution.py:129
  71.7 45.2 %all-gather.2.cloned.1.call-start = ((), (), s32[]{:S(2)}) async-start(), calls=%async_computation.2 | async-start | bytes 1179648 | tf_op jit(solution)/shard_map/all_gather | solution.py:156
  78.5 8.3 %collective-permute-start.7 = (bf16[32,4096]{1,0:T(8,128)(2,1)S(1)}, bf16[32,4096]{1,0:T(8,128)(2,1)S(1)}, u32[]{:S(2)}, u32[]{:S(2)}) collective-permute-start(bf16[32,4096]{1,0:T(8,128)(2,1)S(1)} %bitcast.84), channel_id=1, source_target_pairs={{0,64},{16,80},{32,96},{48,112},{64,0},{80,16},{96,32},{112,48},{1... | collective-permute-start | bytes 786440 | tf_op jit(solution)/shard_map/ppermute | solution.py:141
  82.0 10.1 %collective-permute-start.8 = (bf16[32,4096]{1,0:T(8,128)(2,1)S(1)}, bf16[32,4096]{1,0:T(8,128)(2,1)S(1)}, u32[]{:S(2)}, u32[]{:S(2)}) collective-permute-start(bf16[32,4096]{1,0:T(8,128)(2,1)S(1)} %bitcast.85), channel_id=1, source_target_pairs={{0,448},{16,464},{32,480},{48,496},{64,128},{80,144},{96,160},{112... | collective-permute-start | bytes 786440 | tf_op jit(solution)/shard_map/ppermute | solution.py:142
  86.7 9.7 %collective-permute-start.9 = (bf16[32,4096]{1,0:T(8,128)(2,1)S(1)}, bf16[32,4096]{1,0:T(8,128)(2,1)S(1)}, u32[]{:S(2)}, u32[]{:S(2)}) collective-permute-start(bf16[32,4096]{1,0:T(8,128)(2,1)S(1)} %collective-permute-done.7), channel_id=1, source_target_pairs={{0,448},{16,464},{32,480},{48,496},{64,128},{80,144},{96,160},{112... | collective-permute-start | bytes 786440 | tf_op jit(solution)/shard_map/ppermute | solution.py:149
  92.1 8.3 %collective-permute-start.10 = (bf16[32,4096]{1,0:T(8,128)(2,1)S(1)}, bf16[32,4096]{1,0:T(8,128)(2,1)S(1)}, u32[]{:S(2)}, u32[]{:S(2)}) collective-permute-start(bf16[32,4096]{1,0:T(8,128)(2,1)S(1)} %collective-permute-done.8), channel_id=1, source_target_pairs={{0,64},{16,80},{32,96},{48,112},{64,0},{80,16},{96,32},{112,48},{1... | collective-permute-start | bytes 786440 | tf_op jit(solution)/shard_map/ppermute | solution.py:149
  96.4 8.3 %collective-permute-start.11 = (bf16[32,4096]{1,0:T(8,128)(2,1)S(1)}, bf16[32,4096]{1,0:T(8,128)(2,1)S(1)}, u32[]{:S(2)}, u32[]{:S(2)}) collective-permute-start(bf16[32,4096]{1,0:T(8,128)(2,1)S(1)} %collective-permute-done.9), channel_id=1, source_target_pairs={{0,64},{16,80},{32,96},{48,112},{64,0},{80,16},{96,32},{112,48},{1... | collective-permute-start | bytes 786440 | tf_op jit(solution)/shard_map/ppermute | solution.py:149
  100.4 9.6 %collective-permute-start.12 = (bf16[32,4096]{1,0:T(8,128)(2,1)S(1)}, bf16[32,4096]{1,0:T(8,128)(2,1)S(1)}, u32[]{:S(2)}, u32[]{:S(2)}) collective-permute-start(bf16[32,4096]{1,0:T(8,128)(2,1)S(1)} %collective-permute-done.10), channel_id=1, source_target_pairs={{0,448},{16,464},{32,480},{48,496},{64,128},{80,144},{96,160},{112... | collective-permute-start | bytes 786440 | tf_op jit(solution)/shard_map/ppermute | solution.py:149
  104.7 8.9 %collective-permute-start.13 = (bf16[16,4096]{1,0:T(8,128)(2,1)S(1)}, bf16[16,4096]{1,0:T(8,128)(2,1)S(1)}, u32[]{:S(2)}, u32[]{:S(2)}) collective-permute-start(bf16[16,4096]{1,0:T(8,128)(2,1)S(1)} %slice.62), channel_id=1, source_target_pairs={{0,448},{16,464},{32,480},{48,496},{64,128},{80,144},{96,160},{112... | collective-permute-start | bytes 393224 | tf_op jit(solution)/shard_map/ppermute | solution.py:149
  123.7 11.5 %collective-permute-start.17 = (bf16[256,128]{1,0:T(8,128)(2,1)S(1)}, bf16[256,128]{1,0:T(8,128)(2,1)S(1)}, u32[]{:S(2)}, u32[]{:S(2)}) collective-permute-start(bf16[256,128]{1,0:T(8,128)(2,1)S(1)} %get-tuple-element.21), channel_id=1, source_target_pairs={{0,4},{2,6},{4,0},{6,2},{8,12},{10,14},{12,8},{14,10},{1,5},{3,7},... | collective-permute-start | bytes 196616 | tf_op jit(solution)/shard_map/ppermute | solution.py:35
  127.6 14.8 %collective-permute-start.16 = (bf16[256,128]{1,0:T(8,128)(2,1)S(1)}, bf16[256,128]{1,0:T(8,128)(2,1)S(1)}, u32[]{:S(2)}, u32[]{:S(2)}) collective-permute-start(bf16[256,128]{1,0:T(8,128)(2,1)S(1)} %get-tuple-element.20), channel_id=1, source_target_pairs={{0,4},{2,6},{4,0},{6,2},{8,12},{10,14},{12,8},{14,10},{1,5},{3,7},... | collective-permute-start | bytes 196616 | tf_op jit(solution)/shard_map/ppermute | solution.py:37
  129.6 12.8 %collective-permute-start.21 = (bf16[256,128]{1,0:T(8,128)(2,1)S(1)}, bf16[256,128]{1,0:T(8,128)(2,1)S(1)}, u32[]{:S(2)}, u32[]{:S(2)}) collective-permute-start(bf16[256,128]{1,0:T(8,128)(2,1)S(1)} %get-tuple-element.22), channel_id=1, source_target_pairs={{0,12},{2,14},{4,8},{6,10},{8,4},{10,6},{12,0},{14,2},{1,13},{3,15... | collective-permute-start | bytes 196616 | tf_op jit(solution)/shard_map/ppermute | solution.py:36
  135.3 7.8 %collective-permute-start.18 = (bf16[256,128]{1,0:T(8,128)(2,1)S(1)}, bf16[256,128]{1,0:T(8,128)(2,1)S(1)}, u32[]{:S(2)}, u32[]{:S(2)}) collective-permute-start(bf16[256,128]{1,0:T(8,128)(2,1)S(1)} %fusion.11), channel_id=1, source_target_pairs={{0,12},{2,14},{4,8},{6,10},{8,4},{10,6},{12,0},{14,2},{1,13},{3,15... | collective-permute-start | bytes 196616 | tf_op jit(solution)/shard_map/ppermute | solution.py:39
  137.2 16.7 %collective-permute-start.20 = (bf16[256,128]{1,0:T(8,128)(2,1)S(1)}, bf16[256,128]{1,0:T(8,128)(2,1)S(1)}, u32[]{:S(2)}, u32[]{:S(2)}) collective-permute-start(bf16[256,128]{1,0:T(8,128)(2,1)S(1)} %get-tuple-element.23), channel_id=1, source_target_pairs={{0,12},{2,14},{4,8},{6,10},{8,4},{10,6},{12,0},{14,2},{1,13},{3,15... | collective-permute-start | bytes 196616 | tf_op jit(solution)/shard_map/ppermute | solution.py:38
  143.2 10.8 %collective-permute-start.22 = (bf16[256,128]{1,0:T(8,128)(2,1)S(1)}, bf16[256,128]{1,0:T(8,128)(2,1)S(1)}, u32[]{:S(2)}, u32[]{:S(2)}) collective-permute-start(bf16[256,128]{1,0:T(8,128)(2,1)S(1)} %get-tuple-element.19), channel_id=1, source_target_pairs={{0,4},{2,6},{4,0},{6,2},{8,12},{10,14},{12,8},{14,10},{1,5},{3,7},... | collective-permute-start | bytes 196616 | tf_op jit(solution)/shard_map/ppermute | solution.py:40
  145.8 11.8 %collective-permute-start.19 = (bf16[256,128]{1,0:T(8,128)(2,1)S(1)}, bf16[256,128]{1,0:T(8,128)(2,1)S(1)}, u32[]{:S(2)}, u32[]{:S(2)}) collective-permute-start(bf16[256,128]{1,0:T(8,128)(2,1)S(1)} %get-tuple-element.18), channel_id=1, source_target_pairs={{0,1},{1,0},{2,3},{3,2},{4,5},{5,4},{6,7},{7,6},{8,9},{9,8},{10,11... | collective-permute-start | bytes 196616 | tf_op jit(solution)/shard_map/ppermute | solution.py:195
  154.1 10.5 %collective-permute-start.23 = (bf16[256,128]{1,0:T(8,128)(2,1)S(1)}, bf16[256,128]{1,0:T(8,128)(2,1)S(1)}, u32[]{:S(2)}, u32[]{:S(2)}) collective-permute-start(bf16[256,128]{1,0:T(8,128)(2,1)S(1)} %fusion.10), channel_id=1, source_target_pairs={{0,1},{1,0},{2,3},{3,2},{4,5},{5,4},{6,7},{7,6},{8,9},{9,8},{10,11... | collective-permute-start | bytes 196616 | tf_op jit(solution)/shard_map/ppermute | solution.py:195
  (9 other events, 158.7 us)
Sparse Core Ops, SparseCore 0:
  74.7 29.5 all-gather.1

commit v9 on v7

--- a/solution.py
+++ b/solution.py
@@ -109,7 +109,7 @@
     return (centered * lax.rsqrt(variance + 1e-05) * ln_gain).astype(jnp.bfloat16)
 
 
-def gather_nodes(block):
+def gather_nodes(block, early):
     copies = jnp.broadcast_to(block, (N_Z,) + block.shape)
     line = lax.all_to_all(copies, "node", 0, 0, axis_index_groups=Z_GROUPS, tiled=True)
     line = line.reshape(-1, block.shape[1])
@@ -130,9 +130,10 @@
         way = step if step % 2 else -step
         group = put(put(group, lead, way), trail, -way)
         if step == N_Y // 2 - 1:
+            trail, early = lax.optimization_barrier((trail, early))
             lead, trail = lead[half:], trail[:half]
         lead, trail = lax.ppermute(lead, "node", pairs[0]), lax.ppermute(trail, "node", pairs[1])
-    return put(put(group, lead, N_Y // 2, half), trail, N_Y // 2)
+    return put(put(group, lead, N_Y // 2, half), trail, N_Y // 2), early
 
 
 def local(partials, counts, perm, fm_proj, ln_gain, w_in, d_hidden):
@@ -157,7 +158,7 @@
     pairwise = jnp.einsum("sfe,sek->sfk", pooled, projected, preferred_element_type=jnp.float32)
     z_local = normalize(pairwise.reshape(samples, -1), ln_gain)
 
-    z_group = gather_nodes(z_local)
+    z_group, w_full = gather_nodes(z_local, w_full)
     pre_act = jnp.dot(z_group, w_full, preferred_element_type=jnp.float32)
     sigma = jax.nn.sigmoid(pre_act)
     hidden = (pre_act * sigma).astype(jnp.bfloat16)

time: 162 us -> 162 us (level)
  local copies, waits for them, and re-layouts: 5.49 us -> 9 us
  waiting for transfers between devices: 44.9 us -> 42.5 us
    dynamic_update_slice x9, local copies, waits for them, and re-layouts: 0.2 us -> 2.14 us  [put(): return lax.dynamic_update_slice(group, part, (place, 0))]
  transfers between devices with their start and end apart: 20 -> 20, of which waited for: 15 -> 14; matrix products, arithmetic and copies ran while one was open for 1% -> 3% of each run, Pallas kernels for 0% -> 0%
where the time goes in v9:
time: 162 us; the launch traced here: 161 us
  starting transfers between devices  74.4 us (46%)
  waiting for transfers between devices  42.5 us (26%)
  between operations  14.7 us (9%)
  blocking collectives  14 us (9%)
  local copies, waits for them, and re-layouts  9 us (6%)
  Pallas kernels  2.56 us (2%)
  other arithmetic  2.12 us (1%)
  matrix products  2.09 us (1%)
    all_to_all x1, blocking collectives, local(): lax.all_to_all(pair, 'hst', 0, 0, axis_index_groups=X_GROUPS, tiled=True)  14 us
    ppermute x3, starting transfers between devices, gather_nodes(): lax.ppermute(lead, 'node', pairs[0])  12.1 us
    all_to_all x1, starting transfers between devices, local(): lax.all_to_all(summed.reshape(N_Y * N_Z, samples, rows), 'node', split_ax...  11.9 us
    ppermute x3, waiting for transfers between devices, gather_nodes(): lax.ppermute(trail, 'node', pairs[1])  10.5 us
    ppermute x1, starting transfers between devices, local(): grad_w = add(share, lax.ppermute(share, 'dp', DP_SWAP))  8.26 us
    all_to_all x1, waiting for transfers between devices, local(): lax.all_to_all(summed.reshape(N_Y * N_Z, samples, rows), 'node', split_ax...  8.25 us
    ppermute x3, starting transfers between devices, gather_nodes(): lax.ppermute(trail, 'node', pairs[1])  5.74 us
    all_to_all x1, waiting for transfers between devices, gather_nodes(): lax.all_to_all(copies, 'node', 0, 0, axis_index_groups=Z_GROUPS, tiled=True)  5.37 us
  transfers between devices with their start and end apart: 20, of which 14 were waited for; matrix products, arithmetic and copies ran while one was open for 3% of the time, Pallas kernels for 0%

profile of v9, /device:TPU:96, one launch (start us, length us, event | category | flops | bytes accessed | tf_op | source)
XLA Modules:
  0.0 161.4 jit_solution(2370145529435457813)
XLA Ops:
  9.5 1.9 %collective-permute-start = (bf16[3072,256]{1,0:T(8,128)(2,1)S(1)}, bf16[3072,256]{1,0:T(8,128)(2,1)S(1)}, u32[]{:S(2)}, u32[]{:S(2)}) collective-permute-start(bf16[3072,256]{1,0:T(8,128)(2,1)S(1)} %pack.1), channel_id=1, source_target_pairs={{0,2},{2,0},{4,6},{6,4},{8,10},{10,8},{12,14},{14,12},{1,3},{3,1},... | collective-permute-start | bytes 4718600 | tf_op jit(solution)/shard_map/ppermute | solution.py:76
  11.5 3.4 %collective-permute-done.got_ref = bf16[3072,256]{1,0:T(8,128)(2,1)S(1)} collective-permute-done((bf16[3072,256]{1,0:T(8,128)(2,1)S(1)}, bf16[3072,256]{1,0:T(8,128)(2,1)S(1)}, u32[]{:S(2)}, u32[]{:S(2)}) %collective-permute-start) | collective-permute-done | bytes 1572896 | tf_op jit(solution)/shard_map/ppermute | solution.py:76
  16.0 4.7 %collective-permute-start.5 = (bf16[384,256]{1,0:T(8,128)(2,1)S(1)}, bf16[384,256]{1,0:T(8,128)(2,1)S(1)}, u32[]{:S(2)}, u32[]{:S(2)}) collective-permute-start(bf16[384,256]{1,0:T(8,128)(2,1)S(1)} %get-tuple-element.19), channel_id=1, source_target_pairs={{0,12},{2,14},{4,8},{6,10},{8,4},{10,6},{12,0},{14,2},{1,13},{3,15... | collective-permute-start | bytes 589832 | tf_op jit(solution)/shard_map/ppermute | solution.py:92
  20.7 2.1 %collective-permute-start.2 = (bf16[384,256]{1,0:T(8,128)(2,1)S(1)}, bf16[384,256]{1,0:T(8,128)(2,1)S(1)}, u32[]{:S(2)}, u32[]{:S(2)}) collective-permute-start(bf16[384,256]{1,0:T(8,128)(2,1)S(1)} %get-tuple-element.15), channel_id=1, source_target_pairs={{0,4},{2,6},{4,0},{6,2},{8,12},{10,14},{12,8},{14,10},{1,5},{3,7},... | collective-permute-start | bytes 589832 | tf_op jit(solution)/shard_map/ppermute | solution.py:91
  22.8 3.7 %collective-permute-start.1 = (bf16[384,256]{1,0:T(8,128)(2,1)S(1)}, bf16[384,256]{1,0:T(8,128)(2,1)S(1)}, u32[]{:S(2)}, u32[]{:S(2)}) collective-permute-start(bf16[384,256]{1,0:T(8,128)(2,1)S(1)} %get-tuple-element.13), channel_id=1, source_target_pairs={{0,4},{2,6},{4,0},{6,2},{8,12},{10,14},{12,8},{14,10},{1,5},{3,7},... | collective-permute-start | bytes 589832 | tf_op jit(solution)/shard_map/ppermute | solution.py:93
  26.5 2.4 %collective-permute-start.4 = (bf16[384,256]{1,0:T(8,128)(2,1)S(1)}, bf16[384,256]{1,0:T(8,128)(2,1)S(1)}, u32[]{:S(2)}, u32[]{:S(2)}) collective-permute-start(bf16[384,256]{1,0:T(8,128)(2,1)S(1)} %get-tuple-element.17), channel_id=1, source_target_pairs={{0,12},{2,14},{4,8},{6,10},{8,4},{10,6},{12,0},{14,2},{1,13},{3,15... | collective-permute-start | bytes 589832 | tf_op jit(solution)/shard_map/ppermute | solution.py:94
  29.0 2.2 %collective-permute-start.6 = (bf16[384,256]{1,0:T(8,128)(2,1)S(1)}, bf16[384,256]{1,0:T(8,128)(2,1)S(1)}, u32[]{:S(2)}, u32[]{:S(2)}) collective-permute-start(bf16[384,256]{1,0:T(8,128)(2,1)S(1)} %add_convert_fusion), channel_id=1, source_target_pairs={{0,4},{2,6},{4,0},{6,2},{8,12},{10,14},{12,8},{14,10},{1,5},{3,7},... | collective-permute-start | bytes 589832 | tf_op jit(solution)/shard_map/ppermute | solution.py:96
  31.3 4.4 %collective-permute-start.3 = (bf16[384,256]{1,0:T(8,128)(2,1)S(1)}, bf16[384,256]{1,0:T(8,128)(2,1)S(1)}, u32[]{:S(2)}, u32[]{:S(2)}) collective-permute-start(bf16[384,256]{1,0:T(8,128)(2,1)S(1)} %add_convert_fusion.1), channel_id=1, source_target_pairs={{0,12},{2,14},{4,8},{6,10},{8,4},{10,6},{12,0},{14,2},{1,13},{3,15... | collective-permute-start | bytes 589832 | tf_op jit(solution)/shard_map/ppermute | solution.py:95
  37.7 2.4 %collective-permute-done.3.refs_2_ = bf16[384,256]{1,0:T(8,128)(2,1)S(1)} collective-permute-done((bf16[384,256]{1,0:T(8,128)(2,1)S(1)}, bf16[384,256]{1,0:T(8,128)(2,1)S(1)}, u32[]{:S(2)}, u32[]{:S(2)}) %collective-permute-start.3) | collective-permute-done | bytes 196640 | tf_op jit(solution)/shard_map/ppermute | solution.py:95
  41.0 11.9 %all-to-all-start = ((bf16[32,8,768]{2,1,0:T(8,128)(2,1)}), bf16[32,8,768]{2,1,0:T(8,128)(2,1)S(1)}, u32[]{:S(2)}, u32[]{:S(2)}) async-start(bf16[32,8,768]{2,1,0:T(8,128)(2,1)} %bitcast.7), calls=%async_computation | async-start | bytes 786432 | tf_op jit(solution)/shard_map/all_to_all | solution.py:145
  53.0 8.3 %all-to-all-done = bf16[32,8,768]{2,1,0:T(8,128)(2,1)S(1)} async-done(((bf16[32,8,768]{2,1,0:T(8,128)(2,1)}), bf16[32,8,768]{2,1,0:T(8,128)(2,1)S(1)}, u32[]{:S(2)}, u32[]{:S(2)}) %all-to-all-start) | async-done | bytes 393248 | tf_op jit(solution)/shard_map/all_to_all | solution.py:145
  65.3 5.3 %all-to-all-start.1 = ((bf16[4,8,4096]{2,1,0:T(8,128)(2,1)}), bf16[4,8,4096]{2,1,0:T(8,128)(2,1)S(1)}, u32[]{:S(2)}, u32[]{:S(2)}) async-start(bf16[4,8,4096]{2,1,0:T(8,128)(2,1)} %broadcast_in_dim.30), calls=%async_computation.1 | async-start | bytes 524288 | tf_op jit(solution)/shard_map/all_to_all | solution.py:114
  71.5 5.4 %all-to-all-done.1 = bf16[4,8,4096]{2,1,0:T(8,128)(2,1)S(1)} async-done(((bf16[4,8,4096]{2,1,0:T(8,128)(2,1)}), bf16[4,8,4096]{2,1,0:T(8,128)(2,1)S(1)}, u32[]{:S(2)}, u32[]{:S(2)}) %all-to-all-start.1) | async-done | bytes 262176 | tf_op jit(solution)/shard_map/all_to_all | solution.py:114
  76.9 2.6 %collective-permute-start.7 = (bf16[32,4096]{1,0:T(8,128)(2,1)S(1)}, bf16[32,4096]{1,0:T(8,128)(2,1)S(1)}, u32[]{:S(2)}, u32[]{:S(2)}) collective-permute-start(bf16[32,4096]{1,0:T(8,128)(2,1)S(1)} %bitcast.60), channel_id=1, source_target_pairs={{0,64},{16,80},{32,96},{48,112},{64,0},{80,16},{96,32},{112,48},{1... | collective-permute-start | bytes 786440 | tf_op jit(solution)/shard_map/ppermute | solution.py:126
  79.4 5.3 %collective-permute-start.8 = (bf16[32,4096]{1,0:T(8,128)(2,1)S(1)}, bf16[32,4096]{1,0:T(8,128)(2,1)S(1)}, u32[]{:S(2)}, u32[]{:S(2)}) collective-permute-start(bf16[32,4096]{1,0:T(8,128)(2,1)S(1)} %bitcast.61), channel_id=1, source_target_pairs={{0,448},{16,464},{32,480},{48,496},{64,128},{80,144},{96,160},{112... | collective-permute-start | bytes 786440 | tf_op jit(solution)/shard_map/ppermute | solution.py:127
  85.1 4.3 %collective-permute-start.9 = (bf16[32,4096]{1,0:T(8,128)(2,1)S(1)}, bf16[32,4096]{1,0:T(8,128)(2,1)S(1)}, u32[]{:S(2)}, u32[]{:S(2)}) collective-permute-start(bf16[32,4096]{1,0:T(8,128)(2,1)S(1)} %collective-permute-done.7), channel_id=1, source_target_pairs={{0,448},{16,464},{32,480},{48,496},{64,128},{80,144},{96,160},{112... | collective-permute-start | bytes 786440 | tf_op jit(solution)/shard_map/ppermute | solution.py:135
  89.4 2.1 %collective-permute-done.8 = bf16[32,4096]{1,0:T(8,128)(2,1)S(1)} collective-permute-done((bf16[32,4096]{1,0:T(8,128)(2,1)S(1)}, bf16[32,4096]{1,0:T(8,128)(2,1)S(1)}, u32[]{:S(2)}, u32[]{:S(2)}) %collective-permute-start.8) | collective-permute-done | bytes 262176 | tf_op jit(solution)/shard_map/ppermute | solution.py:127
  94.7 2.7 %collective-permute-start.11 = (bf16[32,4096]{1,0:T(8,128)(2,1)S(1)}, bf16[32,4096]{1,0:T(8,128)(2,1)S(1)}, u32[]{:S(2)}, u32[]{:S(2)}) collective-permute-start(bf16[32,4096]{1,0:T(8,128)(2,1)S(1)} %collective-permute-done.9), channel_id=1, source_target_pairs={{0,64},{16,80},{32,96},{48,112},{64,0},{80,16},{96,32},{112,48},{1... | collective-permute-start | bytes 786440 | tf_op jit(solution)/shard_map/ppermute | solution.py:135
  97.4 4.8 %collective-permute-done.10 = bf16[32,4096]{1,0:T(8,128)(2,1)} collective-permute-done((bf16[32,4096]{1,0:T(8,128)(2,1)S(1)}, bf16[32,4096]{1,0:T(8,128)(2,1)}, u32[]{:S(2)}, u32[]{:S(2)}) %collective-permute-start.10) | collective-permute-done | bytes 262176 | tf_op jit(solution)/shard_map/ppermute | solution.py:135
  105.8 5.1 %collective-permute-start.13 = (bf16[16,4096]{1,0:T(8,128)(2,1)}, bf16[16,4096]{1,0:T(8,128)(2,1)S(1)}, u32[]{:S(2)}, u32[]{:S(2)}) collective-permute-start(bf16[16,4096]{1,0:T(8,128)(2,1)} %slice.26), channel_id=1, source_target_pairs={{0,448},{16,464},{32,480},{48,496},{64,128},{80,144},{96,160},{112... | collective-permute-start | bytes 393224 | tf_op jit(solution)/shard_map/ppermute | solution.py:135
  116.8 3.8 %collective-permute-done.14 = bf16[16,4096]{1,0:T(8,128)(2,1)S(1)} collective-permute-done((bf16[16,4096]{1,0:T(8,128)(2,1)S(1)}, bf16[16,4096]{1,0:T(8,128)(2,1)S(1)}, u32[]{:S(2)}, u32[]{:S(2)}) %collective-permute-start.14) | collective-permute-done | bytes 131104 | tf_op jit(solution)/shard_map/ppermute | solution.py:135
  126.1 14.0 %all_to_all.15 = bf16[4,512,128]{2,1,0:T(8,128)(2,1)S(1)} all-to-all(bf16[4,512,128]{2,1,0:T(8,128)(2,1)S(1)} %fusion.1), channel_id=1, replica_groups={{0,4,8,12},{2,6,10,14},{1,5,9,13},{3,7,11,15},{16,20,24,28},{18,22,26,3..., dimensions={0} | all-to-all | bytes 1048576 | tf_op jit(solution)/shard_map/all_to_all | solution.py:176
  140.2 8.3 %collective-permute-start.16 = (bf16[512,128]{1,0:T(8,128)(2,1)S(1)}, bf16[512,128]{1,0:T(8,128)(2,1)S(1)}, u32[]{:S(2)}, u32[]{:S(2)}) collective-permute-start(bf16[512,128]{1,0:T(8,128)(2,1)S(1)} %fusion.8), channel_id=1, source_target_pairs={{0,1},{1,0},{2,3},{3,2},{4,5},{5,4},{6,7},{7,6},{8,9},{9,8},{10,11... | collective-permute-start | bytes 393224 | tf_op jit(solution)/shard_map/ppermute | solution.py:178
  149.2 4.6 %collective-permute-done.16 = bf16[512,128]{1,0:T(8,128)(2,1)S(1)} collective-permute-done((bf16[512,128]{1,0:T(8,128)(2,1)S(1)}, bf16[512,128]{1,0:T(8,128)(2,1)S(1)}, u32[]{:S(2)}, u32[]{:S(2)}) %collective-permute-start.16) | collective-permute-done | bytes 131104 | tf_op jit(solution)/shard_map/ppermute | solution.py:178
  (72 shorter events, 31.2 us)
Async XLA Ops:
  7.2 56.0 %copy-start = (bf16[128,32]{0,1:T(8,128)(2,1)S(1)}, bf16[128,32]{0,1:T(8,128)(2,1)}, u32[]{:S(2)}) copy-start(bf16[128,32]{0,1:T(8,128)(2,1)} %param.10) | copy-start | bytes 24580
  9.5 5.3 %collective-permute-start = (bf16[3072,256]{1,0:T(8,128)(2,1)S(1)}, bf16[3072,256]{1,0:T(8,128)(2,1)S(1)}, u32[]{:S(2)}, u32[]{:S(2)}) collective-permute-start(bf16[3072,256]{1,0:T(8,128)(2,1)S(1)} %pack.1), channel_id=1, source_target_pairs={{0,2},{2,0},{4,6},{6,4},{8,10},{10,8},{12,14},{14,12},{1,3},{3,1},... | collective-permute-start | bytes 4718600 | tf_op jit(solution)/shard_map/ppermute | solution.py:76
  16.0 36.9 %copy-start.6 = (s32[128]{0:T(128)S(1)}, s32[128]{0:T(128)}, u32[]{:S(2)}) copy-start(s32[128]{0:T(128)} %param.9) | copy-start | bytes 1540
  16.0 36.9 %copy-start.4 = (s32[1,1,8,128]{3,2,1,0:T(8,128)S(1)}, s32[1,1,8,128]{3,2,1,0:T(8,128)}, u32[]{:S(2)}) copy-start(s32[1,1,8,128]{3,2,1,0:T(8,128)} %param.8) | copy-start | bytes 12292
  16.0 12.9 %collective-permute-start.5 = (bf16[384,256]{1,0:T(8,128)(2,1)S(1)}, bf16[384,256]{1,0:T(8,128)(2,1)S(1)}, u32[]{:S(2)}, u32[]{:S(2)}) collective-permute-start(bf16[384,256]{1,0:T(8,128)(2,1)S(1)} %get-tuple-element.19), channel_id=1, source_target_pairs={{0,12},{2,14},{4,8},{6,10},{8,4},{10,6},{12,0},{14,2},{1,13},{3,15... | collective-permute-start | bytes 589832 | tf_op jit(solution)/shard_map/ppermute | solution.py:92
  20.7 10.5 %collective-permute-start.2 = (bf16[384,256]{1,0:T(8,128)(2,1)S(1)}, bf16[384,256]{1,0:T(8,128)(2,1)S(1)}, u32[]{:S(2)}, u32[]{:S(2)}) collective-permute-start(bf16[384,256]{1,0:T(8,128)(2,1)S(1)} %get-tuple-element.15), channel_id=1, source_target_pairs={{0,4},{2,6},{4,0},{6,2},{8,12},{10,14},{12,8},{14,10},{1,5},{3,7},... | collective-permute-start | bytes 589832 | tf_op jit(solution)/shard_map/ppermute | solution.py:91
  22.8 12.9 %collective-permute-start.1 = (bf16[384,256]{1,0:T(8,128)(2,1)S(1)}, bf16[384,256]{1,0:T(8,128)(2,1)S(1)}, u32[]{:S(2)}, u32[]{:S(2)}) collective-permute-start(bf16[384,256]{1,0:T(8,128)(2,1)S(1)} %get-tuple-element.13), channel_id=1, source_target_pairs={{0,4},{2,6},{4,0},{6,2},{8,12},{10,14},{12,8},{14,10},{1,5},{3,7},... | collective-permute-start | bytes 589832 | tf_op jit(solution)/shard_map/ppermute | solution.py:93
  26.5 9.2 %collective-permute-start.4 = (bf16[384,256]{1,0:T(8,128)(2,1)S(1)}, bf16[384,256]{1,0:T(8,128)(2,1)S(1)}, u32[]{:S(2)}, u32[]{:S(2)}) collective-permute-start(bf16[384,256]{1,0:T(8,128)(2,1)S(1)} %get-tuple-element.17), channel_id=1, source_target_pairs={{0,12},{2,14},{4,8},{6,10},{8,4},{10,6},{12,0},{14,2},{1,13},{3,15... | collective-permute-start | bytes 589832 | tf_op jit(solution)/shard_map/ppermute | solution.py:94
  29.0 8.7 %collective-permute-start.6 = (bf16[384,256]{1,0:T(8,128)(2,1)S(1)}, bf16[384,256]{1,0:T(8,128)(2,1)S(1)}, u32[]{:S(2)}, u32[]{:S(2)}) collective-permute-start(bf16[384,256]{1,0:T(8,128)(2,1)S(1)} %add_convert_fusion), channel_id=1, source_target_pairs={{0,4},{2,6},{4,0},{6,2},{8,12},{10,14},{12,8},{14,10},{1,5},{3,7},... | collective-permute-start | bytes 589832 | tf_op jit(solution)/shard_map/ppermute | solution.py:96
  31.3 8.8 %collective-permute-start.3 = (bf16[384,256]{1,0:T(8,128)(2,1)S(1)}, bf16[384,256]{1,0:T(8,128)(2,1)S(1)}, u32[]{:S(2)}, u32[]{:S(2)}) collective-permute-start(bf16[384,256]{1,0:T(8,128)(2,1)S(1)} %add_convert_fusion.1), channel_id=1, source_target_pairs={{0,12},{2,14},{4,8},{6,10},{8,4},{10,6},{12,0},{14,2},{1,13},{3,15... | collective-permute-start | bytes 589832 | tf_op jit(solution)/shard_map/ppermute | solution.py:95
  41.0 20.2 %all-to-all-start = ((bf16[32,8,768]{2,1,0:T(8,128)(2,1)}), bf16[32,8,768]{2,1,0:T(8,128)(2,1)S(1)}, u32[]{:S(2)}, u32[]{:S(2)}) async-start(bf16[32,8,768]{2,1,0:T(8,128)(2,1)} %bitcast.7), calls=%async_computation | async-start | bytes 786432 | tf_op jit(solution)/shard_map/all_to_all | solution.py:145
  65.3 11.6 %all-to-all-start.1 = ((bf16[4,8,4096]{2,1,0:T(8,128)(2,1)}), bf16[4,8,4096]{2,1,0:T(8,128)(2,1)S(1)}, u32[]{:S(2)}, u32[]{:S(2)}) async-start(bf16[4,8,4096]{2,1,0:T(8,128)(2,1)} %broadcast_in_dim.30), calls=%async_computation.1 | async-start | bytes 524288 | tf_op jit(solution)/shard_map/all_to_all | solution.py:114
  70.6 40.4 %all-gather.2.cloned.1.call-start = ((), (), s32[]{:S(2)}) async-start(), calls=%async_computation.3 | async-start | bytes 1179648 | tf_op jit(solution)/shard_map/all_gather | solution.py:142
  76.9 8.3 %collective-permute-start.7 = (bf16[32,4096]{1,0:T(8,128)(2,1)S(1)}, bf16[32,4096]{1,0:T(8,128)(2,1)S(1)}, u32[]{:S(2)}, u32[]{:S(2)}) collective-permute-start(bf16[32,4096]{1,0:T(8,128)(2,1)S(1)} %bitcast.60), channel_id=1, source_target_pairs={{0,64},{16,80},{32,96},{48,112},{64,0},{80,16},{96,32},{112,48},{1... | collective-permute-start | bytes 786440 | tf_op jit(solution)/shard_map/ppermute | solution.py:126
  79.4 12.0 %collective-permute-start.8 = (bf16[32,4096]{1,0:T(8,128)(2,1)S(1)}, bf16[32,4096]{1,0:T(8,128)(2,1)S(1)}, u32[]{:S(2)}, u32[]{:S(2)}) collective-permute-start(bf16[32,4096]{1,0:T(8,128)(2,1)S(1)} %bitcast.61), channel_id=1, source_target_pairs={{0,448},{16,464},{32,480},{48,496},{64,128},{80,144},{96,160},{112... | collective-permute-start | bytes 786440 | tf_op jit(solution)/shard_map/ppermute | solution.py:127
  85.1 9.5 %collective-permute-start.9 = (bf16[32,4096]{1,0:T(8,128)(2,1)S(1)}, bf16[32,4096]{1,0:T(8,128)(2,1)S(1)}, u32[]{:S(2)}, u32[]{:S(2)}) collective-permute-start(bf16[32,4096]{1,0:T(8,128)(2,1)S(1)} %collective-permute-done.7), channel_id=1, source_target_pairs={{0,448},{16,464},{32,480},{48,496},{64,128},{80,144},{96,160},{112... | collective-permute-start | bytes 786440 | tf_op jit(solution)/shard_map/ppermute | solution.py:135
  91.5 10.7 %collective-permute-start.10 = (bf16[32,4096]{1,0:T(8,128)(2,1)S(1)}, bf16[32,4096]{1,0:T(8,128)(2,1)}, u32[]{:S(2)}, u32[]{:S(2)}) collective-permute-start(bf16[32,4096]{1,0:T(8,128)(2,1)S(1)} %collective-permute-done.8), channel_id=1, source_target_pairs={{0,64},{16,80},{32,96},{48,112},{64,0},{80,16},{96,32},{112,48},{1... | collective-permute-start | bytes 786440 | tf_op jit(solution)/shard_map/ppermute | solution.py:135
  94.7 10.5 %collective-permute-start.11 = (bf16[32,4096]{1,0:T(8,128)(2,1)S(1)}, bf16[32,4096]{1,0:T(8,128)(2,1)S(1)}, u32[]{:S(2)}, u32[]{:S(2)}) collective-permute-start(bf16[32,4096]{1,0:T(8,128)(2,1)S(1)} %collective-permute-done.9), channel_id=1, source_target_pairs={{0,64},{16,80},{32,96},{48,112},{64,0},{80,16},{96,32},{112,48},{1... | collective-permute-start | bytes 786440 | tf_op jit(solution)/shard_map/ppermute | solution.py:135
  102.2 10.6 %collective-permute-start.12 = (bf16[32,4096]{1,0:T(8,128)(2,1)}, bf16[32,4096]{1,0:T(8,128)(2,1)}, u32[]{:S(2)}, u32[]{:S(2)}) collective-permute-start(bf16[32,4096]{1,0:T(8,128)(2,1)} %collective-permute-done.10), channel_id=1, source_target_pairs={{0,448},{16,464},{32,480},{48,496},{64,128},{80,144},{96,160},{112... | collective-permute-start | bytes 786440 | tf_op jit(solution)/shard_map/ppermute | solution.py:135
  105.8 10.9 %collective-permute-start.13 = (bf16[16,4096]{1,0:T(8,128)(2,1)}, bf16[16,4096]{1,0:T(8,128)(2,1)S(1)}, u32[]{:S(2)}, u32[]{:S(2)}) collective-permute-start(bf16[16,4096]{1,0:T(8,128)(2,1)} %slice.26), channel_id=1, source_target_pairs={{0,448},{16,464},{32,480},{48,496},{64,128},{80,144},{96,160},{112... | collective-permute-start | bytes 393224 | tf_op jit(solution)/shard_map/ppermute | solution.py:135
  111.0 9.7 %copy-start.2 = (bf16[4096,128]{1,0:T(8,128)(2,1)S(1)}, bf16[4096,128]{1,0:T(8,128)(2,1)}, u32[]{:S(2)}) copy-start(bf16[4096,128]{1,0:T(8,128)(2,1)} %all-gather.2.cloned.1.call-done) | copy-start | bytes 3145732
  113.7 6.9 %collective-permute-start.14 = (bf16[16,4096]{1,0:T(8,128)(2,1)S(1)}, bf16[16,4096]{1,0:T(8,128)(2,1)S(1)}, u32[]{:S(2)}, u32[]{:S(2)}) collective-permute-start(bf16[16,4096]{1,0:T(8,128)(2,1)S(1)} %slice.19), channel_id=1, source_target_pairs={{0,64},{16,80},{32,96},{48,112},{64,0},{80,16},{96,32},{112,48},{1... | collective-permute-start | bytes 393224 | tf_op jit(solution)/shard_map/ppermute | solution.py:135
  122.2 3.8 %collective-permute-start.15 = (bf16[4,512,128]{2,1,0:T(8,128)(2,1)S(1)}, bf16[4,512,128]{2,1,0:T(8,128)(2,1)S(1)}, u32[]{:S(2)}, u32[]{:S(2)}) collective-permute-start(bf16[4,512,128]{2,1,0:T(8,128)(2,1)S(1)} %dynamic-slice_bitcast_fusion), channel_id=1, source_target_pairs={{0,2},{2,0},{4,6},{6,4},{8,10},{10,8},{12,14},{14,12},{1,3},{3,1},... | collective-permute-start | bytes 1572872 | tf_op jit(solution)/shard_map/ppermute | solution.py:175
  140.2 13.5 %collective-permute-start.16 = (bf16[512,128]{1,0:T(8,128)(2,1)S(1)}, bf16[512,128]{1,0:T(8,128)(2,1)S(1)}, u32[]{:S(2)}, u32[]{:S(2)}) collective-permute-start(bf16[512,128]{1,0:T(8,128)(2,1)S(1)} %fusion.8), channel_id=1, source_target_pairs={{0,1},{1,0},{2,3},{3,2},{4,5},{5,4},{6,7},{7,6},{8,9},{9,8},{10,11... | collective-permute-start | bytes 393224 | tf_op jit(solution)/shard_map/ppermute | solution.py:178
  (3 other events, 8.8 us)
Sparse Core Ops, SparseCore 0:
  73.5 30.4 all-gather.1

commit v10 on v7

--- a/solution.py
+++ b/solution.py
@@ -20,7 +20,7 @@
 X_ODD = swaps(N_X * N_CORE, lambda h: h ^ 6)
 Y_EVEN = swaps(N_Y * N_Z, lambda n: n ^ N_Z)
 Y_ODD = swaps(N_Y * N_Z, lambda n: (((n // N_Z + 1) ^ 1) - 1) % N_Y * N_Z + n % N_Z)
-Z_GROUPS = [[N_Z * y + z for z in range(N_Z)] for y in range(N_Y)]
+Z_SWAPS = [swaps(N_Y * N_Z, lambda n, k=k: n ^ k) for k in range(1, N_Z)]
 X_GROUPS = [[N_CORE * x + c for x in range(N_X)] for c in range(N_CORE)]
 DP_SWAP = swaps(2, lambda d: d ^ 1)
 
@@ -110,9 +110,11 @@
 
 
 def gather_nodes(block):
-    copies = jnp.broadcast_to(block, (N_Z,) + block.shape)
-    line = lax.all_to_all(copies, "node", 0, 0, axis_index_groups=Z_GROUPS, tiled=True)
-    line = line.reshape(-1, block.shape[1])
+    z, samples = lax.axis_index("node") % N_Z, block.shape[0]
+    line = jnp.zeros((N_Z * samples, block.shape[1]), block.dtype)
+    near = [lax.ppermute(block, "node", pairs) for pairs in Z_SWAPS]
+    for other, part in enumerate([block] + near):
+        line = lax.dynamic_update_slice(line, part, ((z ^ other) * samples, 0))
     rows, half = line.shape[0], line.shape[0] // 2
     y = lax.axis_index("node") // N_Z
     sign = 1 - 2 * (y % 2)

time: 162 us -> 167 us (1.031)
  the two profiles are of different devices: /device:TPU:96 before, /device:TPU:1 now
where the time goes in v10:
time: 167 us
  starting transfers between devices  84.3 us (50%)
  waiting for transfers between devices  41.5 us (25%)
  between operations  14.9 us (9%)
  blocking collectives  13.1 us (8%)
  local copies, waits for them, and re-layouts  4.82 us (3%)
  matrix products  3.33 us (2%)
  Pallas kernels  2.57 us (2%)
  other arithmetic  2.12 us (1%)
    all_to_all x1, blocking collectives, local(): lax.all_to_all(pair, 'hst', 0, 0, axis_index_groups=X_GROUPS, tiled=True)  13.1 us
    all_to_all x1, waiting for transfers between devices, local(): lax.all_to_all(summed.reshape(N_Y * N_Z, samples, rows), 'node', split_ax...  11.9 us
    ppermute x1, starting transfers between devices, local(): pair = add(kept, lax.ppermute(given, 'hst', CORE_SWAP)).astype(jnp.bfloat16)  10.8 us
    ppermute x3, starting transfers between devices, gather_nodes(): lax.ppermute(trail, 'node', pairs[1])  10.1 us
    ppermute x3, starting transfers between devices, gather_nodes(): near = [lax.ppermute(block, 'node', pairs) for pairs in Z_SWAPS]  9.27 us
    ppermute x1, starting transfers between devices, sum_partials(): got = lax.ppermute(given, 'hst', CORE_SWAP)  8.79 us
    ppermute x1, starting transfers between devices, local(): grad_w = add(share, lax.ppermute(share, 'dp', DP_SWAP))  8.68 us
    ppermute x3, starting transfers between devices, gather_nodes(): lax.ppermute(lead, 'node', pairs[0])  8.27 us
  transfers between devices with their start and end apart: 22, of which 13 were waited for; matrix products, arithmetic and copies ran while one was open for 1% of the time, Pallas kernels for 0%

profile of v10, /device:TPU:1, one launch (start us, length us, event | category | flops | bytes accessed | tf_op | source)
XLA Modules:
  0.0 166.6 jit_solution(1836150786381099868)
XLA Ops:
  9.5 8.8 %collective-permute-start = (bf16[3072,256]{1,0:T(8,128)(2,1)S(1)}, bf16[3072,256]{1,0:T(8,128)(2,1)S(1)}, u32[]{:S(2)}, u32[]{:S(2)}) collective-permute-start(bf16[3072,256]{1,0:T(8,128)(2,1)S(1)} %pack.1), channel_id=1, source_target_pairs={{0,2},{2,0},{4,6},{6,4},{8,10},{10,8},{12,14},{14,12},{1,3},{3,1},... | collective-permute-start | bytes 4718600 | tf_op jit(solution)/shard_map/ppermute | solution.py:76
  18.3 3.0 %collective-permute-done.got_ref = bf16[3072,256]{1,0:T(8,128)(2,1)S(1)} collective-permute-done((bf16[3072,256]{1,0:T(8,128)(2,1)S(1)}, bf16[3072,256]{1,0:T(8,128)(2,1)S(1)}, u32[]{:S(2)}, u32[]{:S(2)}) %collective-permute-start) | collective-permute-done | bytes 1572896 | tf_op jit(solution)/shard_map/ppermute | solution.py:76
  26.4 3.4 %collective-permute-start.1 = (bf16[384,256]{1,0:T(8,128)(2,1)S(1)}, bf16[384,256]{1,0:T(8,128)(2,1)S(1)}, u32[]{:S(2)}, u32[]{:S(2)}) collective-permute-start(bf16[384,256]{1,0:T(8,128)(2,1)S(1)} %get-tuple-element.11), channel_id=1, source_target_pairs={{0,4},{2,6},{4,0},{6,2},{8,12},{10,14},{12,8},{14,10},{1,5},{3,7},... | collective-permute-start | bytes 589832 | tf_op jit(solution)/shard_map/ppermute | solution.py:93
  29.7 4.6 %collective-permute-start.4 = (bf16[384,256]{1,0:T(8,128)(2,1)S(1)}, bf16[384,256]{1,0:T(8,128)(2,1)S(1)}, u32[]{:S(2)}, u32[]{:S(2)}) collective-permute-start(bf16[384,256]{1,0:T(8,128)(2,1)S(1)} %get-tuple-element.15), channel_id=1, source_target_pairs={{0,12},{2,14},{4,8},{6,10},{8,4},{10,6},{12,0},{14,2},{1,13},{3,15... | collective-permute-start | bytes 589832 | tf_op jit(solution)/shard_map/ppermute | solution.py:94
  38.3 2.8 %collective-permute-done.6.refs_5_ = bf16[384,256]{1,0:T(8,128)(2,1)S(1)} collective-permute-done((bf16[384,256]{1,0:T(8,128)(2,1)S(1)}, bf16[384,256]{1,0:T(8,128)(2,1)S(1)}, u32[]{:S(2)}, u32[]{:S(2)}) %collective-permute-start.6) | collective-permute-done | bytes 196640 | tf_op jit(solution)/shard_map/ppermute | solution.py:96
  41.2 3.2 %collective-permute-done.3.refs_2_ = bf16[384,256]{1,0:T(8,128)(2,1)S(1)} collective-permute-done((bf16[384,256]{1,0:T(8,128)(2,1)S(1)}, bf16[384,256]{1,0:T(8,128)(2,1)S(1)}, u32[]{:S(2)}, u32[]{:S(2)}) %collective-permute-start.3) | collective-permute-done | bytes 196640 | tf_op jit(solution)/shard_map/ppermute | solution.py:95
  45.4 6.9 %all-to-all-start = ((bf16[32,8,768]{2,1,0:T(8,128)(2,1)}), bf16[32,8,768]{2,1,0:T(8,128)(2,1)S(1)}, u32[]{:S(2)}, u32[]{:S(2)}) async-start(bf16[32,8,768]{2,1,0:T(8,128)(2,1)} %bitcast.7), calls=%async_computation | async-start | bytes 786432 | tf_op jit(solution)/shard_map/all_to_all | solution.py:146
  52.4 11.9 %all-to-all-done = bf16[32,8,768]{2,1,0:T(8,128)(2,1)S(1)} async-done(((bf16[32,8,768]{2,1,0:T(8,128)(2,1)}), bf16[32,8,768]{2,1,0:T(8,128)(2,1)S(1)}, u32[]{:S(2)}, u32[]{:S(2)}) %all-to-all-start) | async-done | bytes 393248 | tf_op jit(solution)/shard_map/all_to_all | solution.py:146
  69.9 4.2 %collective-permute-start.8 = (bf16[8,4096]{1,0:T(8,128)(2,1)S(1)}, bf16[8,4096]{1,0:T(8,128)(2,1)S(1)}, u32[]{:S(2)}, u32[]{:S(2)}) collective-permute-start(bf16[8,4096]{1,0:T(8,128)(2,1)S(1)} %get-tuple-element.19), channel_id=1, source_target_pairs={{0,32},{16,48},{32,0},{48,16},{64,96},{80,112},{96,64},{112,80},{1... | collective-permute-start | bytes 196616 | tf_op jit(solution)/shard_map/ppermute | solution.py:115
  74.1 3.2 %collective-permute-start.9 = (bf16[8,4096]{1,0:T(8,128)(2,1)S(1)}, bf16[8,4096]{1,0:T(8,128)(2,1)S(1)}, u32[]{:S(2)}, u32[]{:S(2)}) collective-permute-start(bf16[8,4096]{1,0:T(8,128)(2,1)S(1)} %get-tuple-element.19), channel_id=1, source_target_pairs={{0,48},{16,32},{32,16},{48,0},{64,112},{80,96},{96,80},{112,64},{1... | collective-permute-start | bytes 196616 | tf_op jit(solution)/shard_map/ppermute | solution.py:115
  77.4 3.6 %collective-permute-done.9 = bf16[8,4096]{1,0:T(8,128)(2,1)S(1)} collective-permute-done((bf16[8,4096]{1,0:T(8,128)(2,1)S(1)}, bf16[8,4096]{1,0:T(8,128)(2,1)S(1)}, u32[]{:S(2)}, u32[]{:S(2)}) %collective-permute-start.9) | collective-permute-done | bytes 65568 | tf_op jit(solution)/shard_map/ppermute | solution.py:115
  80.9 2.7 %collective-permute-start.10 = (bf16[32,4096]{1,0:T(8,128)(2,1)S(1)}, bf16[32,4096]{1,0:T(8,128)(2,1)S(1)}, u32[]{:S(2)}, u32[]{:S(2)}) collective-permute-start(bf16[32,4096]{1,0:T(8,128)(2,1)S(1)} %constant_dynamic-update-slice_fusion.9), channel_id=1, source_target_pairs={{0,64},{16,80},{32,96},{48,112},{64,0},{80,16},{96,32},{112,48},{1... | collective-permute-start | bytes 786440 | tf_op jit(solution)/shard_map/ppermute | solution.py:128
  83.6 3.2 %collective-permute-start.11 = (bf16[32,4096]{1,0:T(8,128)(2,1)S(1)}, bf16[32,4096]{1,0:T(8,128)(2,1)S(1)}, u32[]{:S(2)}, u32[]{:S(2)}) collective-permute-start(bf16[32,4096]{1,0:T(8,128)(2,1)S(1)} %constant_dynamic-update-slice_fusion.9), channel_id=1, source_target_pairs={{0,448},{16,464},{32,480},{48,496},{64,128},{80,144},{96,160},{112... | collective-permute-start | bytes 786440 | tf_op jit(solution)/shard_map/ppermute | solution.py:129
  88.0 2.5 %collective-permute-start.12 = (bf16[32,4096]{1,0:T(8,128)(2,1)S(1)}, bf16[32,4096]{1,0:T(8,128)(2,1)S(1)}, u32[]{:S(2)}, u32[]{:S(2)}) collective-permute-start(bf16[32,4096]{1,0:T(8,128)(2,1)S(1)} %collective-permute-done.10), channel_id=1, source_target_pairs={{0,448},{16,464},{32,480},{48,496},{64,128},{80,144},{96,160},{112... | collective-permute-start | bytes 786440 | tf_op jit(solution)/shard_map/ppermute | solution.py:136
  94.3 3.2 %collective-permute-done.12 = bf16[32,4096]{1,0:T(8,128)(2,1)S(1)} collective-permute-done((bf16[32,4096]{1,0:T(8,128)(2,1)S(1)}, bf16[32,4096]{1,0:T(8,128)(2,1)S(1)}, u32[]{:S(2)}, u32[]{:S(2)}) %collective-permute-start.12) | collective-permute-done | bytes 262176 | tf_op jit(solution)/shard_map/ppermute | solution.py:136
  99.9 4.0 %collective-permute-start.15 = (bf16[32,4096]{1,0:T(8,128)(2,1)S(1)}, bf16[32,4096]{1,0:T(8,128)(2,1)S(1)}, u32[]{:S(2)}, u32[]{:S(2)}) collective-permute-start(bf16[32,4096]{1,0:T(8,128)(2,1)S(1)} %collective-permute-done.13), channel_id=1, source_target_pairs={{0,448},{16,464},{32,480},{48,496},{64,128},{80,144},{96,160},{112... | collective-permute-start | bytes 786440 | tf_op jit(solution)/shard_map/ppermute | solution.py:136
  105.0 3.8 %collective-permute-start.16 = (bf16[16,4096]{1,0:T(8,128)(2,1)S(1)}, bf16[16,4096]{1,0:T(8,128)(2,1)S(1)}, u32[]{:S(2)}, u32[]{:S(2)}) collective-permute-start(bf16[16,4096]{1,0:T(8,128)(2,1)S(1)} %slice.26), channel_id=1, source_target_pairs={{0,448},{16,464},{32,480},{48,496},{64,128},{80,144},{96,160},{112... | collective-permute-start | bytes 393224 | tf_op jit(solution)/shard_map/ppermute | solution.py:136
  108.9 4.1 %collective-permute-start.17 = (bf16[16,4096]{1,0:T(8,128)(2,1)S(1)}, bf16[16,4096]{1,0:T(8,128)(2,1)S(1)}, u32[]{:S(2)}, u32[]{:S(2)}) collective-permute-start(bf16[16,4096]{1,0:T(8,128)(2,1)S(1)} %slice.27), channel_id=1, source_target_pairs={{0,64},{16,80},{32,96},{48,112},{64,0},{80,16},{96,32},{112,48},{1... | collective-permute-start | bytes 393224 | tf_op jit(solution)/shard_map/ppermute | solution.py:136
  113.1 2.5 %collective-permute-done.17 = bf16[16,4096]{1,0:T(8,128)(2,1)S(1)} collective-permute-done((bf16[16,4096]{1,0:T(8,128)(2,1)S(1)}, bf16[16,4096]{1,0:T(8,128)(2,1)S(1)}, u32[]{:S(2)}, u32[]{:S(2)}) %collective-permute-start.17) | collective-permute-done | bytes 131104 | tf_op jit(solution)/shard_map/ppermute | solution.py:136
  115.7 1.9 %fusion.25 = f32[256,128]{1,0:T(8,128)S(1)} fusion(bf16[256,4096]{1,0:T(8,128)(2,1)S(1)} %constant_dynamic-update-slice_fusion, bf16[4096,128]{1,0:T(8,128)(2,1)} %all-gather.2.cloned.1.call-done), kind=kOutput, calls=%fused_computation.48 | convolution fusion | flops 268435456 | bytes 3276800 | tf_op jit(solution)/shard_map/dot_general | solution.py:163
  118.5 10.8 %collective-permute-start.18 = (bf16[4,512,128]{2,1,0:T(8,128)(2,1)S(1)}, bf16[4,512,128]{2,1,0:T(8,128)(2,1)S(1)}, u32[]{:S(2)}, u32[]{:S(2)}) collective-permute-start(bf16[4,512,128]{2,1,0:T(8,128)(2,1)S(1)} %dynamic-slice_bitcast_fusion), channel_id=1, source_target_pairs={{0,2},{2,0},{4,6},{6,4},{8,10},{10,8},{12,14},{14,12},{1,3},{3,1},... | collective-permute-start | bytes 1572872 | tf_op jit(solution)/shard_map/ppermute | solution.py:176
  130.9 13.1 %all_to_all.10 = bf16[4,512,128]{2,1,0:T(8,128)(2,1)S(1)} all-to-all(bf16[4,512,128]{2,1,0:T(8,128)(2,1)S(1)} %fusion.1), channel_id=1, replica_groups={{0,4,8,12},{2,6,10,14},{1,5,9,13},{3,7,11,15},{16,20,24,28},{18,22,26,3..., dimensions={0} | all-to-all | bytes 1048576 | tf_op jit(solution)/shard_map/all_to_all | solution.py:177
  144.1 8.7 %collective-permute-start.19 = (bf16[512,128]{1,0:T(8,128)(2,1)S(1)}, bf16[512,128]{1,0:T(8,128)(2,1)S(1)}, u32[]{:S(2)}, u32[]{:S(2)}) collective-permute-start(bf16[512,128]{1,0:T(8,128)(2,1)S(1)} %fusion.8), channel_id=1, source_target_pairs={{0,1},{1,0},{2,3},{3,2},{4,5},{5,4},{6,7},{7,6},{8,9},{9,8},{10,11... | collective-permute-start | bytes 393224 | tf_op jit(solution)/shard_map/ppermute | solution.py:179
  153.5 5.5 %collective-permute-done.19 = bf16[512,128]{1,0:T(8,128)(2,1)S(1)} collective-permute-done((bf16[512,128]{1,0:T(8,128)(2,1)S(1)}, bf16[512,128]{1,0:T(8,128)(2,1)S(1)}, u32[]{:S(2)}, u32[]{:S(2)}) %collective-permute-start.19) | collective-permute-done | bytes 131104 | tf_op jit(solution)/shard_map/ppermute | solution.py:179
  (77 shorter events, 30.1 us)
Async XLA Ops:
  7.2 59.1 %copy-start = (bf16[128,32]{0,1:T(8,128)(2,1)S(1)}, bf16[128,32]{0,1:T(8,128)(2,1)}, u32[]{:S(2)}) copy-start(bf16[128,32]{0,1:T(8,128)(2,1)} %param.10) | copy-start | bytes 24580
  9.5 11.8 %collective-permute-start = (bf16[3072,256]{1,0:T(8,128)(2,1)S(1)}, bf16[3072,256]{1,0:T(8,128)(2,1)S(1)}, u32[]{:S(2)}, u32[]{:S(2)}) collective-permute-start(bf16[3072,256]{1,0:T(8,128)(2,1)S(1)} %pack.1), channel_id=1, source_target_pairs={{0,2},{2,0},{4,6},{6,4},{8,10},{10,8},{12,14},{14,12},{1,3},{3,1},... | collective-permute-start | bytes 4718600 | tf_op jit(solution)/shard_map/ppermute | solution.py:76
  22.5 29.9 %copy-start.4 = (s32[1,1,8,128]{3,2,1,0:T(8,128)S(1)}, s32[1,1,8,128]{3,2,1,0:T(8,128)}, u32[]{:S(2)}) copy-start(s32[1,1,8,128]{3,2,1,0:T(8,128)} %param.8) | copy-start | bytes 12292
  22.5 11.8 %collective-permute-start.5 = (bf16[384,256]{1,0:T(8,128)(2,1)S(1)}, bf16[384,256]{1,0:T(8,128)(2,1)S(1)}, u32[]{:S(2)}, u32[]{:S(2)}) collective-permute-start(bf16[384,256]{1,0:T(8,128)(2,1)S(1)} %get-tuple-element.17), channel_id=1, source_target_pairs={{0,12},{2,14},{4,8},{6,10},{8,4},{10,6},{12,0},{14,2},{1,13},{3,15... | collective-permute-start | bytes 589832 | tf_op jit(solution)/shard_map/ppermute | solution.py:92
  24.4 11.9 %collective-permute-start.2 = (bf16[384,256]{1,0:T(8,128)(2,1)S(1)}, bf16[384,256]{1,0:T(8,128)(2,1)S(1)}, u32[]{:S(2)}, u32[]{:S(2)}) collective-permute-start(bf16[384,256]{1,0:T(8,128)(2,1)S(1)} %get-tuple-element.13), channel_id=1, source_target_pairs={{0,4},{2,6},{4,0},{6,2},{8,12},{10,14},{12,8},{14,10},{1,5},{3,7},... | collective-permute-start | bytes 589832 | tf_op jit(solution)/shard_map/ppermute | solution.py:91
  26.4 12.0 %collective-permute-start.1 = (bf16[384,256]{1,0:T(8,128)(2,1)S(1)}, bf16[384,256]{1,0:T(8,128)(2,1)S(1)}, u32[]{:S(2)}, u32[]{:S(2)}) collective-permute-start(bf16[384,256]{1,0:T(8,128)(2,1)S(1)} %get-tuple-element.11), channel_id=1, source_target_pairs={{0,4},{2,6},{4,0},{6,2},{8,12},{10,14},{12,8},{14,10},{1,5},{3,7},... | collective-permute-start | bytes 589832 | tf_op jit(solution)/shard_map/ppermute | solution.py:93
  29.7 8.6 %collective-permute-start.4 = (bf16[384,256]{1,0:T(8,128)(2,1)S(1)}, bf16[384,256]{1,0:T(8,128)(2,1)S(1)}, u32[]{:S(2)}, u32[]{:S(2)}) collective-permute-start(bf16[384,256]{1,0:T(8,128)(2,1)S(1)} %get-tuple-element.15), channel_id=1, source_target_pairs={{0,12},{2,14},{4,8},{6,10},{8,4},{10,6},{12,0},{14,2},{1,13},{3,15... | collective-permute-start | bytes 589832 | tf_op jit(solution)/shard_map/ppermute | solution.py:94
  34.4 6.8 %collective-permute-start.6 = (bf16[384,256]{1,0:T(8,128)(2,1)S(1)}, bf16[384,256]{1,0:T(8,128)(2,1)S(1)}, u32[]{:S(2)}, u32[]{:S(2)}) collective-permute-start(bf16[384,256]{1,0:T(8,128)(2,1)S(1)} %add_convert_fusion), channel_id=1, source_target_pairs={{0,4},{2,6},{4,0},{6,2},{8,12},{10,14},{12,8},{14,10},{1,5},{3,7},... | collective-permute-start | bytes 589832 | tf_op jit(solution)/shard_map/ppermute | solution.py:96
  36.4 8.0 %collective-permute-start.3 = (bf16[384,256]{1,0:T(8,128)(2,1)S(1)}, bf16[384,256]{1,0:T(8,128)(2,1)S(1)}, u32[]{:S(2)}, u32[]{:S(2)}) collective-permute-start(bf16[384,256]{1,0:T(8,128)(2,1)S(1)} %add_convert_fusion.1), channel_id=1, source_target_pairs={{0,12},{2,14},{4,8},{6,10},{8,4},{10,6},{12,0},{14,2},{1,13},{3,15... | collective-permute-start | bytes 589832 | tf_op jit(solution)/shard_map/ppermute | solution.py:95
  45.4 19.0 %all-to-all-start = ((bf16[32,8,768]{2,1,0:T(8,128)(2,1)}), bf16[32,8,768]{2,1,0:T(8,128)(2,1)S(1)}, u32[]{:S(2)}, u32[]{:S(2)}) async-start(bf16[32,8,768]{2,1,0:T(8,128)(2,1)} %bitcast.7), calls=%async_computation | async-start | bytes 786432 | tf_op jit(solution)/shard_map/all_to_all | solution.py:146
  52.3 63.4 %all-gather.2.cloned.1.call-start = ((), (), s32[]{:S(2)}) async-start(), calls=%async_computation.2 | async-start | bytes 1179648 | tf_op jit(solution)/shard_map/all_gather | solution.py:143
  67.7 9.6 %collective-permute-start.7 = (bf16[8,4096]{1,0:T(8,128)(2,1)S(1)}, bf16[8,4096]{1,0:T(8,128)(2,1)S(1)}, u32[]{:S(2)}, u32[]{:S(2)}) collective-permute-start(bf16[8,4096]{1,0:T(8,128)(2,1)S(1)} %get-tuple-element.19), channel_id=1, source_target_pairs={{0,16},{16,0},{32,48},{48,32},{64,80},{80,64},{96,112},{112,96},{1... | collective-permute-start | bytes 196616 | tf_op jit(solution)/shard_map/ppermute | solution.py:115
  69.9 7.4 %collective-permute-start.8 = (bf16[8,4096]{1,0:T(8,128)(2,1)S(1)}, bf16[8,4096]{1,0:T(8,128)(2,1)S(1)}, u32[]{:S(2)}, u32[]{:S(2)}) collective-permute-start(bf16[8,4096]{1,0:T(8,128)(2,1)S(1)} %get-tuple-element.19), channel_id=1, source_target_pairs={{0,32},{16,48},{32,0},{48,16},{64,96},{80,112},{96,64},{112,80},{1... | collective-permute-start | bytes 196616 | tf_op jit(solution)/shard_map/ppermute | solution.py:115
  74.1 6.8 %collective-permute-start.9 = (bf16[8,4096]{1,0:T(8,128)(2,1)S(1)}, bf16[8,4096]{1,0:T(8,128)(2,1)S(1)}, u32[]{:S(2)}, u32[]{:S(2)}) collective-permute-start(bf16[8,4096]{1,0:T(8,128)(2,1)S(1)} %get-tuple-element.19), channel_id=1, source_target_pairs={{0,48},{16,32},{32,16},{48,0},{64,112},{80,96},{96,80},{112,64},{1... | collective-permute-start | bytes 196616 | tf_op jit(solution)/shard_map/ppermute | solution.py:115
  80.9 7.1 %collective-permute-start.10 = (bf16[32,4096]{1,0:T(8,128)(2,1)S(1)}, bf16[32,4096]{1,0:T(8,128)(2,1)S(1)}, u32[]{:S(2)}, u32[]{:S(2)}) collective-permute-start(bf16[32,4096]{1,0:T(8,128)(2,1)S(1)} %constant_dynamic-update-slice_fusion.9), channel_id=1, source_target_pairs={{0,64},{16,80},{32,96},{48,112},{64,0},{80,16},{96,32},{112,48},{1... | collective-permute-start | bytes 786440 | tf_op jit(solution)/shard_map/ppermute | solution.py:128
  83.6 8.7 %collective-permute-start.11 = (bf16[32,4096]{1,0:T(8,128)(2,1)S(1)}, bf16[32,4096]{1,0:T(8,128)(2,1)S(1)}, u32[]{:S(2)}, u32[]{:S(2)}) collective-permute-start(bf16[32,4096]{1,0:T(8,128)(2,1)S(1)} %constant_dynamic-update-slice_fusion.9), channel_id=1, source_target_pairs={{0,448},{16,464},{32,480},{48,496},{64,128},{80,144},{96,160},{112... | collective-permute-start | bytes 786440 | tf_op jit(solution)/shard_map/ppermute | solution.py:129
  88.0 9.5 %collective-permute-start.12 = (bf16[32,4096]{1,0:T(8,128)(2,1)S(1)}, bf16[32,4096]{1,0:T(8,128)(2,1)S(1)}, u32[]{:S(2)}, u32[]{:S(2)}) collective-permute-start(bf16[32,4096]{1,0:T(8,128)(2,1)S(1)} %collective-permute-done.10), channel_id=1, source_target_pairs={{0,448},{16,464},{32,480},{48,496},{64,128},{80,144},{96,160},{112... | collective-permute-start | bytes 786440 | tf_op jit(solution)/shard_map/ppermute | solution.py:136
  92.4 7.5 %collective-permute-start.13 = (bf16[32,4096]{1,0:T(8,128)(2,1)S(1)}, bf16[32,4096]{1,0:T(8,128)(2,1)S(1)}, u32[]{:S(2)}, u32[]{:S(2)}) collective-permute-start(bf16[32,4096]{1,0:T(8,128)(2,1)S(1)} %collective-permute-done.11), channel_id=1, source_target_pairs={{0,64},{16,80},{32,96},{48,112},{64,0},{80,16},{96,32},{112,48},{1... | collective-permute-start | bytes 786440 | tf_op jit(solution)/shard_map/ppermute | solution.py:136
  97.6 7.4 %collective-permute-start.14 = (bf16[32,4096]{1,0:T(8,128)(2,1)S(1)}, bf16[32,4096]{1,0:T(8,128)(2,1)S(1)}, u32[]{:S(2)}, u32[]{:S(2)}) collective-permute-start(bf16[32,4096]{1,0:T(8,128)(2,1)S(1)} %collective-permute-done.12), channel_id=1, source_target_pairs={{0,64},{16,80},{32,96},{48,112},{64,0},{80,16},{96,32},{112,48},{1... | collective-permute-start | bytes 786440 | tf_op jit(solution)/shard_map/ppermute | solution.py:136
  99.9 9.0 %collective-permute-start.15 = (bf16[32,4096]{1,0:T(8,128)(2,1)S(1)}, bf16[32,4096]{1,0:T(8,128)(2,1)S(1)}, u32[]{:S(2)}, u32[]{:S(2)}) collective-permute-start(bf16[32,4096]{1,0:T(8,128)(2,1)S(1)} %collective-permute-done.13), channel_id=1, source_target_pairs={{0,448},{16,464},{32,480},{48,496},{64,128},{80,144},{96,160},{112... | collective-permute-start | bytes 786440 | tf_op jit(solution)/shard_map/ppermute | solution.py:136
  105.0 8.1 %collective-permute-start.16 = (bf16[16,4096]{1,0:T(8,128)(2,1)S(1)}, bf16[16,4096]{1,0:T(8,128)(2,1)S(1)}, u32[]{:S(2)}, u32[]{:S(2)}) collective-permute-start(bf16[16,4096]{1,0:T(8,128)(2,1)S(1)} %slice.26), channel_id=1, source_target_pairs={{0,448},{16,464},{32,480},{48,496},{64,128},{80,144},{96,160},{112... | collective-permute-start | bytes 393224 | tf_op jit(solution)/shard_map/ppermute | solution.py:136
  108.9 6.8 %collective-permute-start.17 = (bf16[16,4096]{1,0:T(8,128)(2,1)S(1)}, bf16[16,4096]{1,0:T(8,128)(2,1)S(1)}, u32[]{:S(2)}, u32[]{:S(2)}) collective-permute-start(bf16[16,4096]{1,0:T(8,128)(2,1)S(1)} %slice.27), channel_id=1, source_target_pairs={{0,64},{16,80},{32,96},{48,112},{64,0},{80,16},{96,32},{112,48},{1... | collective-permute-start | bytes 393224 | tf_op jit(solution)/shard_map/ppermute | solution.py:136
  118.5 12.3 %collective-permute-start.18 = (bf16[4,512,128]{2,1,0:T(8,128)(2,1)S(1)}, bf16[4,512,128]{2,1,0:T(8,128)(2,1)S(1)}, u32[]{:S(2)}, u32[]{:S(2)}) collective-permute-start(bf16[4,512,128]{2,1,0:T(8,128)(2,1)S(1)} %dynamic-slice_bitcast_fusion), channel_id=1, source_target_pairs={{0,2},{2,0},{4,6},{6,4},{8,10},{10,8},{12,14},{14,12},{1,3},{3,1},... | collective-permute-start | bytes 1572872 | tf_op jit(solution)/shard_map/ppermute | solution.py:176
  144.1 14.9 %collective-permute-start.19 = (bf16[512,128]{1,0:T(8,128)(2,1)S(1)}, bf16[512,128]{1,0:T(8,128)(2,1)S(1)}, u32[]{:S(2)}, u32[]{:S(2)}) collective-permute-start(bf16[512,128]{1,0:T(8,128)(2,1)S(1)} %fusion.8), channel_id=1, source_target_pairs={{0,1},{1,0},{2,3},{3,2},{4,5},{5,4},{6,7},{7,6},{8,9},{9,8},{10,11... | collective-permute-start | bytes 393224 | tf_op jit(solution)/shard_map/ppermute | solution.py:179
  (4 other events, 37.7 us)
Sparse Core Ops, SparseCore 0:
  69.8 31.7 all-gather.1
